TPU v7x, 32 devices: a whole 2x2x4 slice. The times are simulated.
32 devices in a mesh: groups: 2 (over y), wide: 8 (over z, x), narrow: 2 (over core).
Axes of the slice: x: 2, y: 2, z: 4, core: 2. Of those that a mesh axis runs over, the one named last changes fastest.
Arguments:
- candidates: bfloat16 [16, 2048, 512], P('groups', ('wide', 'narrow')), parts along dimension 0, may hold values from -6 to 6
- pre_inner: bfloat16 [512, 512], replicated, may hold values from -0.25 to 0.25
- pre_bias: float32 [512], replicated, may hold values from -3 to 3
- pre_outer: bfloat16 [512, 512], replicated, may hold values from -0.25 to 0.25
- user_vector: bfloat16 [16, 512], P('groups'), parts along dimension 0, may hold values from -0.25 to 0.25
- kept_index: int32 [16, 512], P('groups'), parts along dimension 0, may hold values from 0 to 2047, as said below
- slot_request: int32 [16], P('groups'), parts along dimension 0, may hold values from 0 to 7, each once
- history_kv: bfloat16 [16, 2, 512, 512], P(('groups', 'wide'), None, None, 'narrow'), parts along dimension 0, may hold values from -6 to 6
- history_bias: float32 [16, 8, 512], P(('groups', 'wide'), 'narrow'), parts along dimension 0, may hold values from -8 to 404
- history_length: int32 [16], P(('groups', 'wide')), parts along dimension 0, may hold values from 64 to 512, as said below
- query_weight: bfloat16 [512, 512], replicated, may hold values from -0.25 to 0.25
- norm_gain: float32 [512], replicated, may hold values from 0.1 to 1.9
- expert_weight: bfloat16 [8, 512, 256], P('narrow'), may hold values from -0.25 to 0.25
- gate_weight: bfloat16 [512, 64], replicated, may hold values from -0.25 to 0.25
- gate_bias: float32 [8, 8], replicated, may hold values from -4 to 401
- tower_inner: bfloat16 [8, 256, 128], P('narrow'), may hold values from -0.375 to 0.375
- tower_outer: bfloat16 [8, 128], P('narrow'), may hold values from -0.5 to 0.5
Outputs:
- prerank_score: float32 [16, 2048], P('groups', ('wide', 'narrow')), parts along dimension 0
- rank_score: float32 [8, 16, 2048], P(None, 'groups', ('wide', 'narrow')), parts along dimension 1
There are 2 independent parts, one for each index of `groups`. A program takes and returns all parts, laid end to end along the dimension named above; an argument that names none is the same for every part. Nothing has to cross between parts.
Inputs may be any that keep to these rules, and one draw needn't show every extreme that they name: `kept_index`: each row holds 512 distinct candidate numbers; of the candidates of one request in one aligned block of 128 numbers at most 64 are kept, and exactly 64 in some block of every request. `slot_request`: a permutation; slot s belongs to ranking group s. `history_length`: at least one entry equals 512.
All inputs are finite; a program needn't handle non-finite values.
Results may differ from a plain program's by a relative error of at most 0.0085.
Values may be sent and summed in bfloat16 or wider, within the bound.
No kernel may reach another device: no remote copies, remote signals or barrier semaphores. Data moves between devices by JAX's collectives and lax.ppermute only.
A program may use at most 64 MiB of HBM per device.

v0:
```python
import jax
import jax.numpy as jnp
from jax import lax
from jax.sharding import PartitionSpec as P


def attend_slot(inputs):
    queries, history, biases, length = inputs
    heads_here = biases.shape[0]
    history_span = history.shape[1]
    head_size = queries.shape[1] // heads_here
    row_count = queries.shape[0]
    history_keys = history[0].reshape(history_span, heads_here, head_size)
    history_values = history[1].reshape(history_span, heads_here, head_size)
    shaped = queries.reshape(row_count, heads_here, head_size)
    scores = jnp.einsum(
        "khd,lhd->hkl", shaped, history_keys, preferred_element_type=jnp.float32
    ) * float(head_size) ** (-0.5)
    scores = scores + biases[:, None, :]
    visible = jnp.arange(history_span, dtype=jnp.int32) < length
    scores = jnp.where(visible[None, None, :], scores, -jnp.inf)
    row_max = jnp.max(scores, axis=2, keepdims=True)
    powers = jnp.exp(scores - row_max)
    weights = (powers / jnp.sum(powers, axis=2, keepdims=True)).astype(jnp.bfloat16)
    attended = jnp.einsum(
        "hkl,lhd->khd", weights, history_values, preferred_element_type=jnp.float32
    )
    return attended.astype(jnp.bfloat16).reshape(row_count, heads_here * head_size)


def on_device(
    candidates,
    pre_inner,
    pre_bias,
    pre_outer,
    user_vector,
    kept_index,
    slot_request,
    history_kv,
    history_bias,
    history_length,
    query_weight,
    norm_gain,
    expert_weight,
    gate_weight,
    gate_bias,
    tower_inner,
    tower_outer,
):
    wide_count = lax.axis_size("wide")
    narrow_count = lax.axis_size("narrow")
    shards = wide_count * narrow_count
    wide_rank = lax.axis_index("wide")
    narrow_rank = lax.axis_index("narrow")
    device_rank = wide_rank * narrow_count + narrow_rank
    requests, shard_len, features = candidates.shape
    kept_count = kept_index.shape[1]
    capacity = 2 * kept_count // shards
    group_size = history_kv.shape[0]
    width = pre_outer.shape[1]
    query_width = query_weight.shape[1]
    head_width = query_width // narrow_count
    tasks_here = tower_inner.shape[0]
    experts_all = gate_bias.shape[1]
    hidden_pre = jax.nn.relu(
        jnp.dot(
            candidates.reshape(requests * shard_len, features),
            pre_inner,
            preferred_element_type=jnp.float32,
        )
        + pre_bias
    ).astype(jnp.bfloat16)
    embedded = (
        jnp.dot(hidden_pre, pre_outer, preferred_element_type=jnp.float32)
        .astype(jnp.bfloat16)
        .reshape(requests, shard_len, width)
    )
    prerank_score = jnp.einsum(
        "rsd,rd->rs", embedded, user_vector, preferred_element_type=jnp.float32
    )
    local_index = kept_index - device_rank * shard_len
    matches = local_index[:, :, None] == jnp.arange(shard_len, dtype=jnp.int32)[None, None, :]
    flags = jnp.any(matches, axis=1)
    places = jnp.cumsum(flags.astype(jnp.int32), axis=1) - 1
    packing = (places[:, None, :] == jnp.arange(capacity, dtype=jnp.int32)[None, :, None]) & flags[
        :, None, :
    ]
    packed = jnp.einsum(
        "rcs,rsd->rcd", packing.astype(jnp.bfloat16), embedded, preferred_element_type=jnp.float32
    ).astype(jnp.bfloat16)
    by_slot = packed[slot_request]
    sending = by_slot
    sending = sending.reshape(requests, 1, capacity, -1)
    arrived = lax.all_to_all(
        lax.all_to_all(sending, "wide", split_axis=0, concat_axis=1, tiled=True),
        "narrow",
        split_axis=3,
        concat_axis=1,
        tiled=True,
    )
    slots_here = wide_rank * group_size + jnp.arange(group_size, dtype=jnp.int32)
    requests_here = slot_request[slots_here]
    kept_here = kept_index[requests_here]
    block_of = kept_here // shard_len
    counts = jnp.sum(
        (block_of[:, :, None] == jnp.arange(shards, dtype=jnp.int32)[None, None, :]).astype(
            jnp.int32
        ),
        axis=1,
    )
    block_ends = jnp.cumsum(counts, axis=1)
    starts = block_ends - counts
    row_ranks = jnp.arange(kept_count, dtype=jnp.int32)
    block_at = jnp.sum(
        (block_ends[:, None, :] <= row_ranks[None, :, None]).astype(jnp.int32), axis=2
    )
    within = row_ranks[None, :] - jnp.take_along_axis(starts, block_at, axis=1)
    anchor = block_at % narrow_count * wide_count + block_at // narrow_count
    flat_rows = anchor * capacity + within
    compact = jnp.take_along_axis(
        arrived.reshape(group_size, shards * capacity, -1), flat_rows[:, :, None], axis=1
    )
    embed_full = lax.all_gather(compact, "narrow", axis=2, tiled=True)
    query_columns = lax.dynamic_slice_in_dim(query_weight, narrow_rank * head_width, head_width, 1)
    queries = (
        jnp.dot(
            embed_full.reshape(group_size * kept_count, width),
            query_columns,
            preferred_element_type=jnp.float32,
        )
        .astype(jnp.bfloat16)
        .reshape(group_size, kept_count, head_width)
    )
    attended = lax.map(attend_slot, (queries, history_kv, history_bias, history_length))
    attend_full = lax.all_gather(attended, "narrow", axis=2, tiled=True)
    rows_all = group_size * kept_count
    mixed_in = embed_full.reshape(rows_all, width).astype(jnp.float32) + attend_full.reshape(
        rows_all, width
    ).astype(jnp.float32)
    normed = (
        mixed_in
        * lax.rsqrt(jnp.mean(mixed_in * mixed_in, axis=1, keepdims=True) + 1e-06)
        * norm_gain
    ).astype(jnp.bfloat16)
    expert_out = jax.nn.relu(
        jnp.einsum("kd,edh->keh", normed, expert_weight, preferred_element_type=jnp.float32)
    ).astype(jnp.bfloat16)
    gate_cols = lax.dynamic_slice_in_dim(
        gate_weight, narrow_rank * tasks_here * experts_all, tasks_here * experts_all, 1
    )
    gate_offsets = lax.dynamic_slice_in_dim(gate_bias, narrow_rank * tasks_here, tasks_here, 0)
    logits = (
        jnp.dot(normed, gate_cols, preferred_element_type=jnp.float32).reshape(
            rows_all, tasks_here, experts_all
        )
        + gate_offsets[None]
    )
    logit_max = jnp.max(logits, axis=2, keepdims=True)
    gate_pow = jnp.exp(logits - logit_max)
    gate_probs = (gate_pow / jnp.sum(gate_pow, axis=2, keepdims=True)).astype(jnp.bfloat16)
    mixture = jnp.einsum(
        "kte,keh->kth",
        gate_probs,
        lax.all_gather(expert_out, "narrow", axis=1, tiled=True),
        preferred_element_type=jnp.float32,
    ).astype(jnp.bfloat16)
    tower_act = jax.nn.relu(
        jnp.einsum("kth,thj->ktj", mixture, tower_inner, preferred_element_type=jnp.float32)
    ).astype(jnp.bfloat16)
    task_logit = jnp.einsum(
        "ktj,tj->kt", tower_act, tower_outer, preferred_element_type=jnp.float32
    )
    task_logit = task_logit.reshape(group_size, kept_count, tasks_here)
    positions = jnp.arange(shards, dtype=jnp.int32)
    shard_at = positions % wide_count * narrow_count + positions // wide_count
    slot_starts = starts[:, shard_at]
    slot_counts = counts[:, shard_at]
    lanes = jnp.arange(capacity, dtype=jnp.int32)
    source_rows = jnp.minimum(
        slot_starts[:, :, None] + lanes[None, None, :], kept_count - 1
    ).reshape(group_size, shards * capacity)
    gathered = jnp.take_along_axis(task_logit, source_rows[:, :, None], axis=1).reshape(
        group_size, shards, capacity, tasks_here
    )
    filled = lanes[None, None, :] < slot_counts[:, :, None]
    returning = jnp.where(filled[:, :, :, None], gathered, 0.0).reshape(
        group_size, narrow_count, wide_count, capacity, tasks_here
    )
    returned = lax.all_to_all(
        lax.all_to_all(returning, "wide", split_axis=2, concat_axis=0, tiled=True),
        "narrow",
        split_axis=1,
        concat_axis=4,
        tiled=True,
    )
    returned = returned.reshape(requests, capacity, -1)
    request_ids = jnp.arange(requests, dtype=jnp.int32)
    slot_of = jnp.sum(
        jnp.where(slot_request[None, :] == request_ids[:, None], request_ids[None, :], 0), axis=1
    )
    by_request = returned[slot_of]
    rank_score = jnp.einsum(
        "rcs,rct->trs", packing.astype(jnp.float32), by_request, precision=lax.Precision.HIGHEST
    )
    return (prerank_score, rank_score)


def solution(mesh):
    return jax.shard_map(
        on_device,
        mesh=mesh,
        in_specs=(
            P("groups", ("wide", "narrow"), None),
            P(),
            P(),
            P(),
            P("groups", None),
            P("groups", None),
            P("groups"),
            P(("groups", "wide"), None, None, "narrow"),
            P(("groups", "wide"), "narrow", None),
            P(("groups", "wide")),
            P(),
            P(),
            P("narrow", None, None),
            P(),
            P(),
            P("narrow", None, None),
            P("narrow", None),
        ),
        out_specs=(P("groups", ("wide", "narrow")), P(None, "groups", ("wide", "narrow"))),
        check_vma=False,
    )
```

profile of v0, /device:TPU:0, one launch (start us, length us, event | category | flops | bytes accessed | tf_op | source)
XLA Modules:
  0.0 108.9 jit_solution(12506975519350942500)
XLA Ops:
  7.2 0.8 broadcast_subtract_fusion
  9.7 2.5 %convolution_convert_fusion = bf16[1024,512]{1,0:T(8,128)(2,1)S(1)} fusion(bf16[512,512]{1,0:T(8,128)(2,1)} %param.20, bf16[1024,512]{1,0:T(8,128)(2,1)S(1)} %bitcast.140, bf16[512,512]{1,0:T(8,128)(2,1)} %param.18, f32[512]{0:T(512)} %param.19), kind=kOutput, calls=%fused_computation.24 | convolution fusion | flops 1075838976 | bytes 3147776 | tf_op jit(solution)/shard_map/dot_general | solution.py:74
  12.5 1.4 %gather_fusion.2 = bf16[8,64,512]{2,1,0:T(8,128)(2,1)} fusion(bf16[8,64,512]{2,1,0:T(8,128)(2,1)S(1)} %convolution_convert_fusion.1, s32[1024]{0:T(1024)S(1)} %pad_clamp_fusion.2), kind=kCustom, calls=%fused_computation.2 | custom fusion | bytes 1048608 | tf_op jit(solution)/shard_map/gather | solution.py:91
  13.8 7.3 %all-to-all-start = ((bf16[8,1,64,512]{3,2,1,0:T(8,128)(2,1)}), bf16[8,1,64,512]{3,2,1,0:T(8,128)(2,1)S(1)}, u32[]{:S(2)}, u32[]{:S(2)}) async-start(bf16[8,1,64,512]{3,2,1,0:T(8,128)(2,1)} %bitcast.32), calls=%async_computation | async-start | bytes 1048576 | tf_op jit(solution)/shard_map/all_to_all | solution.py:95
  23.0 1.1 fusion.74
  27.6 4.4 %compare_select_fusion.3 = (s32[512,1]{0,1:T(1,128)S(1)}, s32[512,1]{0,1:T(1,128)S(1)}) fusion(s32[]{:T(128)} %bitcast.23, s32[]{:T(128)} %bitcast.24, s32[]{:T(128)} %bitcast.25, s32[]{:T(128)} %bitcast.26, s32[]{:T(128)} %bitcast.27, s32[]{:T(128)} %bitcast.29, s32[]{:T(128)} %bitcast.28, s32[512,1]{0,1:T(1,128)S(1)} %bitcast.158), kind=kLoop, calls=%fused_computation.90 | loop fusion | flops 7680 | bytes 6172 | tf_op jit(solution)/shard_map/jit(take_along_axis)/gather | solution.py:117
  32.0 5.6 %compare_and_fusion.1 = (pred[512]{0:T(512)(128)(4,1)S(1)}, s32[512]{0:T(512)S(1)}) fusion(s32[512]{0:T(512)S(1)} %convert_reduce_fusion, pred[512]{0:T(512)(128)(4,1)S(1)} %get-tuple-element.58, pred[512]{0:T(512)(128)(4,1)S(1)} %get-tuple-element.56, pred[512]{0:T(512)(128)(4,1)S(1)} %get-tuple-element.57, pred[512]{0:T(512)(128)(4,1)S(1)} %get-tuple-element.55, ...), kind=kLoop, calls=%fused_computation.142 | loop fusion | flops 23040 | bytes 11300 | tf_op jit(solution)/shard_map/jit(take_along_axis)/and | solution.py:120
  37.7 0.8 copy.52
  38.5 0.9 reshape.1055
  39.4 4.2 %all_to_all.60 = bf16[2,2,65536]{2,1,0:T(2,128)(2,1)S(1)} all-to-all(bf16[2,2,65536]{2,1,0:T(2,128)(2,1)S(1)} %reshape.1055), channel_id=1, replica_groups=mesh['groups'=2,'wide'=8,'narrow'=2] {'narrow'}, dimensions={0} | all-to-all | bytes 1048576 | tf_op jit(solution)/shard_map/all_to_all | solution.py:94
  44.9 2.0 %gather_fusion.3 = bf16[512,256]{1,0:T(8,128)(2,1)S(1)} fusion(bf16[1024,256]{1,0:T(8,128)(2,1)S(1)} %bitcast.144, s32[1024]{0:T(1024)S(1)} %pad_clamp_fusion.1), kind=kCustom, calls=%fused_computation.3 | custom fusion | bytes 526336 | tf_op jit(solution)/shard_map/jit(take_along_axis)/gather | solution.py:120
  47.0 2.2 %all_gather.9 = bf16[1,512,512]{2,1,0:T(8,128)(2,1)S(1)} all-gather(bf16[1,512,256]{2,1,0:T(8,128)(2,1)S(1)} %bitcast_select_fusion), channel_id=1, replica_groups=mesh['groups'=2,'wide'=8,'narrow'=2] {'narrow'}, dimensions={2}, use_global_device_ids=true | all-gather | bytes 786432 | tf_op jit(solution)/shard_map/all_gather | solution.py:123
  49.2 1.3 %convolution_convert_fusion.2 = bf16[512,256]{0,1:T(8,128)(2,1)S(1)} fusion(bf16[1,512,512]{2,1,0:T(8,128)(2,1)S(1)} %all_gather.9, bf16[512,512]{1,0:T(8,128)(2,1)} %param.27, s32[]{:T(128)S(6)} %select_n.397), kind=kOutput, calls=%fused_computation.32 | convolution fusion | flops 134348800 | bytes 1048580 | tf_op jit(solution)/shard_map/dot_general | solution.py:126
  50.5 3.6 %fusion.76 = (f32[4,512]{1,0:T(4,128)S(1)}, f32[4,512,512]{1,2,0:T(8,128)}) fusion(f32[4,512]{1,0:T(4,128)S(1)} %bitcast.167, pred[512]{0:T(512)(128)(4,1)S(1)} %iota_compare_fusion.6, bf16[512,4,64]{0,2,1:T(8,128)(2,1)S(1)} %bitcast.154, bf16[512,4,64]{0,2,1:T(8,128)(2,1)S(1)} %bitcast.152), kind=kOutput, calls=%fused_computation.163 | convolution fusion | flops 139461120 | bytes 4735488 | tf_op jit(solution)/shard_map/while/body/eval_jaxpr/sub | solution.py:23
  54.0 2.7 %fusion.17 = bf16[4,512,64]{1,2,0:T(8,128)(2,1)S(1)} fusion(bf16[512,4,64]{0,2,1:T(8,128)(2,1)S(1)} %bitcast.151, f32[4,512,512]{1,2,0:T(8,128)} %get-tuple-element.82, f32[4,512]{1,0:T(4,128)S(1)} %get-tuple-element.81), kind=kOutput, calls=%fused_computation.33 | convolution fusion | flops 136445952 | bytes 4726784 | tf_op jit(solution)/shard_map/while/body/eval_jaxpr/hkl,lhd->khd/dot_general | solution.py:25
  56.9 2.4 %all_gather.10 = bf16[1,512,512]{2,1,0:T(8,128)(2,1)S(1)} all-gather(bf16[1,512,256]{2,1,0:T(8,128)(2,1)S(1)} %copy.57), channel_id=1, replica_groups=mesh['groups'=2,'wide'=8,'narrow'=2] {'narrow'}, dimensions={2}, use_global_device_ids=true | all-gather | bytes 786432 | tf_op jit(solution)/shard_map/all_gather | solution.py:135
  59.5 3.0 %maximum_convert_fusion = bf16[512,4,256]{2,0,1:T(8,128)(2,1)} fusion(bf16[4,512,256]{2,1,0:T(8,128)(2,1)} %param.29, bf16[1,512,512]{2,1,0:T(8,128)(2,1)S(1)} %all_gather.10, bf16[1,512,512]{2,1,0:T(8,128)(2,1)S(1)} %all_gather.9, f32[512]{0:T(512)S(1)} %copy-done.8, f32[512]{0:T(512)S(1)} %add_rsqrt_fusion), kind=kOutput, calls=%fused_computation.14 | convolution fusion | flops 539492352 | bytes 3149824 | tf_op jit(solution)/shard_map/kd,edh->keh/dot_general | solution.py:146
  64.8 1.0 fusion.51
  66.5 8.1 %all-gather.2.cloned.1.call-done = bf16[512,8,256]{2,0,1:T(8,128)(2,1)} async-done(((bf16[512,4,256]{2,0,1:T(8,128)(2,1)}), bf16[512,8,256]{2,0,1:T(8,128)(2,1)}) %all-gather.2.cloned.1.call-update) | async-done | bytes 2097168 | tf_op jit(solution)/shard_map/all_gather | solution.py:164
  74.7 3.1 %fusion.11 = bf16[512,4,256]{2,1,0:T(4,128)(2,1)S(1)} fusion(bf16[512,4,8]{2,1,0:T(4,128)(2,1)S(1)} %copy.58, bf16[512,8,256]{2,0,1:T(8,128)(2,1)} %all-gather.2.cloned.1.call-done), kind=kOutput, calls=%fused_computation.23 | convolution fusion | flops 8912896 | bytes 3178496 | tf_op jit(solution)/shard_map/kte,keh->kth/dot_general | solution.py:161
  78.6 2.8 %gather_fusion.4 = f32[1024,4]{1,0:T(8,128)S(1)} fusion(f32[512,4]{1,0:T(8,128)S(1)} %bitcast.143, s32[1024]{0:T(1024)S(1)} %broadcast_clamp_fusion), kind=kCustom, calls=%fused_computation.4 | custom fusion | bytes 36864 | tf_op jit(solution)/shard_map/jit(take_along_axis)/gather | solution.py:182
  82.3 5.8 %all-to-all-start.2 = ((f32[8,1,512]{2,1,0:T(1,128)}), f32[8,1,512]{2,1,0:T(1,128)S(1)}, u32[]{:S(2)}, u32[]{:S(2)}) async-start(f32[8,1,512]{2,1,0:T(1,128)} %reshape.1057), calls=%async_computation.2 | async-start | bytes 32768 | tf_op jit(solution)/shard_map/all_to_all | solution.py:190
  88.1 6.6 %all-to-all-done.2 = f32[8,1,512]{2,1,0:T(1,128)S(1)} async-done(((f32[8,1,512]{2,1,0:T(1,128)}), f32[8,1,512]{2,1,0:T(1,128)S(1)}, u32[]{:S(2)}, u32[]{:S(2)}) %all-to-all-start.2) | async-done | bytes 16416 | tf_op jit(solution)/shard_map/all_to_all | solution.py:190
  96.1 3.7 %all_to_all.61 = f32[2,1,2048]{2,1,0:T(1,128)S(1)} all-to-all(f32[2,1,2048]{2,1,0:T(1,128)S(1)} %reshape.1059), channel_id=1, replica_groups=mesh['groups'=2,'wide'=8,'narrow'=2] {'narrow'}, dimensions={0} | all-to-all | bytes 32768 | tf_op jit(solution)/shard_map/all_to_all | solution.py:189
  (91 shorter events, 14.9 us)
Async XLA Ops:
  7.2 2.5 %copy-start = (bf16[8,128,512]{2,1,0:T(8,128)(2,1)S(1)}, bf16[8,128,512]{2,1,0:T(8,128)(2,1)}, u32[]{:S(2)}) copy-start(bf16[8,128,512]{2,1,0:T(8,128)(2,1)} %param.17) | copy-start | bytes 3145732
  12.1 12.0 %copy-start.1 = (bf16[1024,512]{1,0:T(8,128)(2,1)}, bf16[1024,512]{1,0:T(8,128)(2,1)S(1)}, u32[]{:S(2)}) copy-start(bf16[1024,512]{1,0:T(8,128)(2,1)S(1)} %convolution_convert_fusion) | copy-start | bytes 3145732
  12.1 9.0 %copy-start.10 = (s32[8]{0:T(128)S(1)}, s32[8]{0:T(128)}, u32[]{:S(2)}) copy-start(s32[8]{0:T(128)} %param.23) | copy-start | bytes 100
  13.8 23.9 %all-to-all-start = ((bf16[8,1,64,512]{3,2,1,0:T(8,128)(2,1)}), bf16[8,1,64,512]{3,2,1,0:T(8,128)(2,1)S(1)}, u32[]{:S(2)}, u32[]{:S(2)}) async-start(bf16[8,1,64,512]{3,2,1,0:T(8,128)(2,1)} %bitcast.32), calls=%async_computation | async-start | bytes 1048576 | tf_op jit(solution)/shard_map/all_to_all | solution.py:95
  21.1 53.6 %all-gather.2.cloned.1.call-start = ((), (), s32[]{:S(2)}) async-start(), calls=%async_computation.4 | async-start | bytes 3145728 | tf_op jit(solution)/shard_map/all_gather | solution.py:164
  44.9 5.6 %copy-start.7 = (f32[1,4,512]{2,1,0:T(4,128)S(1)}, f32[1,4,512]{2,1,0:T(4,128)}, u32[]{:S(2)}) copy-start(f32[1,4,512]{2,1,0:T(4,128)} %param.25) | copy-start | bytes 24580
  56.7 2.8 %copy-start.8 = (f32[512]{0:T(512)S(1)}, f32[512]{0:T(512)}, u32[]{:S(2)}) copy-start(f32[512]{0:T(512)} %param.28) | copy-start | bytes 6148
  62.5 2.0 %copy-start.4 = (f32[8,8]{1,0:T(8,128)S(1)}, f32[8,8]{1,0:T(8,128)}, u32[]{:S(2)}) copy-start(f32[8,8]{1,0:T(8,128)} %param.31) | copy-start | bytes 772
  62.5 2.2 %copy-start.2 = (bf16[1024,512]{1,0:T(8,128)(2,1)S(1)}, bf16[1024,512]{1,0:T(8,128)(2,1)}, u32[]{:S(2)}) copy-start(bf16[1024,512]{1,0:T(8,128)(2,1)} %copy-done.1) | copy-start | bytes 3145732
  62.5 2.3 %copy-start.3 = (bf16[8,512]{1,0:T(8,128)(2,1)S(1)}, bf16[8,512]{1,0:T(8,128)(2,1)}, u32[]{:S(2)}) copy-start(bf16[8,512]{1,0:T(8,128)(2,1)} %param.21) | copy-start | bytes 24580
  62.5 3.2 %copy-start.6 = (bf16[512,64]{0,1:T(8,128)(2,1)S(1)}, bf16[512,64]{0,1:T(8,128)(2,1)}, u32[]{:S(2)}) copy-start(bf16[512,64]{0,1:T(8,128)(2,1)} %param.30) | copy-start | bytes 196612
  66.2 11.6 %copy-start.5 = (bf16[4,256,128]{2,1,0:T(8,128)(2,1)S(1)}, bf16[4,256,128]{2,1,0:T(8,128)(2,1)}, u32[]{:S(2)}) copy-start(bf16[4,256,128]{2,1,0:T(8,128)(2,1)} %param.32) | copy-start | bytes 786436
  66.2 11.6 %copy-start.9 = (bf16[4,128]{1,0:T(4,128)(2,1)S(1)}, bf16[4,128]{1,0:T(4,128)(2,1)}, u32[]{:S(2)}) copy-start(bf16[4,128]{1,0:T(4,128)(2,1)} %param.33) | copy-start | bytes 3076
  82.3 12.3 %all-to-all-start.2 = ((f32[8,1,512]{2,1,0:T(1,128)}), f32[8,1,512]{2,1,0:T(1,128)S(1)}, u32[]{:S(2)}, u32[]{:S(2)}) async-start(f32[8,1,512]{2,1,0:T(1,128)} %reshape.1057), calls=%async_computation.2 | async-start | bytes 32768 | tf_op jit(solution)/shard_map/all_to_all | solution.py:190
Sparse Core Ops, SparseCore 0:
  62.7 11.9 all-gather.1
where the time goes:
time: 110 us; the launch traced here: 109 us
  matrix products  18.6 us (17%)
  local copies, waits for them, and re-layouts  17.9 us (16%)
  between operations  17 us (15%)
  other arithmetic  15.1 us (14%)
  waiting for transfers between devices  14.7 us (13%)
  starting transfers between devices  13.1 us (12%)
  blocking collectives  12.4 us (11%)
    all_gather x1, waiting for transfers between devices, on_device(): lax.all_gather(expert_out, 'narrow', axis=1, tiled=True)  8.12 us
    all_to_all x1, starting transfers between devices, on_device(): lax.all_to_all(sending, 'wide', split_axis=0, concat_axis=1, tiled=True)  7.26 us
    all_to_all x1, waiting for transfers between devices, on_device(): lax.all_to_all(returning, 'wide', split_axis=2, concat_axis=0, tiled=True)  6.57 us
    all_to_all x1, starting transfers between devices, on_device(): lax.all_to_all(returning, 'wide', split_axis=2, concat_axis=0, tiled=True)  5.77 us
    and x1, other arithmetic, on_device(): jnp.take_along_axis(arrived.reshape(group_size, shards * capacity, -1), f...  5.6 us
    gather x2, other arithmetic, on_device(): within = row_ranks[None, :] - jnp.take_along_axis(starts, block_at, axis=1)  4.48 us
    all_to_all x1, blocking collectives, on_device(): lax.all_to_all(lax.all_to_all(sending, 'wide', split_axis=0, concat_axis=...  4.15 us
    all_to_all x1, blocking collectives, on_device(): lax.all_to_all(lax.all_to_all(returning, 'wide', split_axis=2, concat_axi...  3.72 us
  transfers between devices with their start and end apart: 3, of which 2 were waited for; matrix products, arithmetic and copies ran while one was open for 16% of the time, Pallas kernels for 0%

commit v1 on v0

v1 whole, which is shorter than its diff:
```python
import functools

import jax
import jax.numpy as jnp
from jax import lax
from jax.experimental import pallas as pl
from jax.experimental.pallas import tpu as pltpu
from jax.sharding import PartitionSpec as P

NT = (((1,), (1,)), ((), ()))
VMEM = pl.BlockSpec(memory_space=pltpu.VMEM)
SMEM = pl.BlockSpec(memory_space=pltpu.SMEM)
ANY = pl.BlockSpec(memory_space=pl.ANY)
VMEM_LIMIT = 40 * 1024 * 1024


def dot_f32(a, b):
    return jnp.dot(a, b, preferred_element_type=jnp.float32)


def dot_nt(a, b):
    return lax.dot_general(a, b, NT, preferred_element_type=jnp.float32)


def split_by(values, divisor):
    if divisor & (divisor - 1) == 0:
        shift = divisor.bit_length() - 1
        return lax.shift_right_logical(values, shift), values & (divisor - 1)
    quotient = lax.div(values, divisor)
    return quotient, values - quotient * divisor


def three_parts(values):
    high = values.astype(jnp.bfloat16)
    rest = values - high.astype(jnp.float32)
    middle = rest.astype(jnp.bfloat16)
    low = (rest - middle.astype(jnp.float32)).astype(jnp.bfloat16)
    return jnp.concatenate([high, middle, low], axis=0)


def sum_parts(stacked, rows):
    return stacked[:rows] + stacked[rows : 2 * rows] + stacked[2 * rows :]


def pack_body(narrow_count, half, where_ref, slot_ref, kept_ref, cand_hbm, out_ref, lane_ref, cand_ref, sems):
    requests, shard_len, _ = cand_ref.shape
    kept_count = kept_ref.shape[1]
    copies = [
        pltpu.make_async_copy(cand_hbm.at[r], cand_ref.at[r], sems.at[r]) for r in range(requests)
    ]
    for copy in copies:
        copy.start()
    base = where_ref[0] * shard_len
    ids = base + lax.broadcasted_iota(jnp.int32, (shard_len, kept_count), 0)
    request_rows = lax.broadcasted_iota(jnp.int32, (requests, kept_count), 0)
    flags = jnp.zeros((requests, shard_len), jnp.float32)
    for r in range(requests):
        hits = jnp.where(kept_ref[r : r + 1, :] == ids, 1.0, 0.0).astype(jnp.bfloat16)
        row = jnp.where(request_rows == r, 1.0, 0.0).astype(jnp.bfloat16)
        flags = flags + dot_nt(row, hits)
    earlier = lax.broadcasted_iota(jnp.int32, (shard_len, shard_len), 0) < lax.broadcasted_iota(
        jnp.int32, (shard_len, shard_len), 1
    )
    places = dot_f32(
        flags.astype(jnp.bfloat16), jnp.where(earlier, 1.0, 0.0).astype(jnp.bfloat16)
    ).astype(jnp.int32)
    before = jnp.sum((kept_ref[...] < base).astype(jnp.int32), axis=1, keepdims=True)
    _, owner = split_by(before + places, narrow_count)
    within, _ = split_by(places, narrow_count)
    lane_ref[...] = jnp.where(flags > 0.5, owner * half + within, -1)
    rows = narrow_count * half
    row_at = lax.broadcasted_iota(jnp.int32, (rows, shard_len), 0)
    for copy in copies:
        copy.wait()
    for s in range(requests):
        r = slot_ref[s]
        pick = jnp.where(lane_ref[pl.ds(r, 1), :] == row_at, 1.0, 0.0).astype(jnp.bfloat16)
        out_ref[s * rows : (s + 1) * rows, :] = dot_f32(pick, cand_ref[r]).astype(jnp.bfloat16)


def pack_rows(where, slot_request, kept_index, candidates, narrow_count, half):
    requests, shard_len, features = candidates.shape
    rows = requests * narrow_count * half
    return pl.pallas_call(
        functools.partial(pack_body, narrow_count, half),
        out_shape=(
            jax.ShapeDtypeStruct((rows, features), jnp.bfloat16),
            jax.ShapeDtypeStruct((requests, shard_len), jnp.int32),
        ),
        in_specs=[SMEM, SMEM, VMEM, ANY],
        out_specs=(VMEM, VMEM),
        scratch_shapes=[
            pltpu.VMEM((requests, shard_len, features), jnp.bfloat16),
            pltpu.SemaphoreType.DMA((requests,)),
        ],
        compiler_params=pltpu.CompilerParams(vmem_limit_bytes=VMEM_LIMIT),
        cost_estimate=pl.CostEstimate(
            flops=2 * rows * shard_len * features, bytes_accessed=4 * rows * features, transcendentals=0
        ),
        name="pack_rows",
    )(where, slot_request, kept_index, candidates)


def prerank_body(shard_len, cand_ref, inner_ref, bias_ref, outer_ref, user_ref, lane_ref, out_ref):
    requests = user_ref.shape[0]
    step = 2 if requests % 2 == 0 else 1
    for r in range(0, requests, step):
        rows = cand_ref[r * shard_len : (r + step) * shard_len, :]
        hidden = jnp.maximum(dot_f32(rows, inner_ref[...]) + bias_ref[...], 0.0).astype(jnp.bfloat16)
        embedded = dot_f32(hidden, outer_ref[...]).astype(jnp.bfloat16)
        scores = dot_nt(user_ref[...], embedded)
        for i in range(step):
            out_ref[r + i : r + i + 1, :] = scores[r + i : r + i + 1, i * shard_len : (i + 1) * shard_len]


def prerank(candidates, pre_inner, pre_bias, pre_outer, user_vector, lanes):
    requests, shard_len, features = candidates.shape
    rows = requests * shard_len
    return pl.pallas_call(
        functools.partial(prerank_body, shard_len),
        out_shape=jax.ShapeDtypeStruct((requests, shard_len), jnp.float32),
        in_specs=[VMEM] * 6,
        out_specs=VMEM,
        compiler_params=pltpu.CompilerParams(vmem_limit_bytes=VMEM_LIMIT),
        cost_estimate=pl.CostEstimate(
            flops=4 * rows * features * pre_inner.shape[1], bytes_accessed=4 * rows * features, transcendentals=0
        ),
        name="prerank",
    )(
        candidates.reshape(rows, features),
        pre_inner,
        pre_bias.reshape(1, -1),
        pre_outer,
        user_vector,
        lanes,
    )


def rank_body(
    narrow_count,
    shards,
    shard_len,
    spread,
    where_ref,
    kept_ref,
    arrived_hbm,
    inner_hbm,
    bias_ref,
    outer_hbm,
    query_hbm,
    gain_ref,
    gate_hbm,
    gate_bias_ref,
    *rest,
):
    history_hbm = rest[:narrow_count]
    history_bias_refs = rest[narrow_count : 2 * narrow_count]
    expert_hbm = rest[2 * narrow_count : 3 * narrow_count]
    tower_hbm = rest[3 * narrow_count : 4 * narrow_count]
    tower_outer_refs = rest[4 * narrow_count : 5 * narrow_count]
    (
        out_ref,
        arrived_ref,
        inner_ref,
        outer_ref,
        query_ref,
        gate_ref,
        history_ref,
        expert_ref,
        tower_ref,
        embed_ref,
        queries_ref,
        attended_ref,
        expert_out_ref,
        gates_ref,
        mixture_ref,
        logit_ref,
        sems,
    ) = rest[5 * narrow_count :]
    rows_in = arrived_ref.shape[0]
    width = arrived_ref.shape[1]
    half = rows_in // shards
    rows = embed_ref.shape[0]
    span = history_ref.shape[2]
    head_columns = history_ref.shape[3]
    heads_here = history_bias_refs[0].shape[0]
    head_size = head_columns // heads_here
    experts_here = expert_ref.shape[1]
    experts = narrow_count * experts_here
    tasks_here = tower_ref.shape[1]
    tasks = narrow_count * tasks_here
    block = rows // experts
    expert_width = expert_ref.shape[3]

    me = where_ref[0]
    length = where_ref[1]
    pairs = [
        (arrived_hbm, arrived_ref),
        (inner_hbm, inner_ref),
        (outer_hbm, outer_ref),
        (query_hbm, query_ref),
        (gate_hbm, gate_ref),
    ]
    pairs += [(history_hbm[i], history_ref.at[i]) for i in range(narrow_count)]
    pairs += [(expert_hbm[i], expert_ref.at[i]) for i in range(narrow_count)]
    pairs += [(tower_hbm[i], tower_ref.at[i]) for i in range(narrow_count)]
    copies = [pltpu.make_async_copy(src, dst, sems.at[i]) for i, (src, dst) in enumerate(pairs)]
    for copy in copies:
        copy.start()

    kept_row = kept_ref[...]
    sources = lax.broadcasted_iota(jnp.int32, (shards, kept_row.shape[1]), 0)
    edge = sources * shard_len
    starts = jnp.sum((kept_row < edge).astype(jnp.int32), axis=1, keepdims=True)
    ends = jnp.sum((kept_row < edge + shard_len).astype(jnp.int32), axis=1, keepdims=True)
    first, _ = split_by(starts + (narrow_count - 1) - me, narrow_count)
    last, _ = split_by(ends + (narrow_count - 1) - me, narrow_count)
    lane_source, lane_within = split_by(lax.broadcasted_iota(jnp.int32, (shards, rows_in), 1), half)
    mine = lane_source == lax.broadcasted_iota(jnp.int32, (shards, rows_in), 0)
    target = jnp.where(mine & (first + lane_within < last), first + lane_within + 1, 0)
    target = jnp.sum(target, axis=0, keepdims=True) - 1
    placing = jnp.where(
        target == lax.broadcasted_iota(jnp.int32, (rows, rows_in), 0), 1.0, 0.0
    ).astype(jnp.bfloat16)

    copies[0].wait()
    packed = dot_f32(placing, arrived_ref[...]).astype(jnp.bfloat16)
    copies[1].wait()
    hidden = jnp.maximum(dot_f32(packed, inner_ref[...]) + bias_ref[...], 0.0).astype(jnp.bfloat16)
    copies[2].wait()
    embed = dot_f32(hidden, outer_ref[...]).astype(jnp.bfloat16)
    embed_ref[...] = embed
    copies[3].wait()
    queries = dot_f32(embed, query_ref[...]).astype(jnp.bfloat16)
    queries_ref[...] = queries

    tile = max(head_size, 128)
    in_tile = tile // head_size
    lane_head, _ = split_by(lax.broadcasted_iota(jnp.int32, (1, tile), 1), head_size)
    visible = lax.broadcasted_iota(jnp.int32, (1, span), 1) < length
    scale = float(head_size) ** (-0.5)
    for i in range(narrow_count):
        copies[5 + i].wait()
        at = lax.rem(me + i, narrow_count) * head_columns
        for t in range(head_columns // tile):
            columns = pl.ds(pl.multiple_of(at + t * tile, tile), tile)
            query_tile = queries_ref[:, columns]
            keys = history_ref[i, 0, :, t * tile : (t + 1) * tile]
            values = history_ref[i, 1, :, t * tile : (t + 1) * tile]
            merged = None
            for h in range(in_tile):
                own = lane_head == h
                head = t * in_tile + h
                masked = jnp.where(own, query_tile, jnp.zeros_like(query_tile))
                scores = dot_nt(masked, keys) * scale
                offset = jnp.where(visible, history_bias_refs[i][head : head + 1, :], -jnp.inf)
                scores = scores + offset
                powers = jnp.exp(scores - jnp.max(scores, axis=1, keepdims=True))
                total = jnp.sum(powers, axis=1, keepdims=True)
                result = dot_f32(powers.astype(jnp.bfloat16), values) / total
                merged = result if merged is None else jnp.where(own, result, merged)
            attended_ref[:, columns] = merged.astype(jnp.bfloat16)

    mixed_in = embed_ref[...].astype(jnp.float32) + attended_ref[...].astype(jnp.float32)
    normed = (
        mixed_in
        * lax.rsqrt(jnp.mean(mixed_in * mixed_in, axis=1, keepdims=True) + 1e-06)
        * gain_ref[...]
    ).astype(jnp.bfloat16)

    copies[4].wait()
    logits = dot_f32(normed, gate_ref[...]) + gate_bias_ref[...]
    by_task = jnp.transpose(logits).reshape(tasks, experts, rows)
    gate_pow = jnp.exp(by_task - jnp.max(by_task, axis=1, keepdims=True))
    gate_probs = gate_pow / jnp.sum(gate_pow, axis=1, keepdims=True)
    gates = jnp.transpose(gate_probs.reshape(tasks * experts, rows)).astype(jnp.bfloat16)

    blocks = rows // block
    for i in range(narrow_count):
        copies[5 + narrow_count + i].wait()
        for e in range(experts_here):
            result = jnp.maximum(dot_f32(normed, expert_ref[i, e]), 0.0).astype(jnp.bfloat16)
            at = (i * experts_here + e) * block
            for b in range(blocks):
                expert_out_ref[b, at : at + block, :] = result[b * block : (b + 1) * block, :]

    gate_at = lax.broadcasted_iota(jnp.int32, (tasks * experts, experts * block), 0)
    column = lax.broadcasted_iota(jnp.int32, (tasks * experts, experts * block), 1)
    column_expert, _ = split_by(column, block)
    _, column_expert = split_by(column_expert + me * experts_here, experts)
    _, row_in_block = split_by(lax.broadcasted_iota(jnp.int32, (rows, experts * block), 0), block)
    _, column_row = split_by(lax.broadcasted_iota(jnp.int32, (rows, experts * block), 1), block)
    diagonal = row_in_block == column_row
    for t in range(tasks):
        expand = jnp.where(gate_at == column_expert + t * experts, 1.0, 0.0).astype(jnp.bfloat16)
        wide = jnp.where(diagonal, dot_f32(gates, expand), 0.0).astype(jnp.bfloat16)
        for b in range(blocks):
            gates_ref[b, t * block : (t + 1) * block, :] = wide[b * block : (b + 1) * block, :]
    for b in range(blocks):
        mixture = dot_f32(gates_ref[b], expert_out_ref[b]).astype(jnp.bfloat16)
        for t in range(tasks):
            mixture_ref[t, b * block : (b + 1) * block, :] = mixture[t * block : (t + 1) * block, :]

    for i in range(narrow_count):
        copies[5 + 2 * narrow_count + i].wait()
        first_task = lax.rem(me + i, narrow_count) * tasks_here
        for t in range(tasks_here):
            task = first_task + t
            act = jnp.maximum(dot_f32(mixture_ref[task], tower_ref[i, t]), 0.0).astype(jnp.bfloat16)
            logit = dot_nt(tower_outer_refs[i][...], act)
            logit_ref[pl.ds(task, 1), :] = logit[t : t + 1, :]

    parts = three_parts(logit_ref[...])
    returned = sum_parts(dot_f32(parts, placing), tasks)
    if not spread:
        out_ref[...] = returned
        return
    lanes = out_ref.shape[2]
    lane = lax.broadcasted_iota(jnp.int32, (tasks, lanes), 1)
    keep = (lane >= me * half) & (lane < (me + 1) * half)
    per_tile = lanes // half
    for s in range(shards):
        tile_at, place = divmod(s, per_tile)
        values = returned[:, tile_at * lanes : (tile_at + 1) * lanes]
        moved = pltpu.roll(values, lax.rem(me * half + (lanes - place * half), lanes), 1)
        out_ref[s] = jnp.where(keep, moved, 0.0)


def rank_slot(
    where,
    kept,
    arrived,
    pre_inner,
    pre_bias,
    pre_outer,
    query_weight,
    norm_gain,
    gate_weight,
    gate_bias,
    history,
    history_bias,
    experts,
    towers,
    tower_outer,
    shards,
    shard_len,
    spread,
):
    narrow_count = len(history)
    rows_in, width = arrived.shape
    kept_count = kept.shape[1]
    rows = kept_count // narrow_count
    tasks = narrow_count * towers[0].shape[0]
    expert_count = narrow_count * experts[0].shape[0]
    expert_width = experts[0].shape[2]
    block = rows // expert_count
    if spread:
        out_shape = jax.ShapeDtypeStruct((shards, tasks, 128), jnp.float32)
    else:
        out_shape = jax.ShapeDtypeStruct((tasks, rows_in), jnp.float32)
    bf16 = jnp.bfloat16
    flops = 2 * rows * (rows_in * width + 3 * width * width + 2 * expert_count * width * expert_width)
    return pl.pallas_call(
        functools.partial(rank_body, narrow_count, shards, shard_len, spread),
        out_shape=out_shape,
        in_specs=[SMEM, VMEM, ANY, ANY, VMEM, ANY, ANY, VMEM, ANY, VMEM]
        + [ANY] * narrow_count
        + [VMEM] * narrow_count
        + [ANY] * narrow_count
        + [ANY] * narrow_count
        + [VMEM] * narrow_count,
        out_specs=VMEM,
        scratch_shapes=[
            pltpu.VMEM(arrived.shape, bf16),
            pltpu.VMEM(pre_inner.shape, bf16),
            pltpu.VMEM(pre_outer.shape, bf16),
            pltpu.VMEM(query_weight.shape, bf16),
            pltpu.VMEM(gate_weight.shape, bf16),
            pltpu.VMEM((narrow_count,) + history[0].shape, bf16),
            pltpu.VMEM((narrow_count,) + experts[0].shape, bf16),
            pltpu.VMEM((narrow_count,) + towers[0].shape, bf16),
            pltpu.VMEM((rows, pre_outer.shape[1]), bf16),
            pltpu.VMEM((rows, query_weight.shape[1]), bf16),
            pltpu.VMEM((rows, query_weight.shape[1]), bf16),
            pltpu.VMEM((rows // block, expert_count * block, expert_width), bf16),
            pltpu.VMEM((rows // block, tasks * block, expert_count * block), bf16),
            pltpu.VMEM((tasks, rows, expert_width), bf16),
            pltpu.VMEM((tasks, rows), jnp.float32),
            pltpu.SemaphoreType.DMA((5 + 3 * narrow_count,)),
        ],
        compiler_params=pltpu.CompilerParams(vmem_limit_bytes=VMEM_LIMIT),
        cost_estimate=pl.CostEstimate(flops=flops, bytes_accessed=6 * 1024 * 1024, transcendentals=0),
        name="rank_slot",
    )(
        where,
        kept,
        arrived,
        pre_inner,
        pre_bias.reshape(1, -1),
        pre_outer,
        query_weight,
        norm_gain.reshape(1, -1),
        gate_weight,
        gate_bias.reshape(1, -1),
        *history,
        *history_bias,
        *experts,
        *towers,
        *tower_outer,
    )


def unpack_body(narrow_count, half, slot_ref, lane_ref, returned_ref, out_ref):
    requests, shard_len = lane_ref.shape
    _, tasks, lanes = returned_ref.shape
    row_at = lax.broadcasted_iota(jnp.int32, (lanes, shard_len), 0)
    for s in range(requests):
        r = slot_ref[s]
        values = returned_ref[s * narrow_count]
        for i in range(1, narrow_count):
            values = values + returned_ref[s * narrow_count + i]
        pick = jnp.where(lane_ref[pl.ds(r, 1), :] == row_at, 1.0, 0.0).astype(jnp.bfloat16)
        result = sum_parts(dot_f32(three_parts(values), pick), tasks)
        for t in range(tasks):
            out_ref[t, pl.ds(r, 1), :] = result[t : t + 1, :]


def unpack_rows(slot_request, lanes, returned, narrow_count, half):
    requests, shard_len = lanes.shape
    tasks = returned.shape[1]
    return pl.pallas_call(
        functools.partial(unpack_body, narrow_count, half),
        out_shape=jax.ShapeDtypeStruct((tasks, requests, shard_len), jnp.float32),
        in_specs=[SMEM, VMEM, VMEM],
        out_specs=VMEM,
        compiler_params=pltpu.CompilerParams(vmem_limit_bytes=VMEM_LIMIT),
        name="unpack_rows",
    )(slot_request, lanes, returned)


def lanes_of(kept_index, device_rank, shard_len, narrow_count, half):
    base = device_rank * shard_len
    ids = base + jnp.arange(shard_len, dtype=jnp.int32)
    flags = jnp.any(kept_index[:, :, None] == ids[None, None, :], axis=1)
    places = jnp.cumsum(flags.astype(jnp.int32), axis=1) - flags.astype(jnp.int32)
    before = jnp.sum((kept_index < base).astype(jnp.int32), axis=1, keepdims=True)
    return jnp.where(flags, (before + places) % narrow_count * half + places // narrow_count, -1)


def from_others(values, narrow_count):
    pieces = [values]
    for shift in range(1, narrow_count):
        steps = [((i + shift) % narrow_count, i) for i in range(narrow_count)]
        pieces.append(lax.ppermute(values, "narrow", steps))
    return pieces


def on_device(
    candidates,
    pre_inner,
    pre_bias,
    pre_outer,
    user_vector,
    kept_index,
    slot_request,
    history_kv,
    history_bias,
    history_length,
    query_weight,
    norm_gain,
    expert_weight,
    gate_weight,
    gate_bias,
    tower_inner,
    tower_outer,
):
    wide_count = lax.axis_size("wide")
    narrow_count = lax.axis_size("narrow")
    shards = wide_count * narrow_count
    wide_rank = lax.axis_index("wide")
    narrow_rank = lax.axis_index("narrow")
    device_rank = wide_rank * narrow_count + narrow_rank
    requests, shard_len, features = candidates.shape
    kept_count = kept_index.shape[1]
    capacity = 2 * kept_count // shards
    half = -(-capacity // narrow_count)
    group_size = history_kv.shape[0]
    tasks = narrow_count * tower_inner.shape[0]
    width = pre_outer.shape[1]
    both = ("wide", "narrow")
    blocked = (
        shard_len % 128 == 0
        and requests % 8 == 0
        and half % 16 == 0
        and narrow_count * half <= 128
        and 128 % half == 0
        and group_size == 1
    )

    if blocked:
        packed, lanes = pack_rows(
            device_rank.reshape(1), slot_request, kept_index, candidates, narrow_count, half
        )
    else:
        lanes = lanes_of(kept_index, device_rank, shard_len, narrow_count, half)
        picks = lanes[:, None, :] == jnp.arange(narrow_count * half, dtype=jnp.int32)[None, :, None]
        packed = jnp.einsum(
            "rcs,rsd->rcd", picks.astype(jnp.bfloat16), candidates, preferred_element_type=jnp.float32
        ).astype(jnp.bfloat16)[slot_request]
    packed = packed.reshape(wide_count, group_size, narrow_count, half, features)
    packed = jnp.swapaxes(packed, 1, 2).reshape(shards, group_size * half, features)
    arrived = lax.all_to_all(packed, both, split_axis=0, concat_axis=0, tiled=True)
    arrived = jnp.swapaxes(arrived.reshape(shards, group_size, half, features), 0, 1)
    arrived = arrived.reshape(group_size, shards * half, features)

    history = from_others(history_kv, narrow_count)
    biases = from_others(history_bias, narrow_count)
    experts = from_others(expert_weight, narrow_count)
    towers = from_others(tower_inner, narrow_count)
    tower_outs = from_others(tower_outer, narrow_count)

    if blocked:
        prerank_score = prerank(candidates, pre_inner, pre_bias, pre_outer, user_vector, lanes)
    else:
        hidden = jax.nn.relu(
            dot_f32(candidates.reshape(requests * shard_len, features), pre_inner) + pre_bias
        ).astype(jnp.bfloat16)
        embedded = dot_f32(hidden, pre_outer).astype(jnp.bfloat16)
        prerank_score = jnp.einsum(
            "rsd,rd->rs",
            embedded.reshape(requests, shard_len, width),
            user_vector,
            preferred_element_type=jnp.float32,
        )

    results = []
    for g in range(group_size):
        request = slot_request[wide_rank * group_size + g]
        results.append(
            rank_slot(
                jnp.stack([narrow_rank, history_length[g]]),
                lax.dynamic_slice_in_dim(kept_index, request, 1, 0),
                arrived[g],
                pre_inner,
                pre_bias,
                pre_outer,
                query_weight,
                norm_gain,
                gate_weight,
                gate_bias,
                [piece[g] for piece in history],
                [piece[g] for piece in biases],
                experts,
                towers,
                tower_outs,
                shards,
                shard_len,
                blocked,
            )
        )

    if blocked:
        returned = lax.all_to_all(results[0], both, split_axis=0, concat_axis=0, tiled=True)
        return (prerank_score, unpack_rows(slot_request, lanes, returned, narrow_count, half))
    sending = jnp.stack(results).reshape(group_size, tasks, shards, half)
    sending = jnp.transpose(sending, (2, 0, 1, 3)).reshape(shards, -1)
    returned = lax.all_to_all(sending, both, split_axis=0, concat_axis=0, tiled=True)
    returned = returned.reshape(wide_count, narrow_count, group_size, tasks, half)
    returned = jnp.transpose(returned, (0, 2, 3, 1, 4)).reshape(requests, tasks, narrow_count * half)
    request_ids = jnp.arange(requests, dtype=jnp.int32)
    slot_of = jnp.sum(
        jnp.where(slot_request[None, :] == request_ids[:, None], request_ids[None, :], 0), axis=1
    )
    rank_score = jnp.einsum(
        "rcs,rtc->trs",
        picks.astype(jnp.float32),
        returned[slot_of],
        precision=lax.Precision.HIGHEST,
    )
    return (prerank_score, rank_score)


def solution(mesh):
    return jax.shard_map(
        on_device,
        mesh=mesh,
        in_specs=(
            P("groups", ("wide", "narrow"), None),
            P(),
            P(),
            P(),
            P("groups", None),
            P("groups", None),
            P("groups"),
            P(("groups", "wide"), None, None, "narrow"),
            P(("groups", "wide"), "narrow", None),
            P(("groups", "wide")),
            P(),
            P(),
            P("narrow", None, None),
            P(),
            P(),
            P("narrow", None, None),
            P("narrow", None),
        ),
        out_specs=(P("groups", ("wide", "narrow")), P(None, "groups", ("wide", "narrow"))),
        check_vma=False,
    )
```

time: 110 us -> 55.8 us (0.51)
  matrix products: 18.6 us -> 0 us
  Pallas kernels: 0 us -> 17.3 us
  other arithmetic: 15.1 us -> 0.59 us
  between operations: 17 us -> 3.37 us
  blocking collectives: 12.4 us -> 0 us
  waiting for transfers between devices: 14.7 us -> 7.49 us
  local copies, waits for them, and re-layouts: 17.9 us -> 13.3 us
    pallas_call x0 -> x4, Pallas kernels: none -> 17.3 us  [the longest x1 10.2 us: rank_slot(): pl.pallas_call(functools.partial(rank_body, narrow_count, shards, shard_l...]
    dot_general x9 -> x0, matrix products: 14.7 us -> none  [the longest x1 3.14 us: on_device(): jnp.einsum('kte,keh->kth', gate_probs, lax.all_gather(expert_out, 'narrow...]
    gather x10 -> x0, local copies, waits for them, and re-layouts: 10.2 us -> none  [the longest x2 3.02 us: on_device(): jnp.take_along_axis(task_logit, source_rows[:, :, None], axis=1)]
    unnamed x29 -> x43, local copies, waits for them, and re-layouts: 3.23 us -> 11.4 us
    all_gather x1 -> x0, waiting for transfers between devices: 8.12 us -> none  [on_device(): lax.all_gather(expert_out, 'narrow', axis=1, tiled=True)]
    all_to_all x2 -> x0, blocking collectives: 7.88 us -> none  [the longest x1 4.15 us: on_device(): lax.all_to_all(lax.all_to_all(sending, 'wide', split_axis=0, concat_axis=...]
    and x2 -> x0, other arithmetic: 5.69 us -> none  [the longest x1 5.6 us: on_device(): jnp.take_along_axis(arrived.reshape(group_size, shards * capacity, -1), f...]
    all_gather x2 -> x0, blocking collectives: 4.54 us -> none  [the longest x1 2.36 us: on_device(): attend_full = lax.all_gather(attended, 'narrow', axis=2, tiled=True)]
  transfers between devices with their start and end apart: 3 -> 7, of which waited for: 2 -> 2; matrix products, arithmetic and copies ran while one was open for 16% -> 6% of each run, Pallas kernels for 0% -> 11%
where the time goes in v1:
time: 55.8 us; the launch traced here: 54.9 us
  Pallas kernels  17.3 us (31%)
  local copies, waits for them, and re-layouts  13.3 us (24%)
  starting transfers between devices  12.9 us (23%)
  waiting for transfers between devices  7.49 us (13%)
  between operations  3.37 us (6%)
  other arithmetic  0.59 us (1%)
    unnamed x43, local copies, waits for them, and re-layouts  11.4 us
    pallas_call x1, Pallas kernels, rank_slot(): pl.pallas_call(functools.partial(rank_body, narrow_count, shards, shard_l...  10.2 us
    all_to_all x1, waiting for transfers between devices, on_device(): lax.all_to_all(packed, both, split_axis=0, concat_axis=0, tiled=True)  7.33 us
    all_to_all x1, starting transfers between devices, on_device(): lax.all_to_all(packed, both, split_axis=0, concat_axis=0, tiled=True)  7.15 us
    all_to_all x1, starting transfers between devices, on_device(): lax.all_to_all(results[0], both, split_axis=0, concat_axis=0, tiled=True)  4.1 us
    pallas_call x1, Pallas kernels, pack_rows(): pl.pallas_call(functools.partial(pack_body, narrow_count, half), out_shap...  3.04 us
    pallas_call x1, Pallas kernels, prerank(): pl.pallas_call(functools.partial(prerank_body, shard_len), out_shape=jax....  2.75 us
    ppermute x5, starting transfers between devices, from_others(): pieces.append(lax.ppermute(values, 'narrow', steps))  1.6 us
  transfers between devices with their start and end apart: 7, of which 2 were waited for; matrix products, arithmetic and copies ran while one was open for 6% of the time, Pallas kernels for 11%

profile of v1, /device:TPU:0, one launch (start us, length us, event | category | flops | bytes accessed | tf_op | source)
XLA Modules:
  0.0 54.9 jit_solution(5595093888493102740)
XLA Ops:
  0.6 0.5 collective-permute-start.2
  1.3 0.5 copy-done.16
  1.8 1.2 %copy-done.1 = bf16[8,128,512]{2,1,0:T(8,128)(2,1)S(1)} copy-done((bf16[8,128,512]{2,1,0:T(8,128)(2,1)S(1)}, bf16[8,128,512]{2,1,0:T(8,128)(2,1)}, u32[]{:S(2)}) %copy-start.1) | copy-done | bytes 1048600
  3.0 3.0 %pack_rows.1 = (bf16[512,512]{1,0:T(8,128)(2,1)S(1)}, s32[8,128]{1,0:T(8,128)S(1)}) custom-call(s32[1]{0:T(128)} %bitcast.2.where_ref, s32[8]{0:T(128)S(1)} %copy-done.16, s32[8,512]{1,0:T(8,128)S(1)} %copy-done.11, bf16[8,128,512]{2,1,0:T(8,128)(2,1)S(1)} %copy-done.1), custom_call_target="tpu_custom_call" | custom-call | flops 67108864 | bytes 1048576 | tf_op jit(solution)/shard_map/pack_rows/pallas_call | solution.py:84
  6.1 0.8 %copy-done.9 = bf16[512,512]{1,0:T(8,128)(2,1)} copy-done((bf16[512,512]{1,0:T(8,128)(2,1)}, bf16[512,512]{1,0:T(8,128)(2,1)S(1)}, u32[]{:S(2)}) %copy-start.9) | copy-done | bytes 524312
  6.9 7.1 %all-to-all-start = ((bf16[16,32,512]{2,1,0:T(8,128)(2,1)}), bf16[16,32,512]{2,1,0:T(8,128)(2,1)S(1)}, u32[]{:S(2)}, u32[]{:S(2)}) async-start(bf16[16,32,512]{2,1,0:T(8,128)(2,1)} %bitcast.15), calls=%async_computation | async-start | bytes 1048576 | tf_op jit(solution)/shard_map/all_to_all | solution.py:512
  14.1 0.4 collective-permute-start
  15.2 0.6 %dynamic_slice.6 = s32[1]{0:T(128)} dynamic-slice(s32[8]{0:T(128)S(1)} %copy-done.16, s32[]{:T(128)S(6)} %select_n.6), dynamic_slice_sizes={1} | dynamic-slice | bytes 12 | tf_op jit(solution)/shard_map/dynamic_slice | solution.py:538
  18.3 0.6 %pad_add_fusion.where_ref = s32[2]{0:T(128)} fusion(s32[1]{0:T(128)S(6)} %copy.20, s32[1]{0:T(128)} %bitcast.3), kind=kLoop, calls=%fused_computation | loop fusion | flops 2 | bytes 16 | tf_op jit(solution)/shard_map/stack | solution.py:541
  18.9 1.0 %copy.19.gate_hbm = bf16[512,64]{1,0:T(8,128)(2,1)S(1)} copy(bf16[512,64]{0,1:T(8,128)(2,1)} %param.30) | data formatting | bytes 131072 | tf_op args[13]
  19.9 1.3 %reshape.24.gate_bias_ref = f32[1,64]{1,0:T(1,128)} reshape(f32[8,8]{1,0:T(8,128)} %param.31) | data formatting | bytes 512 | tf_op jit(solution)/shard_map/reshape | solution.py:404
  21.2 7.3 %all-to-all-done = bf16[16,32,512]{2,1,0:T(8,128)(2,1)S(1)} async-done(((bf16[16,32,512]{2,1,0:T(8,128)(2,1)}), bf16[16,32,512]{2,1,0:T(8,128)(2,1)S(1)}, u32[]{:S(2)}, u32[]{:S(2)}) %all-to-all-start) | async-done | bytes 524320 | tf_op jit(solution)/shard_map/all_to_all | solution.py:512
  28.6 0.6 %copy-done.14 = f32[512]{0:T(512)S(1)} copy-done((f32[512]{0:T(512)S(1)}, f32[512]{0:T(512)}, u32[]{:S(2)}) %copy-start.14) | copy-done | bytes 2072
  29.2 1.0 %copy-done.4 = bf16[1,2,512,256]{3,2,1,0:T(8,128)(2,1)S(1)} copy-done((bf16[1,2,512,256]{3,2,1,0:T(8,128)(2,1)S(1)}, bf16[1,2,512,256]{3,2,1,0:T(8,128)(2,1)}, u32[]{:S(2)}) %copy-start.4) | copy-done | bytes 524312
  30.3 1.0 %copy-done.5 = bf16[512,512]{1,0:T(8,128)(2,1)S(1)} copy-done((bf16[512,512]{1,0:T(8,128)(2,1)S(1)}, bf16[512,512]{1,0:T(8,128)(2,1)}, u32[]{:S(2)}) %copy-start.5) | copy-done | bytes 524312
  31.3 1.0 %copy-done.7 = bf16[512,512]{1,0:T(8,128)(2,1)S(1)} copy-done((bf16[512,512]{1,0:T(8,128)(2,1)S(1)}, bf16[512,512]{1,0:T(8,128)(2,1)}, u32[]{:S(2)}) %copy-start.7) | copy-done | bytes 524312
  32.4 10.2 %rank_slot.1 = f32[16,8,128]{2,1,0:T(8,128)} custom-call(s32[2]{0:T(128)S(1)} %copy-done.19, s32[1,512]{1,0:T(1,128)S(1)} %constant_dynamic-slice_fusion.kept_ref, bf16[512,512]{1,0:T(8,128)(2,1)S(1)} %bitcast.12, bf16[512,512]{1,0:T(8,128)(2,1)S(1)} %copy-done.5, f32[1,512]{1,0:T(1,128)S(1)} %bitcast.18, bf16[512,512]{1,0:T(8,128)(2,1)S(1)} %copy-done.7, ...), custom_call_target="tpu_custom_call" | custom-call | flops 1610612736 | bytes 6291456 | tf_op jit(solution)/shard_map/rank_slot/pallas_call | solution.py:363
  42.5 4.1 %all-to-all-start.1 = ((f32[16,8,128]{2,1,0:T(8,128)}), f32[16,8,128]{2,1,0:T(8,128)S(1)}, u32[]{:S(2)}, u32[]{:S(2)}) async-start(f32[16,8,128]{2,1,0:T(8,128)} %rank_slot.1), calls=%async_computation.1 | async-start | bytes 131072 | tf_op jit(solution)/shard_map/all_to_all | solution.py:563
  46.7 0.7 %copy-done.15 = f32[512]{0:T(512)S(1)} copy-done((f32[512]{0:T(512)S(1)}, f32[512]{0:T(512)}, u32[]{:S(2)}) %copy-start.15) | copy-done | bytes 2072
  47.3 1.2 %copy-done.2 = bf16[8,128,512]{2,1,0:T(8,128)(2,1)S(1)} copy-done((bf16[8,128,512]{2,1,0:T(8,128)(2,1)S(1)}, bf16[8,128,512]{2,1,0:T(8,128)(2,1)}, u32[]{:S(2)}) %copy-start.2) | copy-done | bytes 1048600
  48.6 1.0 %copy-done.6 = bf16[512,512]{1,0:T(8,128)(2,1)S(1)} copy-done((bf16[512,512]{1,0:T(8,128)(2,1)S(1)}, bf16[512,512]{1,0:T(8,128)(2,1)}, u32[]{:S(2)}) %copy-start.6) | copy-done | bytes 524312
  49.6 1.0 %copy-done.8 = bf16[512,512]{1,0:T(8,128)(2,1)S(1)} copy-done((bf16[512,512]{1,0:T(8,128)(2,1)S(1)}, bf16[512,512]{1,0:T(8,128)(2,1)}, u32[]{:S(2)}) %copy-start.8) | copy-done | bytes 524312
  50.7 2.8 %prerank.1 = f32[8,128]{1,0:T(8,128)} custom-call(bf16[1024,512]{1,0:T(8,128)(2,1)S(1)} %bitcast.13, bf16[512,512]{1,0:T(8,128)(2,1)S(1)} %copy-done.6, f32[1,512]{1,0:T(1,128)S(1)} %bitcast.19, bf16[512,512]{1,0:T(8,128)(2,1)S(1)} %copy-done.8, bf16[8,512]{1,0:T(8,128)(2,1)S(1)} %copy-done.20, s32[8,128]{1,0:T(8,128)S(1)} %get-tuple-element.4.lane_ref), custom_call_target="tpu_custom_call" | custom-call | flops 1073741824 | bytes 2097152 | tf_op jit(solution)/shard_map/prerank/pallas_call | solution.py:119
  53.6 1.4 %unpack_rows.1 = f32[8,8,128]{2,1,0:T(8,128)} custom-call(s32[8]{0:T(128)S(1)} %copy-done.17, s32[8,128]{1,0:T(8,128)S(1)} %get-tuple-element.4.lane_ref, f32[16,8,128]{2,1,0:T(8,128)S(1)} %all-to-all-done.1.returned_ref), custom_call_target="tpu_custom_call" | custom-call | tf_op jit(solution)/shard_map/unpack_rows/pallas_call | solution.py:431
  (41 shorter events, 1.1 us)
Async XLA Ops:
  0.6 0.7 %copy-start.11 = (s32[8,512]{1,0:T(8,128)S(1)}, s32[8,512]{1,0:T(8,128)}, u32[]{:S(2)}) copy-start(s32[8,512]{1,0:T(8,128)} %kept_ref.1) | copy-start | bytes 49156
  0.6 27.9 %collective-permute-start.2 = (bf16[4,512,256]{2,1,0:T(8,128)(2,1)}, bf16[4,512,256]{2,1,0:T(8,128)(2,1)S(1)}, u32[]{:S(2)}, u32[]{:S(2)}) collective-permute-start(bf16[4,512,256]{2,1,0:T(8,128)(2,1)} %rest_4_.1), channel_id=1, source_target_pairs={{1,0},{0,1},{3,2},{2,3},{5,4},{4,5},{7,6},{6,7},{9,8},{8,9},{11,10... | collective-permute-start | bytes 3145736 | tf_op jit(solution)/shard_map/ppermute | solution.py:454
  1.8 1.2 %copy-start.1 = (bf16[8,128,512]{2,1,0:T(8,128)(2,1)S(1)}, bf16[8,128,512]{2,1,0:T(8,128)(2,1)}, u32[]{:S(2)}) copy-start(bf16[8,128,512]{2,1,0:T(8,128)(2,1)} %cand_hbm.1) | copy-start | bytes 3145732
  3.0 25.5 %copy-start = (bf16[4,512,256]{2,1,0:T(8,128)(2,1)S(1)}, bf16[4,512,256]{2,1,0:T(8,128)(2,1)}, u32[]{:S(2)}) copy-start(bf16[4,512,256]{2,1,0:T(8,128)(2,1)} %rest_4_.1) | copy-start | bytes 3145732
  6.1 0.8 %copy-start.9 = (bf16[512,512]{1,0:T(8,128)(2,1)}, bf16[512,512]{1,0:T(8,128)(2,1)S(1)}, u32[]{:S(2)}) copy-start(bf16[512,512]{1,0:T(8,128)(2,1)S(1)} %get-tuple-element.5) | copy-start | bytes 1572868
  6.9 7.6 %copy-start.10 = (bf16[4,256,128]{2,1,0:T(8,128)(2,1)S(1)}, bf16[4,256,128]{2,1,0:T(8,128)(2,1)}, u32[]{:S(2)}) copy-start(bf16[4,256,128]{2,1,0:T(8,128)(2,1)} %rest_6_.1) | copy-start | bytes 786436
  6.9 7.7 %copy-start.12 = (f32[1,4,512]{2,1,0:T(4,128)S(1)}, f32[1,4,512]{2,1,0:T(4,128)}, u32[]{:S(2)}) copy-start(f32[1,4,512]{2,1,0:T(4,128)} %param.25) | copy-start | bytes 24580
  6.9 21.7 %copy-start.3 = (bf16[512,512]{1,0:T(8,128)(2,1)S(1)}, bf16[512,512]{1,0:T(8,128)(2,1)}, u32[]{:S(2)}) copy-start(bf16[512,512]{1,0:T(8,128)(2,1)} %query_hbm.1) | copy-start | bytes 1572868
  6.9 21.6 %all-to-all-start = ((bf16[16,32,512]{2,1,0:T(8,128)(2,1)}), bf16[16,32,512]{2,1,0:T(8,128)(2,1)S(1)}, u32[]{:S(2)}, u32[]{:S(2)}) async-start(bf16[16,32,512]{2,1,0:T(8,128)(2,1)} %bitcast.15), calls=%async_computation | async-start | bytes 1048576 | tf_op jit(solution)/shard_map/all_to_all | solution.py:512
  14.1 7.1 %collective-permute-start = (bf16[1,2,512,256]{3,2,1,0:T(8,128)(2,1)}, bf16[1,2,512,256]{3,2,1,0:T(8,128)(2,1)}, u32[]{:S(2)}, u32[]{:S(2)}) collective-permute-start(bf16[1,2,512,256]{3,2,1,0:T(8,128)(2,1)} %param.24), channel_id=1, source_target_pairs={{1,0},{0,1},{3,2},{2,3},{5,4},{4,5},{7,6},{6,7},{9,8},{8,9},{11,10... | collective-permute-start | bytes 1572872 | tf_op jit(solution)/shard_map/ppermute | solution.py:454
  14.5 6.7 %collective-permute-start.3 = (bf16[4,256,128]{2,1,0:T(8,128)(2,1)S(1)}, bf16[4,256,128]{2,1,0:T(8,128)(2,1)}, u32[]{:S(2)}, u32[]{:S(2)}) collective-permute-start(bf16[4,256,128]{2,1,0:T(8,128)(2,1)S(1)} %copy-done.10), channel_id=1, source_target_pairs={{1,0},{0,1},{3,2},{2,3},{5,4},{4,5},{7,6},{6,7},{9,8},{8,9},{11,10... | collective-permute-start | bytes 786440 | tf_op jit(solution)/shard_map/ppermute | solution.py:454
  14.6 6.5 %collective-permute-start.1 = (f32[1,4,512]{2,1,0:T(4,128)S(1)}, f32[1,4,512]{2,1,0:T(4,128)}, u32[]{:S(2)}, u32[]{:S(2)}) collective-permute-start(f32[1,4,512]{2,1,0:T(4,128)S(1)} %copy-done.12), channel_id=1, source_target_pairs={{1,0},{0,1},{3,2},{2,3},{5,4},{4,5},{7,6},{6,7},{9,8},{8,9},{11,10... | collective-permute-start | bytes 24584 | tf_op jit(solution)/shard_map/ppermute | solution.py:454
  15.0 6.2 %collective-permute-start.4 = (bf16[4,128]{1,0:T(4,128)(2,1)}, bf16[4,128]{1,0:T(4,128)(2,1)}, u32[]{:S(2)}, u32[]{:S(2)}) collective-permute-start(bf16[4,128]{1,0:T(4,128)(2,1)} %rest_8_.1), channel_id=1, source_target_pairs={{1,0},{0,1},{3,2},{2,3},{5,4},{4,5},{7,6},{6,7},{9,8},{8,9},{11,10... | collective-permute-start | bytes 3080 | tf_op jit(solution)/shard_map/ppermute | solution.py:454
  28.5 0.7 %copy-start.13 = (f32[512]{0:T(512)S(1)}, f32[512]{0:T(512)}, u32[]{:S(2)}) copy-start(f32[512]{0:T(512)} %param.28) | copy-start | bytes 6148
  28.5 0.7 %copy-start.18 = (f32[1,64]{1,0:T(1,128)S(1)}, f32[1,64]{1,0:T(1,128)}, u32[]{:S(2)}) copy-start(f32[1,64]{1,0:T(1,128)} %reshape.24.gate_bias_ref) | copy-start | bytes 772
  29.2 1.0 %copy-start.4 = (bf16[1,2,512,256]{3,2,1,0:T(8,128)(2,1)S(1)}, bf16[1,2,512,256]{3,2,1,0:T(8,128)(2,1)}, u32[]{:S(2)}) copy-start(bf16[1,2,512,256]{3,2,1,0:T(8,128)(2,1)} %param.24) | copy-start | bytes 1572868
  30.3 1.0 %copy-start.5 = (bf16[512,512]{1,0:T(8,128)(2,1)S(1)}, bf16[512,512]{1,0:T(8,128)(2,1)}, u32[]{:S(2)}) copy-start(bf16[512,512]{1,0:T(8,128)(2,1)} %inner_hbm.1) | copy-start | bytes 1572868
  31.3 1.0 %copy-start.7 = (bf16[512,512]{1,0:T(8,128)(2,1)S(1)}, bf16[512,512]{1,0:T(8,128)(2,1)}, u32[]{:S(2)}) copy-start(bf16[512,512]{1,0:T(8,128)(2,1)} %outer_hbm.1) | copy-start | bytes 1572868
  42.5 4.1 %copy-start.20 = (bf16[8,512]{1,0:T(8,128)(2,1)S(1)}, bf16[8,512]{1,0:T(8,128)(2,1)}, u32[]{:S(2)}) copy-start(bf16[8,512]{1,0:T(8,128)(2,1)} %user_ref.1) | copy-start | bytes 24580
  42.5 11.0 %all-to-all-start.1 = ((f32[16,8,128]{2,1,0:T(8,128)}), f32[16,8,128]{2,1,0:T(8,128)S(1)}, u32[]{:S(2)}, u32[]{:S(2)}) async-start(f32[16,8,128]{2,1,0:T(8,128)} %rank_slot.1), calls=%async_computation.1 | async-start | bytes 131072 | tf_op jit(solution)/shard_map/all_to_all | solution.py:563
  47.3 1.2 %copy-start.2 = (bf16[8,128,512]{2,1,0:T(8,128)(2,1)S(1)}, bf16[8,128,512]{2,1,0:T(8,128)(2,1)}, u32[]{:S(2)}) copy-start(bf16[8,128,512]{2,1,0:T(8,128)(2,1)} %cand_hbm.1) | copy-start | bytes 3145732
  48.6 1.0 %copy-start.6 = (bf16[512,512]{1,0:T(8,128)(2,1)S(1)}, bf16[512,512]{1,0:T(8,128)(2,1)}, u32[]{:S(2)}) copy-start(bf16[512,512]{1,0:T(8,128)(2,1)} %inner_hbm.1) | copy-start | bytes 1572868
  49.6 1.0 %copy-start.8 = (bf16[512,512]{1,0:T(8,128)(2,1)S(1)}, bf16[512,512]{1,0:T(8,128)(2,1)}, u32[]{:S(2)}) copy-start(bf16[512,512]{1,0:T(8,128)(2,1)} %outer_hbm.1) | copy-start | bytes 1572868
  50.6 2.9 %copy-start.17 = (s32[8]{0:T(128)S(1)}, s32[8]{0:T(128)}, u32[]{:S(2)}) copy-start(s32[8]{0:T(128)} %slot_ref.3) | copy-start | bytes 100
  (4 other events, 2.7 us)

commit v2 on v1

v2 whole, which is shorter than its diff:
```python
import functools

import jax
import jax.numpy as jnp
from jax import lax
from jax.experimental import pallas as pl
from jax.experimental.pallas import tpu as pltpu
from jax.sharding import PartitionSpec as P

NT = (((1,), (1,)), ((), ()))
VMEM = pl.BlockSpec(memory_space=pltpu.VMEM)
SMEM = pl.BlockSpec(memory_space=pltpu.SMEM)
ANY = pl.BlockSpec(memory_space=pl.ANY)
VMEM_LIMIT = 16 * 1024 * 1024
LANES = 128
BRIEF = pl.CostEstimate(flops=1, bytes_accessed=1, transcendentals=0)


def in_hbm(values):
    return pltpu.with_memory_space_constraint(values, pltpu.HBM)


def in_vmem(values):
    return pltpu.with_memory_space_constraint(values, pltpu.VMEM)


def dot_f32(a, b):
    return jnp.dot(a, b, preferred_element_type=jnp.float32)


def dot_nt(a, b):
    return lax.dot_general(a, b, NT, preferred_element_type=jnp.float32)


def split_by(values, divisor):
    if divisor & (divisor - 1) == 0:
        shift = divisor.bit_length() - 1
        return lax.shift_right_logical(values, shift), values & (divisor - 1)
    quotient = lax.div(values, divisor)
    return quotient, values - quotient * divisor


def three_parts(values):
    high = values.astype(jnp.bfloat16)
    rest = values - high.astype(jnp.float32)
    middle = rest.astype(jnp.bfloat16)
    low = (rest - middle.astype(jnp.float32)).astype(jnp.bfloat16)
    return jnp.concatenate([high, middle, low], axis=0)


def sum_parts(stacked, rows):
    return stacked[:rows] + stacked[rows : 2 * rows] + stacked[2 * rows :]


def pack_body(
    narrow_count, half, slot_ref, kept_hbm, cand_hbm, out_hbm, lane_ref, back_ref, kept_ref, cand_ref, out_ref, sems
):
    requests, shard_len, _ = cand_ref.shape
    kept_count = kept_ref.shape[1]
    kept_copy = pltpu.make_async_copy(kept_hbm, kept_ref, sems.at[0])
    cand_copy = pltpu.make_async_copy(cand_hbm, cand_ref, sems.at[1])
    kept_copy.start()
    cand_copy.start()
    device = lax.axis_index("wide") * narrow_count + lax.axis_index("narrow")
    base = device * shard_len
    ids = base + lax.broadcasted_iota(jnp.int32, (shard_len, kept_count), 0)
    request_rows = lax.broadcasted_iota(jnp.int32, (requests, kept_count), 0)
    kept_copy.wait()
    flags = jnp.zeros((requests, shard_len), jnp.float32)
    for r in range(requests):
        hits = jnp.where(kept_ref[r : r + 1, :] == ids, 1.0, 0.0).astype(jnp.bfloat16)
        row = jnp.where(request_rows == r, 1.0, 0.0).astype(jnp.bfloat16)
        flags = flags + dot_nt(row, hits)
    earlier = lax.broadcasted_iota(jnp.int32, (shard_len, shard_len), 0) < lax.broadcasted_iota(
        jnp.int32, (shard_len, shard_len), 1
    )
    places = dot_f32(
        flags.astype(jnp.bfloat16), jnp.where(earlier, 1.0, 0.0).astype(jnp.bfloat16)
    ).astype(jnp.int32)
    before = jnp.sum((kept_ref[...] < base).astype(jnp.int32), axis=1, keepdims=True)
    _, owner = split_by(before + places, narrow_count)
    within, _ = split_by(places, narrow_count)
    kept_here = flags > 0.5
    lane_ref[...] = jnp.where(kept_here, owner * half + within, -1)
    offset = lax.rem(device * half, LANES)
    back_ref[...] = jnp.where(kept_here, owner * LANES + offset + within, -1)
    rows = narrow_count * half
    row_at = lax.broadcasted_iota(jnp.int32, (rows, shard_len), 0)
    cand_copy.wait()
    sends = []
    for s in range(requests):
        r = slot_ref[s]
        pick = jnp.where(lane_ref[pl.ds(r, 1), :] == row_at, 1.0, 0.0).astype(jnp.bfloat16)
        out_ref[s * rows : (s + 1) * rows, :] = dot_f32(pick, cand_ref[r]).astype(jnp.bfloat16)
        part = pl.ds(s * rows, rows)
        sends.append(pltpu.make_async_copy(out_ref.at[part], out_hbm.at[part], sems.at[2 + s]))
        sends[s].start()
    for send in sends:
        send.wait()


def pack_rows(slot_request, kept_index, candidates, narrow_count, half):
    requests, shard_len, features = candidates.shape
    rows = requests * narrow_count * half
    return pl.pallas_call(
        functools.partial(pack_body, narrow_count, half),
        out_shape=(
            pltpu.HBM((rows, features), jnp.bfloat16),
            jax.ShapeDtypeStruct((requests, shard_len), jnp.int32),
            jax.ShapeDtypeStruct((requests, shard_len), jnp.int32),
        ),
        in_specs=[SMEM, ANY, ANY],
        out_specs=(ANY, VMEM, VMEM),
        scratch_shapes=[
            pltpu.VMEM(kept_index.shape, jnp.int32),
            pltpu.VMEM((requests, shard_len, features), jnp.bfloat16),
            pltpu.VMEM((rows, features), jnp.bfloat16),
            pltpu.SemaphoreType.DMA((2 + requests,)),
        ],
        compiler_params=pltpu.CompilerParams(vmem_limit_bytes=VMEM_LIMIT),
        cost_estimate=pl.CostEstimate(
            flops=2 * rows * shard_len * features, bytes_accessed=4 * rows * features, transcendentals=0
        ),
        name="pack_rows",
    )(in_hbm(slot_request), in_hbm(kept_index), in_hbm(candidates))


def prerank_body(shard_len, cand_ref, inner_ref, bias_ref, outer_ref, user_ref, lane_ref, out_ref):
    requests = user_ref.shape[0]
    step = 2 if requests % 2 == 0 else 1
    for r in range(0, requests, step):
        rows = cand_ref[r * shard_len : (r + step) * shard_len, :]
        hidden = jnp.maximum(dot_f32(rows, inner_ref[...]) + bias_ref[...], 0.0).astype(jnp.bfloat16)
        embedded = dot_f32(hidden, outer_ref[...]).astype(jnp.bfloat16)
        scores = dot_nt(user_ref[...], embedded)
        for i in range(step):
            out_ref[r + i : r + i + 1, :] = scores[r + i : r + i + 1, i * shard_len : (i + 1) * shard_len]


def prerank(candidates, pre_inner, pre_bias, pre_outer, user_vector, lanes):
    requests, shard_len, features = candidates.shape
    rows = requests * shard_len
    return pl.pallas_call(
        functools.partial(prerank_body, shard_len),
        out_shape=jax.ShapeDtypeStruct((requests, shard_len), jnp.float32),
        in_specs=[VMEM] * 6,
        out_specs=VMEM,
        compiler_params=pltpu.CompilerParams(vmem_limit_bytes=VMEM_LIMIT),
        cost_estimate=BRIEF,
        name="prerank",
    )(
        candidates.reshape(rows, features),
        pre_inner,
        pre_bias.reshape(1, -1),
        pre_outer,
        user_vector,
        lanes,
    )


def prepare_body(narrow_count, weight_count, shards, shard_len, slot_at, slot_ref, length_ref, kept_ref, *rest):
    history_refs = rest[:narrow_count]
    bias_refs = rest[narrow_count : 2 * narrow_count]
    tower_outer_refs = rest[2 * narrow_count : 3 * narrow_count]
    pre_bias_ref, gain_ref, gate_bias_ref = rest[3 * narrow_count : 3 * narrow_count + 3]
    rest = rest[3 * narrow_count + 3 :]
    weight_refs = rest[:weight_count]
    placing_ref, keys_hbm, values_hbm, vectors_ref, gate_offsets_ref, tower_columns_ref = rest[weight_count:][:6]
    loaded_refs = rest[weight_count + 6 : -4]
    keys_ref, values_ref, head_sems, sems = rest[-4:]
    copies = [
        pltpu.make_async_copy(source, loaded, sems.at[i])
        for i, (source, loaded) in enumerate(zip(weight_refs, loaded_refs))
    ]
    for copy in copies:
        copy.start()
    group_size, _, span, head_columns = history_refs[0].shape
    heads_here = bias_refs[0].shape[1]
    rows, rows_in = placing_ref.shape
    half = rows_in // shards
    me = lax.axis_index("narrow")
    request = slot_ref[lax.axis_index("wide") * group_size + slot_at]

    vectors_ref[0:1, :] = pre_bias_ref[...]
    vectors_ref[1:2, :] = gain_ref[...]
    tasks, experts = gate_bias_ref.shape
    gate_lane = lax.broadcasted_iota(jnp.int32, (tasks * experts, experts), 1)
    _, gate_row = split_by(lax.broadcasted_iota(jnp.int32, (tasks * experts, experts), 0), experts)
    offsets = jnp.broadcast_to(gate_bias_ref[...][:, None, :], (tasks, experts, experts))
    offsets = jnp.where(gate_row == gate_lane, offsets.reshape(tasks * experts, experts), 0.0)
    gate_offsets_ref[...] = jnp.broadcast_to(jnp.sum(offsets, axis=1, keepdims=True), gate_offsets_ref.shape)
    tasks_here, tower_width = tower_outer_refs[0].shape
    column = lax.broadcasted_iota(jnp.int32, (tower_width, LANES), 1)
    for i in range(narrow_count):
        outer = jnp.transpose(tower_outer_refs[i][...].astype(jnp.float32))
        for t in range(tasks_here):
            task = lax.rem(me + i, narrow_count) * tasks_here + t
            tower_columns_ref[i * tasks_here + t] = jnp.where(
                column == task, outer[:, t : t + 1], 0.0
            ).astype(jnp.bfloat16)

    kept_row = kept_ref[pl.ds(request, 1), :]
    edge = lax.broadcasted_iota(jnp.int32, (shards, kept_row.shape[1]), 0) * shard_len
    starts = jnp.sum((kept_row < edge).astype(jnp.int32), axis=1, keepdims=True)
    ends = jnp.sum((kept_row < edge + shard_len).astype(jnp.int32), axis=1, keepdims=True)
    first, _ = split_by(starts + (narrow_count - 1) - me, narrow_count)
    last, _ = split_by(ends + (narrow_count - 1) - me, narrow_count)
    lane_source, lane_within = split_by(lax.broadcasted_iota(jnp.int32, (shards, rows_in), 1), half)
    mine = lane_source == lax.broadcasted_iota(jnp.int32, (shards, rows_in), 0)
    target = jnp.where(mine & (first + lane_within < last), first + lane_within + 1, 0)
    target = jnp.sum(target, axis=0, keepdims=True) - 1
    placing_ref[...] = jnp.where(
        target == lax.broadcasted_iota(jnp.int32, (rows, rows_in), 0), 1.0, 0.0
    ).astype(jnp.bfloat16)

    head_size = head_columns // heads_here
    tile = 2 * head_size
    visible = lax.broadcasted_iota(jnp.int32, (1, span), 1) < length_ref[slot_at]
    lane = lax.broadcasted_iota(jnp.int32, (span, tile), 1)
    for i in range(narrow_count):
        for t in range(heads_here // 2):
            keys = history_refs[i][slot_at, 0, :, t * tile : (t + 1) * tile]
            keys = jnp.transpose(keys.astype(jnp.float32)).astype(jnp.bfloat16)
            values = history_refs[i][slot_at, 1, :, t * tile : (t + 1) * tile]
            for h in range(2):
                head = 2 * t + h
                at = i * heads_here + head
                bias = jnp.where(visible, bias_refs[i][slot_at, head : head + 1, :], -1e30)
                parts = three_parts(jnp.broadcast_to(bias, (8, span)).astype(jnp.float32))
                row = lax.broadcasted_iota(jnp.int32, (head_size, span), 0)
                high = jnp.broadcast_to(parts[0:1].astype(jnp.float32), (head_size, span))
                middle = jnp.broadcast_to(parts[8:9].astype(jnp.float32), (head_size, span))
                low = jnp.broadcast_to(parts[16:17].astype(jnp.float32), (head_size, span))
                extra = jnp.where(
                    row == 0, high, jnp.where(row == 1, middle, jnp.where(row == 2, low, 0.0))
                ).astype(jnp.bfloat16)
                own = h * head_size
                other = (1 - h) * head_size
                keys_ref[at, own : own + head_size, :] = keys[own : own + head_size, :]
                keys_ref[at, other : other + head_size, :] = extra
                mine = (lane >= own) & (lane < own + head_size)
                values_ref[at] = jnp.where(mine, values.astype(jnp.float32), 1.0).astype(jnp.bfloat16)
                copies.append(pltpu.make_async_copy(keys_ref.at[at], keys_hbm.at[at], head_sems.at[0, at]))
                copies[-1].start()
                copies.append(pltpu.make_async_copy(values_ref.at[at], values_hbm.at[at], head_sems.at[1, at]))
                copies[-1].start()
    for copy in copies:
        copy.wait()


def prepare(
    slot_request,
    lengths,
    kept_index,
    history,
    biases,
    tower_outer,
    pre_bias,
    norm_gain,
    gate_bias,
    weights,
    shards,
    shard_len,
    half,
    slot_at,
):
    narrow_count = len(history)
    _, _, span, head_columns = history[0].shape
    heads_here = biases[0].shape[1]
    heads = narrow_count * heads_here
    tile = 2 * head_columns // heads_here
    rows = kept_index.shape[1] // narrow_count
    tasks, experts = gate_bias.shape
    width = norm_gain.shape[0]
    bf16 = jnp.bfloat16
    return pl.pallas_call(
        functools.partial(prepare_body, narrow_count, len(weights), shards, shard_len, slot_at),
        out_shape=(
            pltpu.VMEM((rows, shards * half), bf16),
            pltpu.HBM((heads, tile, span), bf16),
            pltpu.HBM((heads, span, tile), bf16),
            pltpu.VMEM((8, width), jnp.float32),
            pltpu.VMEM((tasks * experts, LANES), jnp.float32),
            pltpu.VMEM((tasks, tower_outer[0].shape[1], LANES), bf16),
            *[pltpu.VMEM(weight.shape, weight.dtype) for weight in weights],
        ),
        in_specs=[SMEM, SMEM] + [VMEM] * (4 + 3 * narrow_count) + [ANY] * len(weights),
        out_specs=(VMEM, ANY, ANY) + (VMEM,) * (3 + len(weights)),
        scratch_shapes=[
            pltpu.VMEM((heads, tile, span), bf16),
            pltpu.VMEM((heads, span, tile), bf16),
            pltpu.SemaphoreType.DMA((2, heads)),
            pltpu.SemaphoreType.DMA((len(weights),)),
        ],
        compiler_params=pltpu.CompilerParams(vmem_limit_bytes=VMEM_LIMIT),
        cost_estimate=BRIEF,
        name="prepare",
    )(
        slot_request,
        lengths,
        kept_index,
        *history,
        *biases,
        *tower_outer,
        pre_bias.reshape(1, -1),
        norm_gain.reshape(1, -1),
        gate_bias,
        *[in_hbm(weight) for weight in weights],
    )


def rank_body(narrow_count, pieces, shards, spread, heads, *rest):
    arrived_hbm, keys_hbm, values_hbm = rest[:3]
    expert_hbm = rest[3 : 3 + pieces]
    rest = rest[3 + pieces :]
    placing_ref, vectors_ref, gate_offsets_ref, tower_columns_ref, inner_ref, outer_ref, query_ref, gate_ref = rest[:8]
    tower_refs = rest[8 : 8 + narrow_count]
    (
        out_ref,
        embed_ref,
        queries_ref,
        attended_ref,
        expert_out_ref,
        gates_ref,
        mixture_ref,
        arrived_ref,
        keys_ref,
        values_ref,
        expert_refs,
        sems,
    ) = rest[8 + narrow_count :]
    arrival = pltpu.make_async_copy(arrived_hbm, arrived_ref, sems.at[0])
    head_copies = [
        pltpu.make_async_copy(keys_hbm, keys_ref, sems.at[1]),
        pltpu.make_async_copy(values_hbm, values_ref, sems.at[2]),
    ]
    expert_copies = []
    for i in range(pieces):
        at = sum(piece.shape[0] for piece in expert_hbm[:i])
        here = expert_refs.at[pl.ds(at, expert_hbm[i].shape[0])]
        expert_copies.append(pltpu.make_async_copy(expert_hbm[i], here, sems.at[3 + i]))
    for copy in [arrival] + head_copies + expert_copies:
        copy.start()

    rows = embed_ref.shape[0]
    half = arrived_ref.shape[0] // shards
    width = queries_ref.shape[1]
    head_size = width // heads
    experts = expert_refs.shape[0]
    experts_here = experts // narrow_count
    tasks_here = tower_refs[0].shape[0]
    tasks = narrow_count * tasks_here
    block = rows // experts
    blocks = rows // block
    me = lax.axis_index("narrow")

    arrival.wait()
    packed = dot_f32(placing_ref[...], arrived_ref[...]).astype(jnp.bfloat16)
    hidden = jnp.maximum(dot_f32(packed, inner_ref[...]) + vectors_ref[0:1, :], 0.0).astype(jnp.bfloat16)
    embed = dot_f32(hidden, outer_ref[...]).astype(jnp.bfloat16)
    embed_ref[...] = embed
    queries = dot_f32(embed, query_ref[...]).astype(jnp.bfloat16)
    queries_ref[...] = queries

    tile = 2 * head_size
    heads_here = heads // narrow_count
    scale = float(head_size) ** (-0.5)
    lane = lax.broadcasted_iota(jnp.int32, (rows, tile), 1)
    left = lane < head_size
    for copy in head_copies:
        copy.wait()
    for i in range(narrow_count):
        at = lax.rem(me + i, narrow_count) * (width // narrow_count)
        for t in range(heads_here // 2):
            columns = pl.ds(pl.multiple_of(at + t * tile, tile), tile)
            scaled = queries_ref[:, columns].astype(jnp.float32) * scale
            results = []
            for h in range(2):
                head = i * heads_here + 2 * t + h
                other = (1 - h) * head_size
                ones = jnp.where((lane >= other) & (lane < other + 3), 1.0, 0.0)
                query = jnp.where(left if h == 0 else ~left, scaled, ones).astype(jnp.bfloat16)
                scores = dot_f32(query, keys_ref[head])
                powers = jnp.exp(scores - jnp.max(scores, axis=1, keepdims=True))
                results.append(dot_f32(powers.astype(jnp.bfloat16), values_ref[head]))
            sums = pltpu.roll(jnp.where(left, results[1], results[0]), head_size, 1)
            attended_ref[:, columns] = (jnp.where(left, results[0], results[1]) / sums).astype(jnp.bfloat16)

    mixed_in = embed_ref[...].astype(jnp.float32) + attended_ref[...].astype(jnp.float32)
    normed = (
        mixed_in
        * lax.rsqrt(jnp.mean(mixed_in * mixed_in, axis=1, keepdims=True) + 1e-06)
        * vectors_ref[1:2, :]
    ).astype(jnp.bfloat16)

    logits = dot_nt(gate_ref[...], normed) + gate_offsets_ref[:, 0:1]
    by_task = logits.reshape(tasks, experts, rows)
    gate_pow = jnp.exp(by_task - jnp.max(by_task, axis=1, keepdims=True))
    gate_probs = gate_pow / jnp.sum(gate_pow, axis=1, keepdims=True)
    gates = jnp.transpose(gate_probs.reshape(tasks * experts, rows)).astype(jnp.bfloat16)

    for copy in expert_copies:
        copy.wait()
    for e in range(experts):
        result = jnp.maximum(dot_f32(normed, expert_refs[e]), 0.0).astype(jnp.bfloat16)
        for b in range(blocks):
            expert_out_ref[b, e * block : (e + 1) * block, :] = result[b * block : (b + 1) * block, :]

    gate_at = lax.broadcasted_iota(jnp.int32, (tasks * experts, experts * block), 0)
    column = lax.broadcasted_iota(jnp.int32, (tasks * experts, experts * block), 1)
    column_expert, _ = split_by(column, block)
    _, column_expert = split_by(column_expert + me * experts_here, experts)
    _, row_in_block = split_by(lax.broadcasted_iota(jnp.int32, (rows, experts * block), 0), block)
    _, column_row = split_by(lax.broadcasted_iota(jnp.int32, (rows, experts * block), 1), block)
    diagonal = row_in_block == column_row
    for t in range(tasks):
        _, task = split_by(me * tasks_here + t, tasks)
        expand = jnp.where(gate_at == column_expert + task * experts, 1.0, 0.0).astype(jnp.bfloat16)
        wide = jnp.where(diagonal, dot_f32(gates, expand), 0.0).astype(jnp.bfloat16)
        for b in range(blocks):
            gates_ref[b, t * block : (t + 1) * block, :] = wide[b * block : (b + 1) * block, :]
    for b in range(blocks):
        mixture = dot_f32(gates_ref[b], expert_out_ref[b]).astype(jnp.bfloat16)
        for t in range(tasks):
            mixture_ref[t, b * block : (b + 1) * block, :] = mixture[t * block : (t + 1) * block, :]

    logits = jnp.zeros((rows, LANES), jnp.float32)
    for i in range(narrow_count):
        for t in range(tasks_here):
            at = i * tasks_here + t
            act = jnp.maximum(dot_f32(mixture_ref[at], tower_refs[i][t]), 0.0).astype(jnp.bfloat16)
            logits = logits + dot_f32(act, tower_columns_ref[at])
    by_task = jnp.transpose(logits)[:tasks]

    returned = sum_parts(dot_f32(three_parts(by_task), placing_ref[...]), tasks)
    if not spread:
        out_ref[...] = returned
        return
    for s in range(shards):
        at = s * half // LANES * LANES
        out_ref[s] = returned[:, at : at + LANES]


def rank_slot(
    arrived, placing, keys, values, vectors, gate_offsets, tower_columns, weights, experts, towers, shards, spread
):
    inner, outer, query, gate_rows = weights
    narrow_count = len(towers)
    rows, rows_in = placing.shape
    heads = keys.shape[0]
    width = outer.shape[1]
    tasks = tower_columns.shape[0]
    expert_count = gate_rows.shape[0] // tasks
    expert_width = experts[0].shape[2]
    block = rows // expert_count
    if spread:
        out_shape = jax.ShapeDtypeStruct((shards, tasks, LANES), jnp.float32)
    else:
        out_shape = jax.ShapeDtypeStruct((tasks, rows_in), jnp.float32)
    bf16 = jnp.bfloat16
    flops = 2 * rows * (rows_in * width + 3 * width * width + 2 * expert_count * width * expert_width)
    far = [arrived, keys, values, *experts]
    near = [placing, vectors, gate_offsets, tower_columns, *weights, *towers]
    return pl.pallas_call(
        functools.partial(rank_body, narrow_count, len(experts), shards, spread, heads),
        out_shape=out_shape,
        in_specs=[ANY] * len(far) + [VMEM] * len(near),
        out_specs=VMEM,
        scratch_shapes=[
            pltpu.VMEM((rows, width), bf16),
            pltpu.VMEM((rows, query.shape[1]), bf16),
            pltpu.VMEM((rows, query.shape[1]), bf16),
            pltpu.VMEM((rows // block, expert_count * block, expert_width), bf16),
            pltpu.VMEM((rows // block, tasks * block, expert_count * block), bf16),
            pltpu.VMEM((tasks, rows, expert_width), bf16),
            pltpu.VMEM(arrived.shape, bf16),
            pltpu.VMEM(keys.shape, bf16),
            pltpu.VMEM(values.shape, bf16),
            pltpu.VMEM((expert_count,) + experts[0].shape[1:], bf16),
            pltpu.SemaphoreType.DMA((3 + len(experts),)),
        ],
        compiler_params=pltpu.CompilerParams(vmem_limit_bytes=VMEM_LIMIT),
        cost_estimate=pl.CostEstimate(flops=flops, bytes_accessed=6 * 1024 * 1024, transcendentals=0),
        name="rank_slot",
    )(*[in_hbm(array) for array in far], *[in_vmem(array) for array in near])


def unpack_body(narrow_count, slot_ref, back_ref, returned_ref, out_ref):
    requests, shard_len = back_ref.shape
    _, tasks, lanes = returned_ref.shape
    row_at = lax.broadcasted_iota(jnp.int32, (narrow_count * lanes, shard_len), 0)
    for s in range(requests):
        r = slot_ref[s]
        pieces = [returned_ref[s * narrow_count + i] for i in range(narrow_count)]
        parts = three_parts(jnp.concatenate(pieces, axis=1))
        pick = jnp.where(back_ref[pl.ds(r, 1), :] == row_at, 1.0, 0.0).astype(jnp.bfloat16)
        result = sum_parts(dot_f32(parts, pick), tasks)
        for t in range(tasks):
            out_ref[t, pl.ds(r, 1), :] = result[t : t + 1, :]


def unpack_rows(slot_request, back, returned, narrow_count):
    requests, shard_len = back.shape
    tasks = returned.shape[1]
    return pl.pallas_call(
        functools.partial(unpack_body, narrow_count),
        out_shape=jax.ShapeDtypeStruct((tasks, requests, shard_len), jnp.float32),
        in_specs=[SMEM, VMEM, VMEM],
        out_specs=VMEM,
        compiler_params=pltpu.CompilerParams(vmem_limit_bytes=VMEM_LIMIT),
        name="unpack_rows",
    )(slot_request, back, returned)


def lanes_of(kept_index, device_rank, shard_len, narrow_count, half):
    base = device_rank * shard_len
    ids = base + jnp.arange(shard_len, dtype=jnp.int32)
    flags = jnp.any(kept_index[:, :, None] == ids[None, None, :], axis=1)
    places = jnp.cumsum(flags.astype(jnp.int32), axis=1) - flags.astype(jnp.int32)
    before = jnp.sum((kept_index < base).astype(jnp.int32), axis=1, keepdims=True)
    return jnp.where(flags, (before + places) % narrow_count * half + places // narrow_count, -1)


def from_others(values, narrow_count):
    pieces = [values]
    for shift in range(1, narrow_count):
        steps = [((i + shift) % narrow_count, i) for i in range(narrow_count)]
        pieces.append(lax.ppermute(values, "narrow", steps))
    return pieces


def on_device(
    candidates,
    pre_inner,
    pre_bias,
    pre_outer,
    user_vector,
    kept_index,
    slot_request,
    history_kv,
    history_bias,
    history_length,
    query_weight,
    norm_gain,
    expert_weight,
    gate_weight,
    gate_bias,
    tower_inner,
    tower_outer,
):
    wide_count = lax.axis_size("wide")
    narrow_count = lax.axis_size("narrow")
    shards = wide_count * narrow_count
    wide_rank = lax.axis_index("wide")
    narrow_rank = lax.axis_index("narrow")
    device_rank = wide_rank * narrow_count + narrow_rank
    requests, shard_len, features = candidates.shape
    kept_count = kept_index.shape[1]
    capacity = 2 * kept_count // shards
    half = -(-capacity // narrow_count)
    group_size = history_kv.shape[0]
    tasks = narrow_count * tower_inner.shape[0]
    width = pre_outer.shape[1]
    both = ("wide", "narrow")
    blocked = (
        shard_len % 128 == 0
        and requests % 8 == 0
        and half % 16 == 0
        and LANES % half == 0
        and shards * half % LANES == 0
        and group_size == 1
    )

    if blocked:
        packed, lanes, back = pack_rows(slot_request, kept_index, candidates, narrow_count, half)
    else:
        lanes = lanes_of(kept_index, device_rank, shard_len, narrow_count, half)
        picks = lanes[:, None, :] == jnp.arange(narrow_count * half, dtype=jnp.int32)[None, :, None]
        packed = jnp.einsum(
            "rcs,rsd->rcd", picks.astype(jnp.bfloat16), candidates, preferred_element_type=jnp.float32
        ).astype(jnp.bfloat16)[slot_request]
    packed = packed.reshape(wide_count, group_size, narrow_count, half, features)
    packed = jnp.swapaxes(packed, 1, 2).reshape(shards, group_size * half, features)
    arrived = lax.all_to_all(packed, both, split_axis=0, concat_axis=0, tiled=True)
    arrived = jnp.swapaxes(arrived.reshape(shards, group_size, half, features), 0, 1)
    arrived = arrived.reshape(group_size, shards * half, features)

    experts_here = expert_weight.shape[0]
    halves = [expert_weight[: experts_here // 2], expert_weight[experts_here // 2 :]]
    _, halves, *shared = lax.optimization_barrier(
        (packed, halves, history_kv, history_bias, tower_inner, tower_outer)
    )
    history, biases, towers, tower_outs = [from_others(values, narrow_count) for values in shared]
    halves = [from_others(values, narrow_count)[1:] for values in halves]
    experts = [expert_weight] + [piece for pieces in zip(*halves) for piece in pieces]
    if blocked:
        prerank_score = prerank(candidates, pre_inner, pre_bias, pre_outer, user_vector, lanes)
    else:
        hidden = jax.nn.relu(
            dot_f32(candidates.reshape(requests * shard_len, features), pre_inner) + pre_bias
        ).astype(jnp.bfloat16)
        embedded = dot_f32(hidden, pre_outer).astype(jnp.bfloat16)
        prerank_score = jnp.einsum(
            "rsd,rd->rs",
            embedded.reshape(requests, shard_len, width),
            user_vector,
            preferred_element_type=jnp.float32,
        )

    results = []
    for g in range(group_size):
        placing, keys, values, vectors, gate_offsets, tower_columns, *loaded = prepare(
            slot_request,
            history_length,
            kept_index,
            history,
            biases,
            tower_outs,
            pre_bias,
            norm_gain,
            gate_bias,
            [pre_inner, pre_outer, query_weight, gate_weight.T, tower_inner],
            shards,
            shard_len,
            half,
            g,
        )
        placing, prerank_score = lax.optimization_barrier((placing, prerank_score))
        results.append(
            rank_slot(
                arrived[g],
                placing,
                keys,
                values,
                vectors,
                gate_offsets,
                tower_columns,
                loaded[:4],
                experts,
                loaded[4:] + towers[1:],
                shards,
                blocked,
            )
        )

    if blocked:
        returned = lax.all_to_all(results[0], both, split_axis=0, concat_axis=0, tiled=True)
        return (prerank_score, unpack_rows(slot_request, back, returned, narrow_count))
    sending = jnp.stack(results).reshape(group_size, tasks, shards, half)
    sending = jnp.transpose(sending, (2, 0, 1, 3)).reshape(shards, -1)
    returned = lax.all_to_all(sending, both, split_axis=0, concat_axis=0, tiled=True)
    returned = returned.reshape(wide_count, narrow_count, group_size, tasks, half)
    returned = jnp.transpose(returned, (0, 2, 3, 1, 4)).reshape(requests, tasks, narrow_count * half)
    request_ids = jnp.arange(requests, dtype=jnp.int32)
    slot_of = jnp.sum(
        jnp.where(slot_request[None, :] == request_ids[:, None], request_ids[None, :], 0), axis=1
    )
    rank_score = jnp.einsum(
        "rcs,rtc->trs",
        picks.astype(jnp.float32),
        returned[slot_of],
        precision=lax.Precision.HIGHEST,
    )
    return (prerank_score, rank_score)


def solution(mesh):
    return jax.shard_map(
        on_device,
        mesh=mesh,
        in_specs=(
            P("groups", ("wide", "narrow"), None),
            P(),
            P(),
            P(),
            P("groups", None),
            P("groups", None),
            P("groups"),
            P(("groups", "wide"), None, None, "narrow"),
            P(("groups", "wide"), "narrow", None),
            P(("groups", "wide")),
            P(),
            P(),
            P("narrow", None, None),
            P(),
            P(),
            P("narrow", None, None),
            P("narrow", None),
        ),
        out_specs=(P("groups", ("wide", "narrow")), P(None, "groups", ("wide", "narrow"))),
        check_vma=False,
    )
```

time: 55.8 us -> 46.1 us (0.83)
  local copies, waits for them, and re-layouts: 13.3 us -> 0.77 us
  blocking collectives: 0 us -> 10.8 us
  starting transfers between devices: 12.9 us -> 9.13 us
  waiting for transfers between devices: 7.49 us -> 5.33 us
  between operations: 3.37 us -> 1.54 us
  Pallas kernels: 17.3 us -> 18.2 us
  other arithmetic: 0.59 us -> 0 us
    all_to_all x0 -> x1, blocking collectives: none -> 10.8 us  [on_device(): lax.all_to_all(results[0], both, split_axis=0, concat_axis=0, tiled=True)]
    unnamed x43 -> x28, local copies, waits for them, and re-layouts: 11.4 us -> 0.7 us
    all_to_all x1 -> x0, starting transfers between devices: 4.1 us -> none  [on_device(): lax.all_to_all(results[0], both, split_axis=0, concat_axis=0, tiled=True)]
    all_to_all x1, waiting for transfers between devices: 7.33 us -> 3.29 us  [on_device(): lax.all_to_all(packed, both, split_axis=0, concat_axis=0, tiled=True)]
    ppermute x5 -> x6, waiting for transfers between devices: 0.01 us -> 2.04 us  [from_others(): pieces.append(lax.ppermute(values, 'narrow', steps))]
    reshape x1 -> x0, local copies, waits for them, and re-layouts: 1.28 us -> none  [rank_slot(): gate_bias.reshape(1, -1)]
    pallas_call x2 -> x3, Pallas kernels: 11.5 us -> 12.2 us  [the longest x1 7.52 us: rank_slot(): pl.pallas_call(functools.partial(rank_body, narrow_count, len(experts), s...]
    dynamic_slice x2 -> x0, local copies, waits for them, and re-layouts: 0.59 us -> none  [the longest x1 0.58 us: on_device(): request = slot_request[wide_rank * group_size + g]]
  transfers between devices with their start and end apart: 7 -> 7, of which waited for: 2 -> 2; matrix products, arithmetic and copies ran while one was open for 6% -> 0% of each run, Pallas kernels for 11% -> 13%
where the time goes in v2:
time: 46.1 us; the launch traced here: 45.8 us
  Pallas kernels  18.2 us (39%)
  blocking collectives  10.8 us (23%)
  starting transfers between devices  9.13 us (20%)
  waiting for transfers between devices  5.33 us (12%)
  between operations  1.54 us (3%)
  local copies, waits for them, and re-layouts  0.77 us (2%)
    all_to_all x1, blocking collectives, on_device(): lax.all_to_all(results[0], both, split_axis=0, concat_axis=0, tiled=True)  10.8 us
    all_to_all x1, starting transfers between devices, on_device(): lax.all_to_all(packed, both, split_axis=0, concat_axis=0, tiled=True)  7.55 us
    pallas_call x1, Pallas kernels, rank_slot(): pl.pallas_call(functools.partial(rank_body, narrow_count, len(experts), s...  7.52 us
    pallas_call x1, Pallas kernels, pack_rows(): pl.pallas_call(functools.partial(pack_body, narrow_count, half), out_shap...  3.29 us
    all_to_all x1, waiting for transfers between devices, on_device(): lax.all_to_all(packed, both, split_axis=0, concat_axis=0, tiled=True)  3.29 us
    pallas_call x1, Pallas kernels, prepare(): pl.pallas_call(functools.partial(prepare_body, narrow_count, len(weights)...  3.26 us
    pallas_call x1, Pallas kernels, prerank(): pl.pallas_call(functools.partial(prerank_body, shard_len), out_shape=jax....  2.76 us
    ppermute x6, waiting for transfers between devices, from_others(): pieces.append(lax.ppermute(values, 'narrow', steps))  2.04 us
  transfers between devices with their start and end apart: 7, of which 2 were waited for; matrix products, arithmetic and copies ran while one was open for 0% of the time, Pallas kernels for 13%

profile of v2, /device:TPU:0, one launch (start us, length us, event | category | flops | bytes accessed | tf_op | source)
XLA Modules:
  0.0 45.8 jit_solution(762128462963624196)
XLA Ops:
  0.6 0.0 copy-start.12
  0.6 3.3 %pack_rows.1 = (bf16[512,512]{1,0:T(8,128)(2,1)}, s32[8,128]{1,0:T(8,128)S(1)}, s32[8,128]{1,0:T(8,128)S(1)}) custom-call(s32[8]{0:T(128)} %slot_ref.5, s32[8,512]{1,0:T(8,128)} %kept_ref.1, bf16[8,128,512]{2,1,0:T(8,128)(2,1)} %cand_hbm.1), custom_call_target="tpu_custom_call" | custom-call | flops 67108864 | bytes 1048576 | tf_op jit(solution)/shard_map/pack_rows/pallas_call | solution.py:105
  3.9 0.0 copy-start.3
  4.0 0.0 copy-start.13
  4.0 7.6 %all-to-all-start = ((bf16[16,32,512]{2,1,0:T(8,128)(2,1)}), bf16[16,32,512]{2,1,0:T(8,128)(2,1)}, u32[]{:S(2)}, u32[]{:S(2)}) async-start(bf16[16,32,512]{2,1,0:T(8,128)(2,1)} %bitcast.10), calls=%async_computation | async-start | bytes 1048576 | tf_op jit(solution)/shard_map/all_to_all | solution.py:584
  11.6 0.0 copy-start
  11.6 0.0 copy-start.1
  11.6 0.1 fusion
  11.7 0.4 collective-permute-start
  12.1 0.2 collective-permute-start.3
  12.3 0.4 collective-permute-start.4
  12.6 0.2 collective-permute-start.5
  12.8 0.4 collective-permute-start.2
  13.2 2.0 %collective-permute-done.2.rest_5_ = bf16[4,128]{1,0:T(4,128)(2,1)S(1)} collective-permute-done((bf16[4,128]{1,0:T(4,128)(2,1)S(1)}, bf16[4,128]{1,0:T(4,128)(2,1)S(1)}, u32[]{:S(2)}, u32[]{:S(2)}) %collective-permute-start.2) | collective-permute-done | bytes 1056 | tf_op jit(solution)/shard_map/ppermute | solution.py:528
  15.2 0.1 collective-permute-start.1
  15.4 0.0 copy-start.10
  15.4 2.8 %prerank.1 = f32[8,128]{1,0:T(8,128)} custom-call(bf16[1024,512]{1,0:T(8,128)(2,1)S(1)} %bitcast.6, bf16[512,512]{1,0:T(8,128)(2,1)S(1)} %copy-done.1, f32[1,512]{1,0:T(1,128)S(1)} %bitcast.7, bf16[512,512]{1,0:T(8,128)(2,1)S(1)} %copy-done.2, bf16[8,512]{1,0:T(8,128)(2,1)S(1)} %copy-done.5, s32[8,128]{1,0:T(8,128)S(1)} %get-tuple-element.29.lane_ref), custom_call_target="tpu_custom_call" | custom-call | flops 1 | bytes 1 | tf_op jit(solution)/shard_map/prerank/pallas_call | solution.py:143
  18.8 0.0 copy-start.8
  18.9 0.6 %copy-done.8 = s32[8]{0:T(128)S(1)} copy-done((s32[8]{0:T(128)S(1)}, s32[8]{0:T(128)}, u32[]{:S(2)}) %copy-start.8) | copy-done | bytes 56
  19.5 3.3 %prepare.1 = (bf16[256,512]{1,0:T(8,128)(2,1)S(1)}, bf16[8,128,512]{2,1,0:T(8,128)(2,1)}, bf16[8,512,128]{2,1,0:T(8,128)(2,1)}, f32[8,512]{1,0:T(8,128)S(1)}, f3...) custom-call(s32[8]{0:T(128)S(1)} %copy-done.8, ...), custom_call_target="tpu_custom_call" | custom-call | flops 1 | bytes 1 | tf_op jit(solution)/shard_map/prepare/pallas_call | solution.py:276
  22.8 3.3 %all-to-all-done = bf16[16,32,512]{2,1,0:T(8,128)(2,1)} async-done(((bf16[16,32,512]{2,1,0:T(8,128)(2,1)}), bf16[16,32,512]{2,1,0:T(8,128)(2,1)}, u32[]{:S(2)}, u32[]{:S(2)}) %all-to-all-start) | async-done | bytes 524320 | tf_op jit(solution)/shard_map/all_to_all | solution.py:584
  26.1 7.5 %rank_slot.1 = f32[16,8,128]{2,1,0:T(8,128)S(1)} custom-call(bf16[512,512]{1,0:T(8,128)(2,1)} %bitcast.5.rest_0_, bf16[8,128,512]{2,1,0:T(8,128)(2,1)} %get-tuple-element.32.rest_1_, bf16[8,512,128]{2,1,0:T(8,128)(2,1)} %get-tuple-element.33.rest_2_, bf16[4,512,256]{2,1,0:T(8,128)(2,1)} %rest_3_.1, bf16[2,512,256]{2,1,0:T(8,128)(2,1)} %collective-permute-done.3.rest_4_, ...), custom_call_target="tpu_custom_call" | custom-call | flops 1610612736 | bytes 6291456 | tf_op jit(solution)/shard_map/rank_slot/pallas_call | solution.py:464
  33.6 10.8 %all_to_all.10.returned_ref = f32[16,8,128]{2,1,0:T(8,128)S(1)} all-to-all(f32[16,8,128]{2,1,0:T(8,128)S(1)} %rank_slot.1), channel_id=1, replica_groups=mesh['groups'=2,'wide'=8,'narrow'=2] {'wide','narrow'}, dimensions={0} | all-to-all | bytes 131072 | tf_op jit(solution)/shard_map/all_to_all | solution.py:647
  44.4 1.4 %unpack_rows.1 = f32[8,8,128]{2,1,0:T(8,128)} custom-call(s32[8]{0:T(128)S(1)} %copy-done.8, s32[8,128]{1,0:T(8,128)S(1)} %get-tuple-element.31.back_ref, f32[16,8,128]{2,1,0:T(8,128)S(1)} %all_to_all.10.returned_ref), custom_call_target="tpu_custom_call" | custom-call | tf_op jit(solution)/shard_map/unpack_rows/pallas_call | solution.py:505
  (25 shorter events, 0.1 us)
Async XLA Ops:
  0.6 10.9 %copy-start.12 = (bf16[4,512,256]{2,1,0:T(8,128)(2,1)S(1)}, bf16[4,512,256]{2,1,0:T(8,128)(2,1)}, u32[]{:S(2)}) copy-start(bf16[4,512,256]{2,1,0:T(8,128)(2,1)} %rest_3_.1) | copy-start | bytes 3145732
  3.9 7.8 %copy-start.3 = (bf16[1,2,512,256]{3,2,1,0:T(8,128)(2,1)S(1)}, bf16[1,2,512,256]{3,2,1,0:T(8,128)(2,1)}, u32[]{:S(2)}) copy-start(bf16[1,2,512,256]{3,2,1,0:T(8,128)(2,1)} %rest_0_) | copy-start | bytes 1572868
  4.0 8.7 %copy-start.13 = (bf16[4,256,128]{2,1,0:T(8,128)(2,1)S(1)}, bf16[4,256,128]{2,1,0:T(8,128)(2,1)}, u32[]{:S(2)}) copy-start(bf16[4,256,128]{2,1,0:T(8,128)(2,1)} %rest_13_.1) | copy-start | bytes 786436
  4.0 11.2 %copy-start.6 = (f32[1,4,512]{2,1,0:T(4,128)S(1)}, f32[1,4,512]{2,1,0:T(4,128)}, u32[]{:S(2)}) copy-start(f32[1,4,512]{2,1,0:T(4,128)} %rest_2_) | copy-start | bytes 24580
  4.0 11.4 %copy-start.7 = (f32[512]{0:T(512)S(1)}, f32[512]{0:T(512)}, u32[]{:S(2)}) copy-start(f32[512]{0:T(512)} %param.19) | copy-start | bytes 6148
  4.0 22.1 %all-to-all-start = ((bf16[16,32,512]{2,1,0:T(8,128)(2,1)}), bf16[16,32,512]{2,1,0:T(8,128)(2,1)}, u32[]{:S(2)}, u32[]{:S(2)}) async-start(bf16[16,32,512]{2,1,0:T(8,128)(2,1)} %bitcast.10), calls=%async_computation | async-start | bytes 1048576 | tf_op jit(solution)/shard_map/all_to_all | solution.py:584
  11.6 1.2 %copy-start.11 = (bf16[4,128]{1,0:T(4,128)(2,1)S(1)}, bf16[4,128]{1,0:T(4,128)(2,1)}, u32[]{:S(2)}) copy-start(bf16[4,128]{1,0:T(4,128)(2,1)} %rest_4_) | copy-start | bytes 3076
  11.6 3.8 %copy-start = (bf16[8,128,512]{2,1,0:T(8,128)(2,1)S(1)}, bf16[8,128,512]{2,1,0:T(8,128)(2,1)}, u32[]{:S(2)}) copy-start(bf16[8,128,512]{2,1,0:T(8,128)(2,1)} %cand_hbm.1) | copy-start | bytes 3145732
  11.6 3.8 %copy-start.1 = (bf16[512,512]{1,0:T(8,128)(2,1)S(1)}, bf16[512,512]{1,0:T(8,128)(2,1)}, u32[]{:S(2)}) copy-start(bf16[512,512]{1,0:T(8,128)(2,1)} %inner_ref.1) | copy-start | bytes 1572868
  11.6 3.7 %copy-start.2 = (bf16[512,512]{1,0:T(8,128)(2,1)S(1)}, bf16[512,512]{1,0:T(8,128)(2,1)}, u32[]{:S(2)}) copy-start(bf16[512,512]{1,0:T(8,128)(2,1)} %outer_ref.1) | copy-start | bytes 1572868
  11.7 3.7 %copy-start.5 = (bf16[8,512]{1,0:T(8,128)(2,1)S(1)}, bf16[8,512]{1,0:T(8,128)(2,1)}, u32[]{:S(2)}) copy-start(bf16[8,512]{1,0:T(8,128)(2,1)} %user_ref.1) | copy-start | bytes 24580
  11.7 7.1 %collective-permute-start = (bf16[1,2,512,256]{3,2,1,0:T(8,128)(2,1)S(1)}, bf16[1,2,512,256]{3,2,1,0:T(8,128)(2,1)S(1)}, u32[]{:S(2)}, u32[]{:S(2)}) collective-permute-start(bf16[1,2,512,256]{3,2,1,0:T(8,128)(2,1)S(1)} %copy-done.3), channel_id=1, source_target_pairs={{1,0},{0,1},{3,2},{2,3},{5,4},{4,5},{7,6},{6,7},{9,8},{8,9},{11,10... | collective-permute-start | bytes 1572872 | tf_op jit(solution)/shard_map/ppermute | solution.py:528
  12.1 10.6 %collective-permute-start.3 = (bf16[2,512,256]{2,1,0:T(8,128)(2,1)S(1)}, bf16[2,512,256]{2,1,0:T(8,128)(2,1)}, u32[]{:S(2)}, u32[]{:S(2)}) collective-permute-start(bf16[2,512,256]{2,1,0:T(8,128)(2,1)S(1)} %get-tuple-element.34), channel_id=1, source_target_pairs={{1,0},{0,1},{3,2},{2,3},{5,4},{4,5},{7,6},{6,7},{9,8},{8,9},{11,10... | collective-permute-start | bytes 1572872 | tf_op jit(solution)/shard_map/ppermute | solution.py:528
  12.3 10.5 %collective-permute-start.4 = (bf16[2,512,256]{2,1,0:T(8,128)(2,1)S(1)}, bf16[2,512,256]{2,1,0:T(8,128)(2,1)}, u32[]{:S(2)}, u32[]{:S(2)}) collective-permute-start(bf16[2,512,256]{2,1,0:T(8,128)(2,1)S(1)} %get-tuple-element.35), channel_id=1, source_target_pairs={{1,0},{0,1},{3,2},{2,3},{5,4},{4,5},{7,6},{6,7},{9,8},{8,9},{11,10... | collective-permute-start | bytes 1572872 | tf_op jit(solution)/shard_map/ppermute | solution.py:528
  12.6 10.1 %collective-permute-start.5 = (bf16[4,256,128]{2,1,0:T(8,128)(2,1)S(1)}, bf16[4,256,128]{2,1,0:T(8,128)(2,1)S(1)}, u32[]{:S(2)}, u32[]{:S(2)}) collective-permute-start(bf16[4,256,128]{2,1,0:T(8,128)(2,1)S(1)} %copy-done.13), channel_id=1, source_target_pairs={{1,0},{0,1},{3,2},{2,3},{5,4},{4,5},{7,6},{6,7},{9,8},{8,9},{11,10... | collective-permute-start | bytes 786440 | tf_op jit(solution)/shard_map/ppermute | solution.py:528
  12.8 2.4 %collective-permute-start.2 = (bf16[4,128]{1,0:T(4,128)(2,1)S(1)}, bf16[4,128]{1,0:T(4,128)(2,1)S(1)}, u32[]{:S(2)}, u32[]{:S(2)}) collective-permute-start(bf16[4,128]{1,0:T(4,128)(2,1)S(1)} %copy-done.11), channel_id=1, source_target_pairs={{1,0},{0,1},{3,2},{2,3},{5,4},{4,5},{7,6},{6,7},{9,8},{8,9},{11,10... | collective-permute-start | bytes 3080 | tf_op jit(solution)/shard_map/ppermute | solution.py:528
  15.2 3.6 %collective-permute-start.1 = (f32[1,4,512]{2,1,0:T(4,128)S(1)}, f32[1,4,512]{2,1,0:T(4,128)S(1)}, u32[]{:S(2)}, u32[]{:S(2)}) collective-permute-start(f32[1,4,512]{2,1,0:T(4,128)S(1)} %copy-done.6), channel_id=1, source_target_pairs={{1,0},{0,1},{3,2},{2,3},{5,4},{4,5},{7,6},{6,7},{9,8},{8,9},{11,10... | collective-permute-start | bytes 24584 | tf_op jit(solution)/shard_map/ppermute | solution.py:528
  15.3 3.5 %copy-start.4 = (s32[8,512]{1,0:T(8,128)S(1)}, s32[8,512]{1,0:T(8,128)}, u32[]{:S(2)}) copy-start(s32[8,512]{1,0:T(8,128)} %kept_ref.1) | copy-start | bytes 49156
  15.4 3.5 %copy-start.10 = (f32[512]{0:T(512)S(1)}, f32[512]{0:T(512)}, u32[]{:S(2)}) copy-start(f32[512]{0:T(512)} %param.28) | copy-start | bytes 6148
  18.1 0.7 %copy-start.9 = (f32[8,8]{1,0:T(8,128)S(1)}, f32[8,8]{1,0:T(8,128)}, u32[]{:S(2)}) copy-start(f32[8,8]{1,0:T(8,128)} %rest_8_.1) | copy-start | bytes 772
  18.8 0.7 %copy-start.8 = (s32[8]{0:T(128)S(1)}, s32[8]{0:T(128)}, u32[]{:S(2)}) copy-start(s32[8]{0:T(128)} %slot_ref.5) | copy-start | bytes 100

commit v3 on v2

--- a/solution.py
+++ b/solution.py
@@ -13,6 +13,7 @@
 ANY = pl.BlockSpec(memory_space=pl.ANY)
 VMEM_LIMIT = 16 * 1024 * 1024
 LANES = 128
+BIAS_ROWS = 8
 BRIEF = pl.CostEstimate(flops=1, bytes_accessed=1, transcendentals=0)
 
 
@@ -53,14 +54,27 @@
 
 
 def pack_body(
-    narrow_count, half, slot_ref, kept_hbm, cand_hbm, out_hbm, lane_ref, back_ref, kept_ref, cand_ref, out_ref, sems
+    narrow_count,
+    half,
+    slot_hbm,
+    kept_hbm,
+    cand_hbm,
+    out_hbm,
+    lane_ref,
+    back_ref,
+    slot_ref,
+    kept_ref,
+    cand_ref,
+    out_ref,
+    sems,
 ):
     requests, shard_len, _ = cand_ref.shape
     kept_count = kept_ref.shape[1]
     kept_copy = pltpu.make_async_copy(kept_hbm, kept_ref, sems.at[0])
     cand_copy = pltpu.make_async_copy(cand_hbm, cand_ref, sems.at[1])
-    kept_copy.start()
-    cand_copy.start()
+    slot_copy = pltpu.make_async_copy(slot_hbm, slot_ref, sems.at[2])
+    for copy in (kept_copy, slot_copy, cand_copy):
+        copy.start()
     device = lax.axis_index("wide") * narrow_count + lax.axis_index("narrow")
     base = device * shard_len
     ids = base + lax.broadcasted_iota(jnp.int32, (shard_len, kept_count), 0)
@@ -86,6 +100,7 @@
     back_ref[...] = jnp.where(kept_here, owner * LANES + offset + within, -1)
     rows = narrow_count * half
     row_at = lax.broadcasted_iota(jnp.int32, (rows, shard_len), 0)
+    slot_copy.wait()
     cand_copy.wait()
     sends = []
     for s in range(requests):
@@ -93,7 +108,7 @@
         pick = jnp.where(lane_ref[pl.ds(r, 1), :] == row_at, 1.0, 0.0).astype(jnp.bfloat16)
         out_ref[s * rows : (s + 1) * rows, :] = dot_f32(pick, cand_ref[r]).astype(jnp.bfloat16)
         part = pl.ds(s * rows, rows)
-        sends.append(pltpu.make_async_copy(out_ref.at[part], out_hbm.at[part], sems.at[2 + s]))
+        sends.append(pltpu.make_async_copy(out_ref.at[part], out_hbm.at[part], sems.at[3 + s]))
         sends[s].start()
     for send in sends:
         send.wait()
@@ -109,13 +124,14 @@
             jax.ShapeDtypeStruct((requests, shard_len), jnp.int32),
             jax.ShapeDtypeStruct((requests, shard_len), jnp.int32),
         ),
-        in_specs=[SMEM, ANY, ANY],
+        in_specs=[ANY, ANY, ANY],
         out_specs=(ANY, VMEM, VMEM),
         scratch_shapes=[
+            pltpu.SMEM(slot_request.shape, jnp.int32),
             pltpu.VMEM(kept_index.shape, jnp.int32),
             pltpu.VMEM((requests, shard_len, features), jnp.bfloat16),
             pltpu.VMEM((rows, features), jnp.bfloat16),
-            pltpu.SemaphoreType.DMA((2 + requests,)),
+            pltpu.SemaphoreType.DMA((3 + requests,)),
         ],
         compiler_params=pltpu.CompilerParams(vmem_limit_bytes=VMEM_LIMIT),
         cost_estimate=pl.CostEstimate(
@@ -215,34 +231,27 @@
 
     head_size = head_columns // heads_here
     tile = 2 * head_size
+    pairs_here = heads_here // 2
     visible = lax.broadcasted_iota(jnp.int32, (1, span), 1) < length_ref[slot_at]
-    lane = lax.broadcasted_iota(jnp.int32, (span, tile), 1)
+    row = lax.broadcasted_iota(jnp.int32, (BIAS_ROWS, span), 0)
     for i in range(narrow_count):
-        for t in range(heads_here // 2):
+        for t in range(pairs_here):
+            at = i * pairs_here + t
             keys = history_refs[i][slot_at, 0, :, t * tile : (t + 1) * tile]
-            keys = jnp.transpose(keys.astype(jnp.float32)).astype(jnp.bfloat16)
-            values = history_refs[i][slot_at, 1, :, t * tile : (t + 1) * tile]
+            keys_ref[at, :tile, :] = jnp.transpose(keys.astype(jnp.float32)).astype(jnp.bfloat16)
+            bias = jnp.zeros((BIAS_ROWS, span), jnp.float32)
             for h in range(2):
                 head = 2 * t + h
-                at = i * heads_here + head
-                bias = jnp.where(visible, bias_refs[i][slot_at, head : head + 1, :], -1e30)
-                parts = three_parts(jnp.broadcast_to(bias, (8, span)).astype(jnp.float32))
-                row = lax.broadcasted_iota(jnp.int32, (head_size, span), 0)
-                high = jnp.broadcast_to(parts[0:1].astype(jnp.float32), (head_size, span))
-                middle = jnp.broadcast_to(parts[8:9].astype(jnp.float32), (head_size, span))
-                low = jnp.broadcast_to(parts[16:17].astype(jnp.float32), (head_size, span))
-                extra = jnp.where(
-                    row == 0, high, jnp.where(row == 1, middle, jnp.where(row == 2, low, 0.0))
-                ).astype(jnp.bfloat16)
-                own = h * head_size
-                other = (1 - h) * head_size
-                keys_ref[at, own : own + head_size, :] = keys[own : own + head_size, :]
-                keys_ref[at, other : other + head_size, :] = extra
-                mine = (lane >= own) & (lane < own + head_size)
-                values_ref[at] = jnp.where(mine, values.astype(jnp.float32), 1.0).astype(jnp.bfloat16)
-                copies.append(pltpu.make_async_copy(keys_ref.at[at], keys_hbm.at[at], head_sems.at[0, at]))
-                copies[-1].start()
-                copies.append(pltpu.make_async_copy(values_ref.at[at], values_hbm.at[at], head_sems.at[1, at]))
+                masked = jnp.where(visible, bias_refs[i][slot_at, head : head + 1, :], -1e30)
+                bias = jnp.where(row == h, masked, bias)
+            parts = three_parts(bias)
+            keys_ref[at, tile:, :] = jnp.concatenate(
+                [parts, jnp.zeros((tile - parts.shape[0], span), jnp.bfloat16)], axis=0
+            )
+            values_ref[at, :, :tile] = history_refs[i][slot_at, 1, :, t * tile : (t + 1) * tile]
+            values_ref[at, :, tile:] = jnp.ones((span, tile), jnp.bfloat16)
+            for j, (source, target) in enumerate([(keys_ref, keys_hbm), (values_ref, values_hbm)]):
+                copies.append(pltpu.make_async_copy(source.at[at], target.at[at], head_sems.at[j, at]))
                 copies[-1].start()
     for copy in copies:
         copy.wait()
@@ -267,7 +276,7 @@
     narrow_count = len(history)
     _, _, span, head_columns = history[0].shape
     heads_here = biases[0].shape[1]
-    heads = narrow_count * heads_here
+    pairs = narrow_count * heads_here // 2
     tile = 2 * head_columns // heads_here
     rows = kept_index.shape[1] // narrow_count
     tasks, experts = gate_bias.shape
@@ -277,8 +286,8 @@
         functools.partial(prepare_body, narrow_count, len(weights), shards, shard_len, slot_at),
         out_shape=(
             pltpu.VMEM((rows, shards * half), bf16),
-            pltpu.HBM((heads, tile, span), bf16),
-            pltpu.HBM((heads, span, tile), bf16),
+            pltpu.HBM((pairs, 2 * tile, span), bf16),
+            pltpu.HBM((pairs, span, 2 * tile), bf16),
             pltpu.VMEM((8, width), jnp.float32),
             pltpu.VMEM((tasks * experts, LANES), jnp.float32),
             pltpu.VMEM((tasks, tower_outer[0].shape[1], LANES), bf16),
@@ -287,9 +296,9 @@
         in_specs=[SMEM, SMEM] + [VMEM] * (4 + 3 * narrow_count) + [ANY] * len(weights),
         out_specs=(VMEM, ANY, ANY) + (VMEM,) * (3 + len(weights)),
         scratch_shapes=[
-            pltpu.VMEM((heads, tile, span), bf16),
-            pltpu.VMEM((heads, span, tile), bf16),
-            pltpu.SemaphoreType.DMA((2, heads)),
+            pltpu.VMEM((pairs, 2 * tile, span), bf16),
+            pltpu.VMEM((pairs, span, 2 * tile), bf16),
+            pltpu.SemaphoreType.DMA((2, pairs)),
             pltpu.SemaphoreType.DMA((len(weights),)),
         ],
         compiler_params=pltpu.CompilerParams(vmem_limit_bytes=VMEM_LIMIT),
@@ -309,7 +318,7 @@
     )
 
 
-def rank_body(narrow_count, pieces, shards, spread, heads, *rest):
+def rank_body(narrow_count, pieces, shards, spread, *rest):
     arrived_hbm, keys_hbm, values_hbm = rest[:3]
     expert_hbm = rest[3 : 3 + pieces]
     rest = rest[3 + pieces :]
@@ -344,8 +353,6 @@
 
     rows = embed_ref.shape[0]
     half = arrived_ref.shape[0] // shards
-    width = queries_ref.shape[1]
-    head_size = width // heads
     experts = expert_refs.shape[0]
     experts_here = experts // narrow_count
     tasks_here = tower_refs[0].shape[0]
@@ -362,29 +369,27 @@
     queries = dot_f32(embed, query_ref[...]).astype(jnp.bfloat16)
     queries_ref[...] = queries
 
-    tile = 2 * head_size
-    heads_here = heads // narrow_count
-    scale = float(head_size) ** (-0.5)
+    tile = keys_ref.shape[1] // 2
+    pairs = keys_ref.shape[0]
+    scale = (tile // 2) ** (-0.5)
     lane = lax.broadcasted_iota(jnp.int32, (rows, tile), 1)
-    left = lane < head_size
+    left = lane < tile // 2
+    _, part = split_by(lane, BIAS_ROWS)
+    bias_lanes = lane < 3 * BIAS_ROWS
+    ones = [jnp.where(bias_lanes & (part == h), 1.0, 0.0).astype(jnp.bfloat16) for h in range(2)]
     for copy in head_copies:
         copy.wait()
-    for i in range(narrow_count):
-        at = lax.rem(me + i, narrow_count) * (width // narrow_count)
-        for t in range(heads_here // 2):
-            columns = pl.ds(pl.multiple_of(at + t * tile, tile), tile)
-            scaled = queries_ref[:, columns].astype(jnp.float32) * scale
-            results = []
-            for h in range(2):
-                head = i * heads_here + 2 * t + h
-                other = (1 - h) * head_size
-                ones = jnp.where((lane >= other) & (lane < other + 3), 1.0, 0.0)
-                query = jnp.where(left if h == 0 else ~left, scaled, ones).astype(jnp.bfloat16)
-                scores = dot_f32(query, keys_ref[head])
-                powers = jnp.exp(scores - jnp.max(scores, axis=1, keepdims=True))
-                results.append(dot_f32(powers.astype(jnp.bfloat16), values_ref[head]))
-            sums = pltpu.roll(jnp.where(left, results[1], results[0]), head_size, 1)
-            attended_ref[:, columns] = (jnp.where(left, results[0], results[1]) / sums).astype(jnp.bfloat16)
+    for pair in range(pairs):
+        _, place = split_by(me * (pairs // narrow_count) + pair, pairs)
+        columns = pl.ds(pl.multiple_of(place * tile, tile), tile)
+        scaled = queries_ref[:, columns].astype(jnp.float32) * scale
+        query = [jnp.where(own, scaled, 0.0).astype(jnp.bfloat16) for own in (left, ~left)]
+        query = jnp.concatenate([jnp.concatenate([query[h], ones[h]], axis=1) for h in range(2)], axis=0)
+        scores = dot_f32(query, keys_ref[pair])
+        powers = jnp.exp(scores - jnp.max(scores, axis=1, keepdims=True))
+        result = dot_f32(powers.astype(jnp.bfloat16), values_ref[pair])
+        result = result[:, :tile] / result[:, tile:]
+        attended_ref[:, columns] = jnp.where(left, result[:rows], result[rows:]).astype(jnp.bfloat16)
 
     mixed_in = embed_ref[...].astype(jnp.float32) + attended_ref[...].astype(jnp.float32)
     normed = (
@@ -412,11 +417,11 @@
     _, column_expert = split_by(column_expert + me * experts_here, experts)
     _, row_in_block = split_by(lax.broadcasted_iota(jnp.int32, (rows, experts * block), 0), block)
     _, column_row = split_by(lax.broadcasted_iota(jnp.int32, (rows, experts * block), 1), block)
-    diagonal = row_in_block == column_row
+    diagonal = jnp.where(row_in_block == column_row, 1.0, 0.0).astype(jnp.bfloat16)
     for t in range(tasks):
         _, task = split_by(me * tasks_here + t, tasks)
         expand = jnp.where(gate_at == column_expert + task * experts, 1.0, 0.0).astype(jnp.bfloat16)
-        wide = jnp.where(diagonal, dot_f32(gates, expand), 0.0).astype(jnp.bfloat16)
+        wide = dot_f32(gates, expand).astype(jnp.bfloat16) * diagonal
         for b in range(blocks):
             gates_ref[b, t * block : (t + 1) * block, :] = wide[b * block : (b + 1) * block, :]
     for b in range(blocks):
@@ -424,12 +429,14 @@
         for t in range(tasks):
             mixture_ref[t, b * block : (b + 1) * block, :] = mixture[t * block : (t + 1) * block, :]
 
-    logits = jnp.zeros((rows, LANES), jnp.float32)
+    acts = []
     for i in range(narrow_count):
         for t in range(tasks_here):
             at = i * tasks_here + t
-            act = jnp.maximum(dot_f32(mixture_ref[at], tower_refs[i][t]), 0.0).astype(jnp.bfloat16)
-            logits = logits + dot_f32(act, tower_columns_ref[at])
+            acts.append(jnp.maximum(dot_f32(mixture_ref[at], tower_refs[i][t]), 0.0).astype(jnp.bfloat16))
+    columns = tower_columns_ref[...]
+    columns = columns.reshape(columns.shape[0] * columns.shape[1], columns.shape[2])
+    logits = dot_f32(jnp.concatenate(acts, axis=1), columns)
     by_task = jnp.transpose(logits)[:tasks]
 
     returned = sum_parts(dot_f32(three_parts(by_task), placing_ref[...]), tasks)
@@ -447,7 +454,6 @@
     inner, outer, query, gate_rows = weights
     narrow_count = len(towers)
     rows, rows_in = placing.shape
-    heads = keys.shape[0]
     width = outer.shape[1]
     tasks = tower_columns.shape[0]
     expert_count = gate_rows.shape[0] // tasks
@@ -462,7 +468,7 @@
     far = [arrived, keys, values, *experts]
     near = [placing, vectors, gate_offsets, tower_columns, *weights, *towers]
     return pl.pallas_call(
-        functools.partial(rank_body, narrow_count, len(experts), shards, spread, heads),
+        functools.partial(rank_body, narrow_count, len(experts), shards, spread),
         out_shape=out_shape,
         in_specs=[ANY] * len(far) + [VMEM] * len(near),
         out_specs=VMEM,

time: 46.1 us -> 43.9 us (0.952)
  Pallas kernels: 18.2 us -> 16.1 us
    pallas_call x1, Pallas kernels: 7.52 us -> 6.02 us  [rank_slot(): pl.pallas_call(functools.partial(rank_body, narrow_count, len(experts), s...]
    pallas_call x1, Pallas kernels: 3.29 us -> 2.6 us  [pack_rows(): pl.pallas_call(functools.partial(pack_body, narrow_count, half), out_shap...]
  transfers between devices with their start and end apart: 7 -> 7, of which waited for: 2 -> 2; matrix products, arithmetic and copies ran while one was open for 0% -> 0% of each run, Pallas kernels for 13% -> 14%
where the time goes in v3:
time: 43.9 us; the launch traced here: 43.6 us
  Pallas kernels  16.1 us (37%)
  blocking collectives  10.8 us (25%)
  starting transfers between devices  9.13 us (21%)
  waiting for transfers between devices  5.28 us (12%)
  between operations  1.54 us (4%)
  local copies, waits for them, and re-layouts  0.77 us (2%)
    all_to_all x1, blocking collectives, on_device(): lax.all_to_all(results[0], both, split_axis=0, concat_axis=0, tiled=True)  10.8 us
    all_to_all x1, starting transfers between devices, on_device(): lax.all_to_all(packed, both, split_axis=0, concat_axis=0, tiled=True)  7.55 us
    pallas_call x1, Pallas kernels, rank_slot(): pl.pallas_call(functools.partial(rank_body, narrow_count, len(experts), s...  6.02 us
    pallas_call x1, Pallas kernels, prepare(): pl.pallas_call(functools.partial(prepare_body, narrow_count, len(weights)...  3.31 us
    all_to_all x1, waiting for transfers between devices, on_device(): lax.all_to_all(packed, both, split_axis=0, concat_axis=0, tiled=True)  3.24 us
    pallas_call x1, Pallas kernels, prerank(): pl.pallas_call(functools.partial(prerank_body, shard_len), out_shape=jax....  2.76 us
    pallas_call x1, Pallas kernels, pack_rows(): pl.pallas_call(functools.partial(pack_body, narrow_count, half), out_shap...  2.6 us
    ppermute x6, waiting for transfers between devices, from_others(): pieces.append(lax.ppermute(values, 'narrow', steps))  2.04 us
  transfers between devices with their start and end apart: 7, of which 2 were waited for; matrix products, arithmetic and copies ran while one was open for 0% of the time, Pallas kernels for 14%

profile of v3, /device:TPU:0, one launch (start us, length us, event | category | flops | bytes accessed | tf_op | source)
XLA Modules:
  0.0 43.6 jit_solution(1593832745388937152)
XLA Ops:
  0.6 0.0 copy-start.12
  0.6 2.6 %pack_rows.1 = (bf16[512,512]{1,0:T(8,128)(2,1)}, s32[8,128]{1,0:T(8,128)S(1)}, s32[8,128]{1,0:T(8,128)S(1)}) custom-call(s32[8]{0:T(128)} %slot_ref.3, s32[8,512]{1,0:T(8,128)} %kept_ref.1, bf16[8,128,512]{2,1,0:T(8,128)(2,1)} %cand_hbm.1), custom_call_target="tpu_custom_call" | custom-call | flops 67108864 | bytes 1048576 | tf_op jit(solution)/shard_map/pack_rows/pallas_call | solution.py:120
  3.2 0.0 copy-start.3
  3.3 0.0 copy-start.13
  3.3 7.6 %all-to-all-start = ((bf16[16,32,512]{2,1,0:T(8,128)(2,1)}), bf16[16,32,512]{2,1,0:T(8,128)(2,1)}, u32[]{:S(2)}, u32[]{:S(2)}) async-start(bf16[16,32,512]{2,1,0:T(8,128)(2,1)} %bitcast.10), calls=%async_computation | async-start | bytes 1048576 | tf_op jit(solution)/shard_map/all_to_all | solution.py:590
  10.9 0.0 copy-start.11
  10.9 0.0 copy-start
  10.9 0.0 copy-start.2
  10.9 0.1 fusion
  11.0 0.0 copy-start.5
  11.0 0.4 collective-permute-start
  11.4 0.2 collective-permute-start.3
  11.6 0.4 collective-permute-start.4
  11.9 0.2 collective-permute-start.5
  12.1 0.4 collective-permute-start.2
  12.5 2.0 %collective-permute-done.2.rest_5_ = bf16[4,128]{1,0:T(4,128)(2,1)S(1)} collective-permute-done((bf16[4,128]{1,0:T(4,128)(2,1)S(1)}, bf16[4,128]{1,0:T(4,128)(2,1)S(1)}, u32[]{:S(2)}, u32[]{:S(2)}) %collective-permute-start.2) | collective-permute-done | bytes 1056 | tf_op jit(solution)/shard_map/ppermute | solution.py:534
  14.5 0.1 collective-permute-start.1
  14.7 2.8 %prerank.1 = f32[8,128]{1,0:T(8,128)} custom-call(bf16[1024,512]{1,0:T(8,128)(2,1)S(1)} %bitcast.6, bf16[512,512]{1,0:T(8,128)(2,1)S(1)} %copy-done.1, f32[1,512]{1,0:T(1,128)S(1)} %bitcast.7, bf16[512,512]{1,0:T(8,128)(2,1)S(1)} %copy-done.2, bf16[8,512]{1,0:T(8,128)(2,1)S(1)} %copy-done.5, s32[8,128]{1,0:T(8,128)S(1)} %get-tuple-element.29.lane_ref), custom_call_target="tpu_custom_call" | custom-call | flops 1 | bytes 1 | tf_op jit(solution)/shard_map/prerank/pallas_call | solution.py:159
  18.2 0.6 %copy-done.8 = s32[8]{0:T(128)S(1)} copy-done((s32[8]{0:T(128)S(1)}, s32[8]{0:T(128)}, u32[]{:S(2)}) %copy-start.8) | copy-done | bytes 56
  18.8 3.3 %prepare.1 = (bf16[256,512]{1,0:T(8,128)(2,1)S(1)}, bf16[4,256,512]{2,1,0:T(8,128)(2,1)}, bf16[4,512,256]{2,1,0:T(8,128)(2,1)}, f32[8,512]{1,0:T(8,128)S(1)}, f3...) custom-call(s32[8]{0:T(128)S(1)} %copy-done.8, ...), custom_call_target="tpu_custom_call" | custom-call | flops 1 | bytes 1 | tf_op jit(solution)/shard_map/prepare/pallas_call | solution.py:285
  22.1 3.2 %all-to-all-done = bf16[16,32,512]{2,1,0:T(8,128)(2,1)} async-done(((bf16[16,32,512]{2,1,0:T(8,128)(2,1)}), bf16[16,32,512]{2,1,0:T(8,128)(2,1)}, u32[]{:S(2)}, u32[]{:S(2)}) %all-to-all-start) | async-done | bytes 524320 | tf_op jit(solution)/shard_map/all_to_all | solution.py:590
  25.4 6.0 %rank_slot.1 = f32[16,8,128]{2,1,0:T(8,128)S(1)} custom-call(bf16[512,512]{1,0:T(8,128)(2,1)} %bitcast.5.rest_0_, bf16[4,256,512]{2,1,0:T(8,128)(2,1)} %get-tuple-element.32.rest_1_, bf16[4,512,256]{2,1,0:T(8,128)(2,1)} %get-tuple-element.33.rest_2_, bf16[4,512,256]{2,1,0:T(8,128)(2,1)} %rest_3_.1, bf16[2,512,256]{2,1,0:T(8,128)(2,1)} %collective-permute-done.3.rest_4_, ...), custom_call_target="tpu_custom_call" | custom-call | flops 1610612736 | bytes 6291456 | tf_op jit(solution)/shard_map/rank_slot/pallas_call | solution.py:470
  31.4 10.8 %all_to_all.10.returned_ref = f32[16,8,128]{2,1,0:T(8,128)S(1)} all-to-all(f32[16,8,128]{2,1,0:T(8,128)S(1)} %rank_slot.1), channel_id=1, replica_groups=mesh['groups'=2,'wide'=8,'narrow'=2] {'wide','narrow'}, dimensions={0} | all-to-all | bytes 131072 | tf_op jit(solution)/shard_map/all_to_all | solution.py:653
  42.2 1.4 %unpack_rows.1 = f32[8,8,128]{2,1,0:T(8,128)} custom-call(s32[8]{0:T(128)S(1)} %copy-done.8, s32[8,128]{1,0:T(8,128)S(1)} %get-tuple-element.31.back_ref, f32[16,8,128]{2,1,0:T(8,128)S(1)} %all_to_all.10.returned_ref), custom_call_target="tpu_custom_call" | custom-call | tf_op jit(solution)/shard_map/unpack_rows/pallas_call | solution.py:511
  (25 shorter events, 0.1 us)
Async XLA Ops:
  0.6 10.2 %copy-start.12 = (bf16[4,512,256]{2,1,0:T(8,128)(2,1)S(1)}, bf16[4,512,256]{2,1,0:T(8,128)(2,1)}, u32[]{:S(2)}) copy-start(bf16[4,512,256]{2,1,0:T(8,128)(2,1)} %rest_3_.1) | copy-start | bytes 3145732
  3.2 7.8 %copy-start.3 = (bf16[1,2,512,256]{3,2,1,0:T(8,128)(2,1)S(1)}, bf16[1,2,512,256]{3,2,1,0:T(8,128)(2,1)}, u32[]{:S(2)}) copy-start(bf16[1,2,512,256]{3,2,1,0:T(8,128)(2,1)} %rest_0_) | copy-start | bytes 1572868
  3.3 8.7 %copy-start.13 = (bf16[4,256,128]{2,1,0:T(8,128)(2,1)S(1)}, bf16[4,256,128]{2,1,0:T(8,128)(2,1)}, u32[]{:S(2)}) copy-start(bf16[4,256,128]{2,1,0:T(8,128)(2,1)} %rest_13_.1) | copy-start | bytes 786436
  3.3 11.2 %copy-start.6 = (f32[1,4,512]{2,1,0:T(4,128)S(1)}, f32[1,4,512]{2,1,0:T(4,128)}, u32[]{:S(2)}) copy-start(f32[1,4,512]{2,1,0:T(4,128)} %rest_2_) | copy-start | bytes 24580
  3.3 11.3 %copy-start.7 = (f32[512]{0:T(512)S(1)}, f32[512]{0:T(512)}, u32[]{:S(2)}) copy-start(f32[512]{0:T(512)} %param.19) | copy-start | bytes 6148
  3.3 22.1 %all-to-all-start = ((bf16[16,32,512]{2,1,0:T(8,128)(2,1)}), bf16[16,32,512]{2,1,0:T(8,128)(2,1)}, u32[]{:S(2)}, u32[]{:S(2)}) async-start(bf16[16,32,512]{2,1,0:T(8,128)(2,1)} %bitcast.10), calls=%async_computation | async-start | bytes 1048576 | tf_op jit(solution)/shard_map/all_to_all | solution.py:590
  10.9 1.2 %copy-start.11 = (bf16[4,128]{1,0:T(4,128)(2,1)S(1)}, bf16[4,128]{1,0:T(4,128)(2,1)}, u32[]{:S(2)}) copy-start(bf16[4,128]{1,0:T(4,128)(2,1)} %rest_4_) | copy-start | bytes 3076
  10.9 3.8 %copy-start = (bf16[8,128,512]{2,1,0:T(8,128)(2,1)S(1)}, bf16[8,128,512]{2,1,0:T(8,128)(2,1)}, u32[]{:S(2)}) copy-start(bf16[8,128,512]{2,1,0:T(8,128)(2,1)} %cand_hbm.1) | copy-start | bytes 3145732
  10.9 3.8 %copy-start.1 = (bf16[512,512]{1,0:T(8,128)(2,1)S(1)}, bf16[512,512]{1,0:T(8,128)(2,1)}, u32[]{:S(2)}) copy-start(bf16[512,512]{1,0:T(8,128)(2,1)} %inner_ref.1) | copy-start | bytes 1572868
  10.9 3.7 %copy-start.2 = (bf16[512,512]{1,0:T(8,128)(2,1)S(1)}, bf16[512,512]{1,0:T(8,128)(2,1)}, u32[]{:S(2)}) copy-start(bf16[512,512]{1,0:T(8,128)(2,1)} %outer_ref.1) | copy-start | bytes 1572868
  11.0 3.7 %copy-start.5 = (bf16[8,512]{1,0:T(8,128)(2,1)S(1)}, bf16[8,512]{1,0:T(8,128)(2,1)}, u32[]{:S(2)}) copy-start(bf16[8,512]{1,0:T(8,128)(2,1)} %user_ref.1) | copy-start | bytes 24580
  11.0 7.1 %collective-permute-start = (bf16[1,2,512,256]{3,2,1,0:T(8,128)(2,1)S(1)}, bf16[1,2,512,256]{3,2,1,0:T(8,128)(2,1)S(1)}, u32[]{:S(2)}, u32[]{:S(2)}) collective-permute-start(bf16[1,2,512,256]{3,2,1,0:T(8,128)(2,1)S(1)} %copy-done.3), channel_id=1, source_target_pairs={{1,0},{0,1},{3,2},{2,3},{5,4},{4,5},{7,6},{6,7},{9,8},{8,9},{11,10... | collective-permute-start | bytes 1572872 | tf_op jit(solution)/shard_map/ppermute | solution.py:534
  11.4 10.7 %collective-permute-start.3 = (bf16[2,512,256]{2,1,0:T(8,128)(2,1)S(1)}, bf16[2,512,256]{2,1,0:T(8,128)(2,1)}, u32[]{:S(2)}, u32[]{:S(2)}) collective-permute-start(bf16[2,512,256]{2,1,0:T(8,128)(2,1)S(1)} %get-tuple-element.34), channel_id=1, source_target_pairs={{1,0},{0,1},{3,2},{2,3},{5,4},{4,5},{7,6},{6,7},{9,8},{8,9},{11,10... | collective-permute-start | bytes 1572872 | tf_op jit(solution)/shard_map/ppermute | solution.py:534
  11.6 10.5 %collective-permute-start.4 = (bf16[2,512,256]{2,1,0:T(8,128)(2,1)S(1)}, bf16[2,512,256]{2,1,0:T(8,128)(2,1)}, u32[]{:S(2)}, u32[]{:S(2)}) collective-permute-start(bf16[2,512,256]{2,1,0:T(8,128)(2,1)S(1)} %get-tuple-element.35), channel_id=1, source_target_pairs={{1,0},{0,1},{3,2},{2,3},{5,4},{4,5},{7,6},{6,7},{9,8},{8,9},{11,10... | collective-permute-start | bytes 1572872 | tf_op jit(solution)/shard_map/ppermute | solution.py:534
  11.9 10.2 %collective-permute-start.5 = (bf16[4,256,128]{2,1,0:T(8,128)(2,1)S(1)}, bf16[4,256,128]{2,1,0:T(8,128)(2,1)S(1)}, u32[]{:S(2)}, u32[]{:S(2)}) collective-permute-start(bf16[4,256,128]{2,1,0:T(8,128)(2,1)S(1)} %copy-done.13), channel_id=1, source_target_pairs={{1,0},{0,1},{3,2},{2,3},{5,4},{4,5},{7,6},{6,7},{9,8},{8,9},{11,10... | collective-permute-start | bytes 786440 | tf_op jit(solution)/shard_map/ppermute | solution.py:534
  12.1 2.4 %collective-permute-start.2 = (bf16[4,128]{1,0:T(4,128)(2,1)S(1)}, bf16[4,128]{1,0:T(4,128)(2,1)S(1)}, u32[]{:S(2)}, u32[]{:S(2)}) collective-permute-start(bf16[4,128]{1,0:T(4,128)(2,1)S(1)} %copy-done.11), channel_id=1, source_target_pairs={{1,0},{0,1},{3,2},{2,3},{5,4},{4,5},{7,6},{6,7},{9,8},{8,9},{11,10... | collective-permute-start | bytes 3080 | tf_op jit(solution)/shard_map/ppermute | solution.py:534
  14.5 3.6 %collective-permute-start.1 = (f32[1,4,512]{2,1,0:T(4,128)S(1)}, f32[1,4,512]{2,1,0:T(4,128)S(1)}, u32[]{:S(2)}, u32[]{:S(2)}) collective-permute-start(f32[1,4,512]{2,1,0:T(4,128)S(1)} %copy-done.6), channel_id=1, source_target_pairs={{1,0},{0,1},{3,2},{2,3},{5,4},{4,5},{7,6},{6,7},{9,8},{8,9},{11,10... | collective-permute-start | bytes 24584 | tf_op jit(solution)/shard_map/ppermute | solution.py:534
  14.7 3.5 %copy-start.4 = (s32[8,512]{1,0:T(8,128)S(1)}, s32[8,512]{1,0:T(8,128)}, u32[]{:S(2)}) copy-start(s32[8,512]{1,0:T(8,128)} %kept_ref.1) | copy-start | bytes 49156
  14.7 3.5 %copy-start.10 = (f32[512]{0:T(512)S(1)}, f32[512]{0:T(512)}, u32[]{:S(2)}) copy-start(f32[512]{0:T(512)} %param.28) | copy-start | bytes 6148
  17.4 0.7 %copy-start.9 = (f32[8,8]{1,0:T(8,128)S(1)}, f32[8,8]{1,0:T(8,128)}, u32[]{:S(2)}) copy-start(f32[8,8]{1,0:T(8,128)} %rest_8_.1) | copy-start | bytes 772
  18.1 0.7 %copy-start.8 = (s32[8]{0:T(128)S(1)}, s32[8]{0:T(128)}, u32[]{:S(2)}) copy-start(s32[8]{0:T(128)} %slot_ref.3) | copy-start | bytes 100

commit v4 on v3

--- a/solution.py
+++ b/solution.py
@@ -62,6 +62,7 @@
     out_hbm,
     lane_ref,
     back_ref,
+    order_ref,
     slot_ref,
     kept_ref,
     cand_ref,
@@ -105,6 +106,7 @@
     sends = []
     for s in range(requests):
         r = slot_ref[s]
+        order_ref[s : s + 1, :] = jnp.full((1, LANES), r, jnp.int32)
         pick = jnp.where(lane_ref[pl.ds(r, 1), :] == row_at, 1.0, 0.0).astype(jnp.bfloat16)
         out_ref[s * rows : (s + 1) * rows, :] = dot_f32(pick, cand_ref[r]).astype(jnp.bfloat16)
         part = pl.ds(s * rows, rows)
@@ -123,9 +125,10 @@
             pltpu.HBM((rows, features), jnp.bfloat16),
             jax.ShapeDtypeStruct((requests, shard_len), jnp.int32),
             jax.ShapeDtypeStruct((requests, shard_len), jnp.int32),
+            jax.ShapeDtypeStruct((requests, LANES), jnp.int32),
         ),
         in_specs=[ANY, ANY, ANY],
-        out_specs=(ANY, VMEM, VMEM),
+        out_specs=(ANY, VMEM, VMEM, VMEM),
         scratch_shapes=[
             pltpu.SMEM(slot_request.shape, jnp.int32),
             pltpu.VMEM(kept_index.shape, jnp.int32),
@@ -181,9 +184,9 @@
     pre_bias_ref, gain_ref, gate_bias_ref = rest[3 * narrow_count : 3 * narrow_count + 3]
     rest = rest[3 * narrow_count + 3 :]
     weight_refs = rest[:weight_count]
-    placing_ref, keys_hbm, values_hbm, vectors_ref, gate_offsets_ref, tower_columns_ref = rest[weight_count:][:6]
-    loaded_refs = rest[weight_count + 6 : -4]
-    keys_ref, values_ref, head_sems, sems = rest[-4:]
+    target_ref, keys_ref, values_ref, vectors_ref, gate_offsets_ref, tower_rows_ref = rest[weight_count:][:6]
+    loaded_refs = rest[weight_count + 6 : -1]
+    sems = rest[-1]
     copies = [
         pltpu.make_async_copy(source, loaded, sems.at[i])
         for i, (source, loaded) in enumerate(zip(weight_refs, loaded_refs))
@@ -192,7 +195,7 @@
         copy.start()
     group_size, _, span, head_columns = history_refs[0].shape
     heads_here = bias_refs[0].shape[1]
-    rows, rows_in = placing_ref.shape
+    rows_in = target_ref.shape[1]
     half = rows_in // shards
     me = lax.axis_index("narrow")
     request = slot_ref[lax.axis_index("wide") * group_size + slot_at]
@@ -206,14 +209,13 @@
     offsets = jnp.where(gate_row == gate_lane, offsets.reshape(tasks * experts, experts), 0.0)
     gate_offsets_ref[...] = jnp.broadcast_to(jnp.sum(offsets, axis=1, keepdims=True), gate_offsets_ref.shape)
     tasks_here, tower_width = tower_outer_refs[0].shape
-    column = lax.broadcasted_iota(jnp.int32, (tower_width, LANES), 1)
+    row = lax.broadcasted_iota(jnp.int32, (tasks, tower_width), 0)
     for i in range(narrow_count):
-        outer = jnp.transpose(tower_outer_refs[i][...].astype(jnp.float32))
         for t in range(tasks_here):
             task = lax.rem(me + i, narrow_count) * tasks_here + t
-            tower_columns_ref[i * tasks_here + t] = jnp.where(
-                column == task, outer[:, t : t + 1], 0.0
-            ).astype(jnp.bfloat16)
+            outer = tower_outer_refs[i][t : t + 1, :].astype(jnp.float32)
+            at = (i * tasks_here + t) * tower_width
+            tower_rows_ref[:, at : at + tower_width] = jnp.where(row == task, outer, 0.0).astype(jnp.bfloat16)
 
     kept_row = kept_ref[pl.ds(request, 1), :]
     edge = lax.broadcasted_iota(jnp.int32, (shards, kept_row.shape[1]), 0) * shard_len
@@ -225,9 +227,7 @@
     mine = lane_source == lax.broadcasted_iota(jnp.int32, (shards, rows_in), 0)
     target = jnp.where(mine & (first + lane_within < last), first + lane_within + 1, 0)
     target = jnp.sum(target, axis=0, keepdims=True) - 1
-    placing_ref[...] = jnp.where(
-        target == lax.broadcasted_iota(jnp.int32, (rows, rows_in), 0), 1.0, 0.0
-    ).astype(jnp.bfloat16)
+    target_ref[...] = jnp.broadcast_to(target, target_ref.shape)
 
     head_size = head_columns // heads_here
     tile = 2 * head_size
@@ -246,13 +246,9 @@
                 bias = jnp.where(row == h, masked, bias)
             parts = three_parts(bias)
             keys_ref[at, tile:, :] = jnp.concatenate(
-                [parts, jnp.zeros((tile - parts.shape[0], span), jnp.bfloat16)], axis=0
+                [parts, jnp.zeros((BIAS_ROWS, span), jnp.bfloat16)], axis=0
             )
-            values_ref[at, :, :tile] = history_refs[i][slot_at, 1, :, t * tile : (t + 1) * tile]
-            values_ref[at, :, tile:] = jnp.ones((span, tile), jnp.bfloat16)
-            for j, (source, target) in enumerate([(keys_ref, keys_hbm), (values_ref, values_hbm)]):
-                copies.append(pltpu.make_async_copy(source.at[at], target.at[at], head_sems.at[j, at]))
-                copies[-1].start()
+            values_ref[at] = history_refs[i][slot_at, 1, :, t * tile : (t + 1) * tile]
     for copy in copies:
         copy.wait()
 
@@ -278,27 +274,23 @@
     heads_here = biases[0].shape[1]
     pairs = narrow_count * heads_here // 2
     tile = 2 * head_columns // heads_here
-    rows = kept_index.shape[1] // narrow_count
     tasks, experts = gate_bias.shape
     width = norm_gain.shape[0]
     bf16 = jnp.bfloat16
     return pl.pallas_call(
         functools.partial(prepare_body, narrow_count, len(weights), shards, shard_len, slot_at),
         out_shape=(
-            pltpu.VMEM((rows, shards * half), bf16),
-            pltpu.HBM((pairs, 2 * tile, span), bf16),
-            pltpu.HBM((pairs, span, 2 * tile), bf16),
+            pltpu.VMEM((8, shards * half), jnp.int32),
+            pltpu.VMEM((pairs, tile + 4 * BIAS_ROWS, span), bf16),
+            pltpu.VMEM((pairs, span, tile), bf16),
             pltpu.VMEM((8, width), jnp.float32),
             pltpu.VMEM((tasks * experts, LANES), jnp.float32),
-            pltpu.VMEM((tasks, tower_outer[0].shape[1], LANES), bf16),
+            pltpu.VMEM((tasks, tasks * tower_outer[0].shape[1]), bf16),
             *[pltpu.VMEM(weight.shape, weight.dtype) for weight in weights],
         ),
         in_specs=[SMEM, SMEM] + [VMEM] * (4 + 3 * narrow_count) + [ANY] * len(weights),
-        out_specs=(VMEM, ANY, ANY) + (VMEM,) * (3 + len(weights)),
+        out_specs=(VMEM,) * (6 + len(weights)),
         scratch_shapes=[
-            pltpu.VMEM((pairs, 2 * tile, span), bf16),
-            pltpu.VMEM((pairs, span, 2 * tile), bf16),
-            pltpu.SemaphoreType.DMA((2, pairs)),
             pltpu.SemaphoreType.DMA((len(weights),)),
         ],
         compiler_params=pltpu.CompilerParams(vmem_limit_bytes=VMEM_LIMIT),
@@ -319,11 +311,11 @@
 
 
 def rank_body(narrow_count, pieces, shards, spread, *rest):
-    arrived_hbm, keys_hbm, values_hbm = rest[:3]
-    expert_hbm = rest[3 : 3 + pieces]
-    rest = rest[3 + pieces :]
-    placing_ref, vectors_ref, gate_offsets_ref, tower_columns_ref, inner_ref, outer_ref, query_ref, gate_ref = rest[:8]
-    tower_refs = rest[8 : 8 + narrow_count]
+    expert_hbm = rest[:pieces]
+    tower_hbm = rest[pieces : pieces + narrow_count]
+    rest = rest[pieces + narrow_count :]
+    arrived_ref, target_ref, vectors_ref, gate_offsets_ref, tower_rows_ref, keys_ref, values_ref = rest[:7]
+    inner_ref, outer_ref, query_ref, gate_ref = rest[7:11]
     (
         out_ref,
         embed_ref,
@@ -332,53 +324,45 @@
         expert_out_ref,
         gates_ref,
         mixture_ref,
-        arrived_ref,
-        keys_ref,
-        values_ref,
         expert_refs,
+        tower_refs,
         sems,
-    ) = rest[8 + narrow_count :]
-    arrival = pltpu.make_async_copy(arrived_hbm, arrived_ref, sems.at[0])
-    head_copies = [
-        pltpu.make_async_copy(keys_hbm, keys_ref, sems.at[1]),
-        pltpu.make_async_copy(values_hbm, values_ref, sems.at[2]),
-    ]
-    expert_copies = []
+    ) = rest[11:]
     for i in range(pieces):
         at = sum(piece.shape[0] for piece in expert_hbm[:i])
         here = expert_refs.at[pl.ds(at, expert_hbm[i].shape[0])]
-        expert_copies.append(pltpu.make_async_copy(expert_hbm[i], here, sems.at[3 + i]))
-    for copy in [arrival] + head_copies + expert_copies:
-        copy.start()
+        pltpu.make_async_copy(expert_hbm[i], here, sems.at[0]).start()
+    for i in range(narrow_count):
+        pltpu.make_async_copy(tower_hbm[i], tower_refs.at[i], sems.at[1]).start()
 
     rows = embed_ref.shape[0]
     half = arrived_ref.shape[0] // shards
     experts = expert_refs.shape[0]
     experts_here = experts // narrow_count
-    tasks_here = tower_refs[0].shape[0]
+    tasks_here = tower_refs.shape[1]
     tasks = narrow_count * tasks_here
     block = rows // experts
     blocks = rows // block
     me = lax.axis_index("narrow")
 
-    arrival.wait()
-    packed = dot_f32(placing_ref[...], arrived_ref[...]).astype(jnp.bfloat16)
+    here = lax.broadcasted_iota(jnp.int32, (rows, target_ref.shape[1]), 0)
+    placing = jnp.where(target_ref[0:1, :] == here, 1.0, 0.0).astype(jnp.bfloat16)
+    packed = dot_f32(placing, arrived_ref[...]).astype(jnp.bfloat16)
     hidden = jnp.maximum(dot_f32(packed, inner_ref[...]) + vectors_ref[0:1, :], 0.0).astype(jnp.bfloat16)
     embed = dot_f32(hidden, outer_ref[...]).astype(jnp.bfloat16)
     embed_ref[...] = embed
     queries = dot_f32(embed, query_ref[...]).astype(jnp.bfloat16)
     queries_ref[...] = queries
 
-    tile = keys_ref.shape[1] // 2
+    tile = values_ref.shape[2]
     pairs = keys_ref.shape[0]
     scale = (tile // 2) ** (-0.5)
-    lane = lax.broadcasted_iota(jnp.int32, (rows, tile), 1)
-    left = lane < tile // 2
+    left = lax.broadcasted_iota(jnp.int32, (rows, tile), 1) < tile // 2
+    lane = lax.broadcasted_iota(jnp.int32, (rows, 4 * BIAS_ROWS), 1)
     _, part = split_by(lane, BIAS_ROWS)
     bias_lanes = lane < 3 * BIAS_ROWS
     ones = [jnp.where(bias_lanes & (part == h), 1.0, 0.0).astype(jnp.bfloat16) for h in range(2)]
-    for copy in head_copies:
-        copy.wait()
+    sum_columns = jnp.ones(values_ref.shape[1:], jnp.bfloat16)
     for pair in range(pairs):
         _, place = split_by(me * (pairs // narrow_count) + pair, pairs)
         columns = pl.ds(pl.multiple_of(place * tile, tile), tile)
@@ -387,10 +371,13 @@
         query = jnp.concatenate([jnp.concatenate([query[h], ones[h]], axis=1) for h in range(2)], axis=0)
         scores = dot_f32(query, keys_ref[pair])
         powers = jnp.exp(scores - jnp.max(scores, axis=1, keepdims=True))
-        result = dot_f32(powers.astype(jnp.bfloat16), values_ref[pair])
-        result = result[:, :tile] / result[:, tile:]
-        attended_ref[:, columns] = jnp.where(left, result[:rows], result[rows:]).astype(jnp.bfloat16)
-
+        values = jnp.concatenate([values_ref[pair], sum_columns], axis=1)
+        result = dot_f32(powers.astype(jnp.bfloat16), values)
+        merged = jnp.where(left, result[:rows, :tile], result[rows:, :tile])
+        sums = jnp.where(left, result[:rows, tile:], result[rows:, tile:])
+        attended_ref[:, columns] = (merged / sums).astype(jnp.bfloat16)
+
+    pltpu.make_async_copy(expert_refs, expert_refs, sems.at[0]).wait()
     mixed_in = embed_ref[...].astype(jnp.float32) + attended_ref[...].astype(jnp.float32)
     normed = (
         mixed_in
@@ -404,8 +391,6 @@
     gate_probs = gate_pow / jnp.sum(gate_pow, axis=1, keepdims=True)
     gates = jnp.transpose(gate_probs.reshape(tasks * experts, rows)).astype(jnp.bfloat16)
 
-    for copy in expert_copies:
-        copy.wait()
     for e in range(experts):
         result = jnp.maximum(dot_f32(normed, expert_refs[e]), 0.0).astype(jnp.bfloat16)
         for b in range(blocks):
@@ -429,17 +414,15 @@
         for t in range(tasks):
             mixture_ref[t, b * block : (b + 1) * block, :] = mixture[t * block : (t + 1) * block, :]
 
+    pltpu.make_async_copy(tower_refs, tower_refs, sems.at[1]).wait()
     acts = []
     for i in range(narrow_count):
         for t in range(tasks_here):
             at = i * tasks_here + t
-            acts.append(jnp.maximum(dot_f32(mixture_ref[at], tower_refs[i][t]), 0.0).astype(jnp.bfloat16))
-    columns = tower_columns_ref[...]
-    columns = columns.reshape(columns.shape[0] * columns.shape[1], columns.shape[2])
-    logits = dot_f32(jnp.concatenate(acts, axis=1), columns)
-    by_task = jnp.transpose(logits)[:tasks]
-
-    returned = sum_parts(dot_f32(three_parts(by_task), placing_ref[...]), tasks)
+            acts.append(jnp.maximum(dot_f32(mixture_ref[at], tower_refs[i, t]), 0.0).astype(jnp.bfloat16))
+    by_task = dot_nt(tower_rows_ref[...], jnp.concatenate(acts, axis=1))
+
+    returned = sum_parts(dot_f32(three_parts(by_task), placing), tasks)
     if not spread:
         out_ref[...] = returned
         return
@@ -449,13 +432,13 @@
 
 
 def rank_slot(
-    arrived, placing, keys, values, vectors, gate_offsets, tower_columns, weights, experts, towers, shards, spread
+    arrived, target, keys, values, vectors, gate_offsets, tower_rows, weights, experts, towers, rows, shards, spread
 ):
     inner, outer, query, gate_rows = weights
     narrow_count = len(towers)
-    rows, rows_in = placing.shape
+    rows_in = arrived.shape[0]
     width = outer.shape[1]
-    tasks = tower_columns.shape[0]
+    tasks = tower_rows.shape[0]
     expert_count = gate_rows.shape[0] // tasks
     expert_width = experts[0].shape[2]
     block = rows // expert_count
@@ -465,8 +448,8 @@
         out_shape = jax.ShapeDtypeStruct((tasks, rows_in), jnp.float32)
     bf16 = jnp.bfloat16
     flops = 2 * rows * (rows_in * width + 3 * width * width + 2 * expert_count * width * expert_width)
-    far = [arrived, keys, values, *experts]
-    near = [placing, vectors, gate_offsets, tower_columns, *weights, *towers]
+    far = [*experts, *towers]
+    near = [arrived, target, vectors, gate_offsets, tower_rows, keys, values, *weights]
     return pl.pallas_call(
         functools.partial(rank_body, narrow_count, len(experts), shards, spread),
         out_shape=out_shape,
@@ -479,11 +462,9 @@
             pltpu.VMEM((rows // block, expert_count * block, expert_width), bf16),
             pltpu.VMEM((rows // block, tasks * block, expert_count * block), bf16),
             pltpu.VMEM((tasks, rows, expert_width), bf16),
-            pltpu.VMEM(arrived.shape, bf16),
-            pltpu.VMEM(keys.shape, bf16),
-            pltpu.VMEM(values.shape, bf16),
             pltpu.VMEM((expert_count,) + experts[0].shape[1:], bf16),
-            pltpu.SemaphoreType.DMA((3 + len(experts),)),
+            pltpu.VMEM((narrow_count,) + towers[0].shape, bf16),
+            pltpu.SemaphoreType.DMA((2,)),
         ],
         compiler_params=pltpu.CompilerParams(vmem_limit_bytes=VMEM_LIMIT),
         cost_estimate=pl.CostEstimate(flops=flops, bytes_accessed=6 * 1024 * 1024, transcendentals=0),
@@ -491,31 +472,36 @@
     )(*[in_hbm(array) for array in far], *[in_vmem(array) for array in near])
 
 
-def unpack_body(narrow_count, slot_ref, back_ref, returned_ref, out_ref):
+def unpack_body(narrow_count, order_ref, back_ref, returned_ref, out_ref):
     requests, shard_len = back_ref.shape
     _, tasks, lanes = returned_ref.shape
     row_at = lax.broadcasted_iota(jnp.int32, (narrow_count * lanes, shard_len), 0)
+    request_at = lax.broadcasted_iota(jnp.int32, (requests, shard_len), 0)
+    results = [jnp.zeros((requests, shard_len), jnp.float32) for t in range(tasks)]
     for s in range(requests):
-        r = slot_ref[s]
+        mine = request_at == order_ref[s : s + 1, 0:1]
+        back = jnp.sum(jnp.where(mine, back_ref[...], 0), axis=0, keepdims=True)
         pieces = [returned_ref[s * narrow_count + i] for i in range(narrow_count)]
         parts = three_parts(jnp.concatenate(pieces, axis=1))
-        pick = jnp.where(back_ref[pl.ds(r, 1), :] == row_at, 1.0, 0.0).astype(jnp.bfloat16)
+        pick = jnp.where(back == row_at, 1.0, 0.0).astype(jnp.bfloat16)
         result = sum_parts(dot_f32(parts, pick), tasks)
         for t in range(tasks):
-            out_ref[t, pl.ds(r, 1), :] = result[t : t + 1, :]
-
-
-def unpack_rows(slot_request, back, returned, narrow_count):
+            results[t] = jnp.where(mine, result[t : t + 1, :], results[t])
+    for t in range(tasks):
+        out_ref[t] = results[t]
+
+
+def unpack_rows(order, back, returned, narrow_count):
     requests, shard_len = back.shape
     tasks = returned.shape[1]
     return pl.pallas_call(
         functools.partial(unpack_body, narrow_count),
         out_shape=jax.ShapeDtypeStruct((tasks, requests, shard_len), jnp.float32),
-        in_specs=[SMEM, VMEM, VMEM],
+        in_specs=[VMEM, VMEM, VMEM],
         out_specs=VMEM,
         compiler_params=pltpu.CompilerParams(vmem_limit_bytes=VMEM_LIMIT),
         name="unpack_rows",
-    )(slot_request, back, returned)
+    )(order, back, returned)
 
 
 def lanes_of(kept_index, device_rank, shard_len, narrow_count, half):
@@ -578,7 +564,7 @@
     )
 
     if blocked:
-        packed, lanes, back = pack_rows(slot_request, kept_index, candidates, narrow_count, half)
+        packed, lanes, back, order = pack_rows(slot_request, kept_index, candidates, narrow_count, half)
     else:
         lanes = lanes_of(kept_index, device_rank, shard_len, narrow_count, half)
         picks = lanes[:, None, :] == jnp.arange(narrow_count * half, dtype=jnp.int32)[None, :, None]
@@ -615,7 +601,7 @@
 
     results = []
     for g in range(group_size):
-        placing, keys, values, vectors, gate_offsets, tower_columns, *loaded = prepare(
+        target, keys, values, vectors, gate_offsets, tower_rows, *loaded = prepare(
             slot_request,
             history_length,
             kept_index,
@@ -625,25 +611,26 @@
             pre_bias,
             norm_gain,
             gate_bias,
-            [pre_inner, pre_outer, query_weight, gate_weight.T, tower_inner],
+            [pre_inner, pre_outer, query_weight, gate_weight.T],
             shards,
             shard_len,
             half,
             g,
         )
-        placing, prerank_score = lax.optimization_barrier((placing, prerank_score))
+        target, prerank_score = lax.optimization_barrier((target, prerank_score))
         results.append(
             rank_slot(
                 arrived[g],
-                placing,
+                target,
                 keys,
                 values,
                 vectors,
                 gate_offsets,
-                tower_columns,
-                loaded[:4],
+                tower_rows,
+                loaded,
                 experts,
-                loaded[4:] + towers[1:],
+                towers,
+                kept_count // narrow_count,
                 shards,
                 blocked,
             )
@@ -651,7 +638,7 @@
 
     if blocked:
         returned = lax.all_to_all(results[0], both, split_axis=0, concat_axis=0, tiled=True)
-        return (prerank_score, unpack_rows(slot_request, back, returned, narrow_count))
+        return (prerank_score, unpack_rows(order, back, returned, narrow_count))
     sending = jnp.stack(results).reshape(group_size, tasks, shards, half)
     sending = jnp.transpose(sending, (2, 0, 1, 3)).reshape(shards, -1)
     returned = lax.all_to_all(sending, both, split_axis=0, concat_axis=0, tiled=True)

time: 43.9 us -> 43.3 us (0.986)
  Pallas kernels: 16.1 us -> 14.1 us
  local copies, waits for them, and re-layouts: 0.77 us -> 2.27 us
  waiting for transfers between devices: 5.28 us -> 4.77 us
    unnamed x28 -> x32, local copies, waits for them, and re-layouts: 0.7 us -> 2.2 us
    pallas_call x1, Pallas kernels: 3.31 us -> 1.96 us  [prepare(): pl.pallas_call(functools.partial(prepare_body, narrow_count, len(weights)...]
    all_to_all x1, waiting for transfers between devices: 3.24 us -> 2.37 us  [on_device(): lax.all_to_all(packed, both, split_axis=0, concat_axis=0, tiled=True)]
    pallas_call x1, Pallas kernels: 1.37 us -> 0.93 us  [unpack_rows(): pl.pallas_call(functools.partial(unpack_body, narrow_count), out_shape=ja...]
  transfers between devices with their start and end apart: 7 -> 7, of which waited for: 2 -> 2; matrix products, arithmetic and copies ran while one was open for 0% -> 0% of each run, Pallas kernels for 14% -> 11%
where the time goes in v4:
time: 43.3 us; the launch traced here: 42.9 us
  Pallas kernels  14.1 us (33%)
  blocking collectives  10.8 us (25%)
  starting transfers between devices  9.36 us (22%)
  waiting for transfers between devices  4.77 us (11%)
  local copies, waits for them, and re-layouts  2.27 us (5%)
  between operations  1.55 us (4%)
    all_to_all x1, blocking collectives, on_device(): lax.all_to_all(results[0], both, split_axis=0, concat_axis=0, tiled=True)  10.8 us
    all_to_all x1, starting transfers between devices, on_device(): lax.all_to_all(packed, both, split_axis=0, concat_axis=0, tiled=True)  7.5 us
    pallas_call x1, Pallas kernels, rank_slot(): pl.pallas_call(functools.partial(rank_body, narrow_count, len(experts), s...  5.9 us
    pallas_call x1, Pallas kernels, prerank(): pl.pallas_call(functools.partial(prerank_body, shard_len), out_shape=jax....  2.76 us
    pallas_call x1, Pallas kernels, pack_rows(): pl.pallas_call(functools.partial(pack_body, narrow_count, half), out_shap...  2.59 us
    ppermute x6, waiting for transfers between devices, from_others(): pieces.append(lax.ppermute(values, 'narrow', steps))  2.4 us
    all_to_all x1, waiting for transfers between devices, on_device(): lax.all_to_all(packed, both, split_axis=0, concat_axis=0, tiled=True)  2.37 us
    unnamed x32, local copies, waits for them, and re-layouts  2.2 us
  transfers between devices with their start and end apart: 7, of which 2 were waited for; matrix products, arithmetic and copies ran while one was open for 0% of the time, Pallas kernels for 11%

profile of v4, /device:TPU:0, one launch (start us, length us, event | category | flops | bytes accessed | tf_op | source)
XLA Modules:
  0.0 42.9 jit_solution(8912488096646662921)
XLA Ops:
  0.6 0.0 copy-start.13
  0.6 2.6 %pack_rows.1 = (bf16[512,512]{1,0:T(8,128)(2,1)}, s32[8,128]{1,0:T(8,128)S(1)}, s32[8,128]{1,0:T(8,128)S(1)}, s32[8,128]{1,0:T(8,128)S(1)}) custom-call(s32[8]{0:T(128)} %slot_ref.1, s32[8,512]{1,0:T(8,128)} %kept_ref.1, bf16[8,128,512]{2,1,0:T(8,128)(2,1)} %cand_hbm.1), custom_call_target="tpu_custom_call" | custom-call | flops 67108864 | bytes 1048576 | tf_op jit(solution)/shard_map/pack_rows/pallas_call | solution.py:122
  3.2 0.0 copy-start.3
  3.3 0.0 copy-start.8
  3.3 7.5 %all-to-all-start = ((bf16[16,32,512]{2,1,0:T(8,128)(2,1)}), bf16[16,32,512]{2,1,0:T(8,128)(2,1)S(1)}, u32[]{:S(2)}, u32[]{:S(2)}) async-start(bf16[16,32,512]{2,1,0:T(8,128)(2,1)} %bitcast.11), calls=%async_computation | async-start | bytes 1048576 | tf_op jit(solution)/shard_map/all_to_all | solution.py:576
  10.8 0.0 copy-start.1
  10.8 0.0 copy-start.2
  10.8 0.1 fusion
  10.9 0.5 %collective-permute-start = (bf16[1,2,512,256]{3,2,1,0:T(8,128)(2,1)S(1)}, bf16[1,2,512,256]{3,2,1,0:T(8,128)(2,1)S(1)}, u32[]{:S(2)}, u32[]{:S(2)}) collective-permute-start(bf16[1,2,512,256]{3,2,1,0:T(8,128)(2,1)S(1)} %copy-done.3), channel_id=1, source_target_pairs={{1,0},{0,1},{3,2},{2,3},{5,4},{4,5},{7,6},{6,7},{9,8},{8,9},{11,10... | collective-permute-start | bytes 1572872 | tf_op jit(solution)/shard_map/ppermute | solution.py:520
  11.4 0.1 collective-permute-start.3
  11.5 0.4 collective-permute-start.4
  11.9 0.1 collective-permute-start.5
  12.0 0.4 collective-permute-start.2
  12.4 2.4 %collective-permute-done.2.rest_5_ = bf16[4,128]{1,0:T(4,128)(2,1)S(1)} collective-permute-done((bf16[4,128]{1,0:T(4,128)(2,1)S(1)}, bf16[4,128]{1,0:T(4,128)(2,1)S(1)}, u32[]{:S(2)}, u32[]{:S(2)}) %collective-permute-start.2) | collective-permute-done | bytes 1056 | tf_op jit(solution)/shard_map/ppermute | solution.py:520
  14.8 0.4 collective-permute-start.1
  15.3 2.8 %prerank.1 = f32[8,128]{1,0:T(8,128)} custom-call(bf16[1024,512]{1,0:T(8,128)(2,1)S(1)} %bitcast.6, bf16[512,512]{1,0:T(8,128)(2,1)S(1)} %copy-done.1, f32[1,512]{1,0:T(1,128)S(1)} %bitcast.8, bf16[512,512]{1,0:T(8,128)(2,1)S(1)} %copy-done.2, bf16[8,512]{1,0:T(8,128)(2,1)S(1)} %copy-done.6, s32[8,128]{1,0:T(8,128)S(1)} %get-tuple-element.29.lane_ref), custom_call_target="tpu_custom_call" | custom-call | flops 1 | bytes 1 | tf_op jit(solution)/shard_map/prerank/pallas_call | solution.py:162
  18.8 0.6 %copy-done.11 = s32[8]{0:T(128)S(1)} copy-done((s32[8]{0:T(128)S(1)}, s32[8]{0:T(128)}, u32[]{:S(2)}) %copy-start.11) | copy-done | bytes 56
  19.4 2.0 %prepare.1 = (s32[8,512]{1,0:T(8,128)S(1)}, bf16[4,160,512]{2,1,0:T(8,128)(2,1)S(1)}, bf16[4,512,128]{2,1,0:T(8,128)(2,1)S(1)}, f32[8,512]{1,0:T(8,128)S(1)}, f3...) custom-call(s32[8]{0:T(128)S(1)} %copy-done.11, ...), custom_call_target="tpu_custom_call" | custom-call | flops 1 | bytes 1 | tf_op jit(solution)/shard_map/prepare/pallas_call | solution.py:280
  21.4 0.7 %copy-done.15 = bf16[4,256,128]{2,1,0:T(8,128)(2,1)} copy-done((bf16[4,256,128]{2,1,0:T(8,128)(2,1)}, bf16[4,256,128]{2,1,0:T(8,128)(2,1)S(1)}, u32[]{:S(2)}) %copy-start.15) | copy-done | bytes 262168
  22.1 0.8 %copy-done.14 = bf16[2,512,256]{2,1,0:T(8,128)(2,1)} copy-done((bf16[2,512,256]{2,1,0:T(8,128)(2,1)}, bf16[2,512,256]{2,1,0:T(8,128)(2,1)S(1)}, u32[]{:S(2)}) %copy-start.14) | copy-done | bytes 524312
  22.9 2.4 %all-to-all-done = bf16[16,32,512]{2,1,0:T(8,128)(2,1)S(1)} async-done(((bf16[16,32,512]{2,1,0:T(8,128)(2,1)}), bf16[16,32,512]{2,1,0:T(8,128)(2,1)S(1)}, u32[]{:S(2)}, u32[]{:S(2)}) %all-to-all-start) | async-done | bytes 524320 | tf_op jit(solution)/shard_map/all_to_all | solution.py:576
  25.2 5.9 %rank_slot.1 = f32[16,8,128]{2,1,0:T(8,128)S(1)} custom-call(bf16[4,512,256]{2,1,0:T(8,128)(2,1)} %rest_0_.2, bf16[2,512,256]{2,1,0:T(8,128)(2,1)} %copy-done.14, bf16[2,512,256]{2,1,0:T(8,128)(2,1)} %collective-permute-done.4.rest_2_, bf16[4,256,128]{2,1,0:T(8,128)(2,1)} %rest_3_, bf16[4,256,128]{2,1,0:T(8,128)(2,1)} %copy-done.15, ...), custom_call_target="tpu_custom_call" | custom-call | flops 1610612736 | bytes 6291456 | tf_op jit(solution)/shard_map/rank_slot/pallas_call | solution.py:453
  31.2 10.8 %all_to_all.10.returned_ref = f32[16,8,128]{2,1,0:T(8,128)S(1)} all-to-all(f32[16,8,128]{2,1,0:T(8,128)S(1)} %rank_slot.1), channel_id=1, replica_groups=mesh['groups'=2,'wide'=8,'narrow'=2] {'wide','narrow'}, dimensions={0} | all-to-all | bytes 131072 | tf_op jit(solution)/shard_map/all_to_all | solution.py:640
  42.0 0.9 %unpack_rows.1 = f32[8,8,128]{2,1,0:T(8,128)} custom-call(s32[8,128]{1,0:T(8,128)S(1)} %get-tuple-element.31.order_ref, s32[8,128]{1,0:T(8,128)S(1)} %get-tuple-element.32.back_ref, f32[16,8,128]{2,1,0:T(8,128)S(1)} %all_to_all.10.returned_ref), custom_call_target="tpu_custom_call" | custom-call | tf_op jit(solution)/shard_map/unpack_rows/pallas_call | solution.py:497
  (29 shorter events, 0.1 us)
Async XLA Ops:
  0.6 10.2 %copy-start.13 = (bf16[4,512,256]{2,1,0:T(8,128)(2,1)S(1)}, bf16[4,512,256]{2,1,0:T(8,128)(2,1)}, u32[]{:S(2)}) copy-start(bf16[4,512,256]{2,1,0:T(8,128)(2,1)} %rest_0_.2) | copy-start | bytes 3145732
  3.2 7.7 %copy-start.3 = (bf16[1,2,512,256]{3,2,1,0:T(8,128)(2,1)S(1)}, bf16[1,2,512,256]{3,2,1,0:T(8,128)(2,1)}, u32[]{:S(2)}) copy-start(bf16[1,2,512,256]{3,2,1,0:T(8,128)(2,1)} %rest_0_.1) | copy-start | bytes 1572868
  3.2 11.6 %copy-start.7 = (f32[1,4,512]{2,1,0:T(4,128)S(1)}, f32[1,4,512]{2,1,0:T(4,128)}, u32[]{:S(2)}) copy-start(f32[1,4,512]{2,1,0:T(4,128)} %rest_2_) | copy-start | bytes 24580
  3.3 11.9 %copy-start.8 = (f32[512]{0:T(512)S(1)}, f32[512]{0:T(512)}, u32[]{:S(2)}) copy-start(f32[512]{0:T(512)} %param.19) | copy-start | bytes 6148
  3.3 22.0 %all-to-all-start = ((bf16[16,32,512]{2,1,0:T(8,128)(2,1)}), bf16[16,32,512]{2,1,0:T(8,128)(2,1)S(1)}, u32[]{:S(2)}, u32[]{:S(2)}) async-start(bf16[16,32,512]{2,1,0:T(8,128)(2,1)} %bitcast.11), calls=%async_computation | async-start | bytes 1048576 | tf_op jit(solution)/shard_map/all_to_all | solution.py:576
  10.8 1.2 %copy-start.12 = (bf16[4,128]{1,0:T(4,128)(2,1)S(1)}, bf16[4,128]{1,0:T(4,128)(2,1)}, u32[]{:S(2)}) copy-start(bf16[4,128]{1,0:T(4,128)(2,1)} %rest_4_) | copy-start | bytes 3076
  10.8 4.4 %copy-start = (bf16[8,128,512]{2,1,0:T(8,128)(2,1)S(1)}, bf16[8,128,512]{2,1,0:T(8,128)(2,1)}, u32[]{:S(2)}) copy-start(bf16[8,128,512]{2,1,0:T(8,128)(2,1)} %cand_hbm.1) | copy-start | bytes 3145732
  10.8 4.4 %copy-start.1 = (bf16[512,512]{1,0:T(8,128)(2,1)S(1)}, bf16[512,512]{1,0:T(8,128)(2,1)}, u32[]{:S(2)}) copy-start(bf16[512,512]{1,0:T(8,128)(2,1)} %inner_ref.1) | copy-start | bytes 1572868
  10.8 4.4 %copy-start.2 = (bf16[512,512]{1,0:T(8,128)(2,1)S(1)}, bf16[512,512]{1,0:T(8,128)(2,1)}, u32[]{:S(2)}) copy-start(bf16[512,512]{1,0:T(8,128)(2,1)} %outer_ref.1) | copy-start | bytes 1572868
  10.9 4.3 %copy-start.6 = (bf16[8,512]{1,0:T(8,128)(2,1)S(1)}, bf16[8,512]{1,0:T(8,128)(2,1)}, u32[]{:S(2)}) copy-start(bf16[8,512]{1,0:T(8,128)(2,1)} %user_ref.1) | copy-start | bytes 24580
  10.9 7.8 %collective-permute-start = (bf16[1,2,512,256]{3,2,1,0:T(8,128)(2,1)S(1)}, bf16[1,2,512,256]{3,2,1,0:T(8,128)(2,1)S(1)}, u32[]{:S(2)}, u32[]{:S(2)}) collective-permute-start(bf16[1,2,512,256]{3,2,1,0:T(8,128)(2,1)S(1)} %copy-done.3), channel_id=1, source_target_pairs={{1,0},{0,1},{3,2},{2,3},{5,4},{4,5},{7,6},{6,7},{9,8},{8,9},{11,10... | collective-permute-start | bytes 1572872 | tf_op jit(solution)/shard_map/ppermute | solution.py:520
  11.4 10.0 %collective-permute-start.3 = (bf16[2,512,256]{2,1,0:T(8,128)(2,1)S(1)}, bf16[2,512,256]{2,1,0:T(8,128)(2,1)S(1)}, u32[]{:S(2)}, u32[]{:S(2)}) collective-permute-start(bf16[2,512,256]{2,1,0:T(8,128)(2,1)S(1)} %get-tuple-element.33), channel_id=1, source_target_pairs={{1,0},{0,1},{3,2},{2,3},{5,4},{4,5},{7,6},{6,7},{9,8},{8,9},{11,10... | collective-permute-start | bytes 1572872 | tf_op jit(solution)/shard_map/ppermute | solution.py:520
  11.5 11.4 %collective-permute-start.4 = (bf16[2,512,256]{2,1,0:T(8,128)(2,1)S(1)}, bf16[2,512,256]{2,1,0:T(8,128)(2,1)}, u32[]{:S(2)}, u32[]{:S(2)}) collective-permute-start(bf16[2,512,256]{2,1,0:T(8,128)(2,1)S(1)} %get-tuple-element.34), channel_id=1, source_target_pairs={{1,0},{0,1},{3,2},{2,3},{5,4},{4,5},{7,6},{6,7},{9,8},{8,9},{11,10... | collective-permute-start | bytes 1572872 | tf_op jit(solution)/shard_map/ppermute | solution.py:520
  11.9 9.4 %collective-permute-start.5 = (bf16[4,256,128]{2,1,0:T(8,128)(2,1)}, bf16[4,256,128]{2,1,0:T(8,128)(2,1)S(1)}, u32[]{:S(2)}, u32[]{:S(2)}) collective-permute-start(bf16[4,256,128]{2,1,0:T(8,128)(2,1)} %rest_3_), channel_id=1, source_target_pairs={{1,0},{0,1},{3,2},{2,3},{5,4},{4,5},{7,6},{6,7},{9,8},{8,9},{11,10... | collective-permute-start | bytes 786440 | tf_op jit(solution)/shard_map/ppermute | solution.py:520
  12.0 2.8 %collective-permute-start.2 = (bf16[4,128]{1,0:T(4,128)(2,1)S(1)}, bf16[4,128]{1,0:T(4,128)(2,1)S(1)}, u32[]{:S(2)}, u32[]{:S(2)}) collective-permute-start(bf16[4,128]{1,0:T(4,128)(2,1)S(1)} %copy-done.12), channel_id=1, source_target_pairs={{1,0},{0,1},{3,2},{2,3},{5,4},{4,5},{7,6},{6,7},{9,8},{8,9},{11,10... | collective-permute-start | bytes 3080 | tf_op jit(solution)/shard_map/ppermute | solution.py:520
  14.8 3.9 %collective-permute-start.1 = (f32[1,4,512]{2,1,0:T(4,128)S(1)}, f32[1,4,512]{2,1,0:T(4,128)S(1)}, u32[]{:S(2)}, u32[]{:S(2)}) collective-permute-start(f32[1,4,512]{2,1,0:T(4,128)S(1)} %copy-done.7), channel_id=1, source_target_pairs={{1,0},{0,1},{3,2},{2,3},{5,4},{4,5},{7,6},{6,7},{9,8},{8,9},{11,10... | collective-permute-start | bytes 24584 | tf_op jit(solution)/shard_map/ppermute | solution.py:520
  15.2 3.5 %copy-start.4 = (bf16[1,2,512,256]{3,2,1,0:T(8,128)(2,1)S(1)}, bf16[1,2,512,256]{3,2,1,0:T(8,128)(2,1)}, u32[]{:S(2)}) copy-start(bf16[1,2,512,256]{3,2,1,0:T(8,128)(2,1)} %rest_0_.1) | copy-start | bytes 1572868
  15.2 3.5 %copy-start.5 = (s32[8,512]{1,0:T(8,128)S(1)}, s32[8,512]{1,0:T(8,128)}, u32[]{:S(2)}) copy-start(s32[8,512]{1,0:T(8,128)} %kept_ref.1) | copy-start | bytes 49156
  15.2 3.5 %copy-start.10 = (f32[512]{0:T(512)S(1)}, f32[512]{0:T(512)}, u32[]{:S(2)}) copy-start(f32[512]{0:T(512)} %param.28) | copy-start | bytes 6148
  18.0 0.7 %copy-start.9 = (f32[8,8]{1,0:T(8,128)S(1)}, f32[8,8]{1,0:T(8,128)}, u32[]{:S(2)}) copy-start(f32[8,8]{1,0:T(8,128)} %rest_8_.1) | copy-start | bytes 772
  18.7 0.7 %copy-start.11 = (s32[8]{0:T(128)S(1)}, s32[8]{0:T(128)}, u32[]{:S(2)}) copy-start(s32[8]{0:T(128)} %slot_ref.1) | copy-start | bytes 100
  21.3 0.7 %copy-start.15 = (bf16[4,256,128]{2,1,0:T(8,128)(2,1)}, bf16[4,256,128]{2,1,0:T(8,128)(2,1)S(1)}, u32[]{:S(2)}) copy-start(bf16[4,256,128]{2,1,0:T(8,128)(2,1)S(1)} %collective-permute-done.5.rest_4_) | copy-start | bytes 786436
  22.1 0.8 %copy-start.14 = (bf16[2,512,256]{2,1,0:T(8,128)(2,1)}, bf16[2,512,256]{2,1,0:T(8,128)(2,1)S(1)}, u32[]{:S(2)}) copy-start(bf16[2,512,256]{2,1,0:T(8,128)(2,1)S(1)} %collective-permute-done.3.rest_1_) | copy-start | bytes 1572868

commit v5 on v4

--- a/solution.py
+++ b/solution.py
@@ -103,17 +103,20 @@
     row_at = lax.broadcasted_iota(jnp.int32, (rows, shard_len), 0)
     slot_copy.wait()
     cand_copy.wait()
-    sends = []
-    for s in range(requests):
-        r = slot_ref[s]
-        order_ref[s : s + 1, :] = jnp.full((1, LANES), r, jnp.int32)
-        pick = jnp.where(lane_ref[pl.ds(r, 1), :] == row_at, 1.0, 0.0).astype(jnp.bfloat16)
-        out_ref[s * rows : (s + 1) * rows, :] = dot_f32(pick, cand_ref[r]).astype(jnp.bfloat16)
-        part = pl.ds(s * rows, rows)
-        sends.append(pltpu.make_async_copy(out_ref.at[part], out_hbm.at[part], sems.at[3 + s]))
-        sends[s].start()
-    for send in sends:
-        send.wait()
+    zeros = jnp.zeros((rows, shard_len), jnp.bfloat16)
+    for s in range(0, requests, 2):
+        picks, blocks = [], []
+        for i in range(2):
+            r = slot_ref[s + i]
+            order_ref[s + i : s + i + 1, :] = jnp.full((1, LANES), r, jnp.int32)
+            pick = jnp.where(lane_ref[pl.ds(r, 1), :] == row_at, 1.0, 0.0).astype(jnp.bfloat16)
+            picks.append(jnp.concatenate([pick, zeros] if i == 0 else [zeros, pick], axis=1))
+            blocks.append(cand_ref[r])
+        both = dot_f32(jnp.concatenate(picks, axis=0), jnp.concatenate(blocks, axis=0))
+        part = pl.ds(s * rows, 2 * rows)
+        out_ref[part, :] = both.astype(jnp.bfloat16)
+        pltpu.make_async_copy(out_ref.at[part], out_hbm.at[part], sems.at[3]).start()
+    pltpu.make_async_copy(out_ref, out_hbm, sems.at[3]).wait()
 
 
 def pack_rows(slot_request, kept_index, candidates, narrow_count, half):
@@ -134,7 +137,7 @@
             pltpu.VMEM(kept_index.shape, jnp.int32),
             pltpu.VMEM((requests, shard_len, features), jnp.bfloat16),
             pltpu.VMEM((rows, features), jnp.bfloat16),
-            pltpu.SemaphoreType.DMA((3 + requests,)),
+            pltpu.SemaphoreType.DMA((4,)),
         ],
         compiler_params=pltpu.CompilerParams(vmem_limit_bytes=VMEM_LIMIT),
         cost_estimate=pl.CostEstimate(
@@ -328,12 +331,18 @@
         tower_refs,
         sems,
     ) = rest[11:]
-    for i in range(pieces):
+    own = expert_hbm[0].shape[0]
+    own_copy = pltpu.make_async_copy(expert_hbm[0], expert_refs.at[pl.ds(0, own)], sems.at[0])
+    own_copy.start()
+    late_copies = []
+    for i in range(1, pieces):
         at = sum(piece.shape[0] for piece in expert_hbm[:i])
         here = expert_refs.at[pl.ds(at, expert_hbm[i].shape[0])]
-        pltpu.make_async_copy(expert_hbm[i], here, sems.at[0]).start()
+        late_copies.append(pltpu.make_async_copy(expert_hbm[i], here, sems.at[1]))
     for i in range(narrow_count):
-        pltpu.make_async_copy(tower_hbm[i], tower_refs.at[i], sems.at[1]).start()
+        late_copies.append(pltpu.make_async_copy(tower_hbm[i], tower_refs.at[i], sems.at[2]))
+    for copy in late_copies:
+        copy.start()
 
     rows = embed_ref.shape[0]
     half = arrived_ref.shape[0] // shards
@@ -364,6 +373,8 @@
     ones = [jnp.where(bias_lanes & (part == h), 1.0, 0.0).astype(jnp.bfloat16) for h in range(2)]
     sum_columns = jnp.ones(values_ref.shape[1:], jnp.bfloat16)
     for pair in range(pairs):
+        if pair == pairs - 1:
+            own_copy.wait()
         _, place = split_by(me * (pairs // narrow_count) + pair, pairs)
         columns = pl.ds(pl.multiple_of(place * tile, tile), tile)
         scaled = queries_ref[:, columns].astype(jnp.float32) * scale
@@ -377,7 +388,6 @@
         sums = jnp.where(left, result[:rows, tile:], result[rows:, tile:])
         attended_ref[:, columns] = (merged / sums).astype(jnp.bfloat16)
 
-    pltpu.make_async_copy(expert_refs, expert_refs, sems.at[0]).wait()
     mixed_in = embed_ref[...].astype(jnp.float32) + attended_ref[...].astype(jnp.float32)
     normed = (
         mixed_in
@@ -392,6 +402,10 @@
     gates = jnp.transpose(gate_probs.reshape(tasks * experts, rows)).astype(jnp.bfloat16)
 
     for e in range(experts):
+        if e == own:
+            here = expert_refs.at[pl.ds(own, experts - own)]
+            pltpu.make_async_copy(here, here, sems.at[1]).wait()
+            pltpu.make_async_copy(tower_refs, tower_refs, sems.at[2]).wait()
         result = jnp.maximum(dot_f32(normed, expert_refs[e]), 0.0).astype(jnp.bfloat16)
         for b in range(blocks):
             expert_out_ref[b, e * block : (e + 1) * block, :] = result[b * block : (b + 1) * block, :]
@@ -414,7 +428,6 @@
         for t in range(tasks):
             mixture_ref[t, b * block : (b + 1) * block, :] = mixture[t * block : (t + 1) * block, :]
 
-    pltpu.make_async_copy(tower_refs, tower_refs, sems.at[1]).wait()
     acts = []
     for i in range(narrow_count):
         for t in range(tasks_here):
@@ -464,7 +477,7 @@
             pltpu.VMEM((tasks, rows, expert_width), bf16),
             pltpu.VMEM((expert_count,) + experts[0].shape[1:], bf16),
             pltpu.VMEM((narrow_count,) + towers[0].shape, bf16),
-            pltpu.SemaphoreType.DMA((2,)),
+            pltpu.SemaphoreType.DMA((3,)),
         ],
         compiler_params=pltpu.CompilerParams(vmem_limit_bytes=VMEM_LIMIT),
         cost_estimate=pl.CostEstimate(flops=flops, bytes_accessed=6 * 1024 * 1024, transcendentals=0),

time: 43.3 us -> 42.8 us (0.988)
    pallas_call x1, Pallas kernels: 5.9 us -> 5.46 us  [rank_slot(): pl.pallas_call(functools.partial(rank_body, narrow_count, len(experts), s...]
where the time goes in v5:
time: 42.8 us; the launch traced here: 42.5 us
  Pallas kernels  13.7 us (32%)
  blocking collectives  10.8 us (25%)
  starting transfers between devices  9.36 us (22%)
  waiting for transfers between devices  4.78 us (11%)
  local copies, waits for them, and re-layouts  2.27 us (5%)
  between operations  1.55 us (4%)
    all_to_all x1, blocking collectives, on_device(): lax.all_to_all(results[0], both, split_axis=0, concat_axis=0, tiled=True)  10.8 us
    all_to_all x1, starting transfers between devices, on_device(): lax.all_to_all(packed, both, split_axis=0, concat_axis=0, tiled=True)  7.5 us
    pallas_call x1, Pallas kernels, rank_slot(): pl.pallas_call(functools.partial(rank_body, narrow_count, len(experts), s...  5.46 us
    pallas_call x1, Pallas kernels, prerank(): pl.pallas_call(functools.partial(prerank_body, shard_len), out_shape=jax....  2.76 us
    pallas_call x1, Pallas kernels, pack_rows(): pl.pallas_call(functools.partial(pack_body, narrow_count, half), out_shap...  2.6 us
    ppermute x6, waiting for transfers between devices, from_others(): pieces.append(lax.ppermute(values, 'narrow', steps))  2.4 us
    all_to_all x1, waiting for transfers between devices, on_device(): lax.all_to_all(packed, both, split_axis=0, concat_axis=0, tiled=True)  2.37 us
    unnamed x32, local copies, waits for them, and re-layouts  2.2 us
  transfers between devices with their start and end apart: 7, of which 2 were waited for; matrix products, arithmetic and copies ran while one was open for 0% of the time, Pallas kernels for 11%

profile of v5, /device:TPU:0, one launch (start us, length us, event | category | flops | bytes accessed | tf_op | source)
XLA Modules:
  0.0 42.5 jit_solution(5442526462053388235)
XLA Ops:
  0.6 0.0 copy-start.13
  0.6 2.6 %pack_rows.1 = (bf16[512,512]{1,0:T(8,128)(2,1)}, s32[8,128]{1,0:T(8,128)S(1)}, s32[8,128]{1,0:T(8,128)S(1)}, s32[8,128]{1,0:T(8,128)S(1)}) custom-call(s32[8]{0:T(128)} %slot_ref.1, s32[8,512]{1,0:T(8,128)} %kept_ref.1, bf16[8,128,512]{2,1,0:T(8,128)(2,1)} %cand_hbm.1), custom_call_target="tpu_custom_call" | custom-call | flops 67108864 | bytes 1048576 | tf_op jit(solution)/shard_map/pack_rows/pallas_call | solution.py:125
  3.2 0.0 copy-start.3
  3.3 0.0 copy-start.7
  3.3 7.5 %all-to-all-start = ((bf16[16,32,512]{2,1,0:T(8,128)(2,1)}), bf16[16,32,512]{2,1,0:T(8,128)(2,1)S(1)}, u32[]{:S(2)}, u32[]{:S(2)}) async-start(bf16[16,32,512]{2,1,0:T(8,128)(2,1)} %bitcast.11), calls=%async_computation | async-start | bytes 1048576 | tf_op jit(solution)/shard_map/all_to_all | solution.py:589
  10.8 0.0 copy-start.12
  10.8 0.0 copy-start.2
  10.9 0.1 fusion
  11.0 0.5 %collective-permute-start = (bf16[1,2,512,256]{3,2,1,0:T(8,128)(2,1)S(1)}, bf16[1,2,512,256]{3,2,1,0:T(8,128)(2,1)S(1)}, u32[]{:S(2)}, u32[]{:S(2)}) collective-permute-start(bf16[1,2,512,256]{3,2,1,0:T(8,128)(2,1)S(1)} %copy-done.3), channel_id=1, source_target_pairs={{1,0},{0,1},{3,2},{2,3},{5,4},{4,5},{7,6},{6,7},{9,8},{8,9},{11,10... | collective-permute-start | bytes 1572872 | tf_op jit(solution)/shard_map/ppermute | solution.py:533
  11.4 0.1 collective-permute-start.3
  11.5 0.4 collective-permute-start.4
  11.9 0.1 collective-permute-start.5
  12.0 0.4 collective-permute-start.2
  12.4 2.4 %collective-permute-done.2.rest_5_ = bf16[4,128]{1,0:T(4,128)(2,1)S(1)} collective-permute-done((bf16[4,128]{1,0:T(4,128)(2,1)S(1)}, bf16[4,128]{1,0:T(4,128)(2,1)S(1)}, u32[]{:S(2)}, u32[]{:S(2)}) %collective-permute-start.2) | collective-permute-done | bytes 1056 | tf_op jit(solution)/shard_map/ppermute | solution.py:533
  14.8 0.4 collective-permute-start.1
  15.3 2.8 %prerank.1 = f32[8,128]{1,0:T(8,128)} custom-call(bf16[1024,512]{1,0:T(8,128)(2,1)S(1)} %bitcast.6, bf16[512,512]{1,0:T(8,128)(2,1)S(1)} %copy-done.1, f32[1,512]{1,0:T(1,128)S(1)} %bitcast.8, bf16[512,512]{1,0:T(8,128)(2,1)S(1)} %copy-done.2, bf16[8,512]{1,0:T(8,128)(2,1)S(1)} %copy-done.6, s32[8,128]{1,0:T(8,128)S(1)} %get-tuple-element.29.lane_ref), custom_call_target="tpu_custom_call" | custom-call | flops 1 | bytes 1 | tf_op jit(solution)/shard_map/prerank/pallas_call | solution.py:165
  18.8 0.6 %copy-done.11 = s32[8]{0:T(128)S(1)} copy-done((s32[8]{0:T(128)S(1)}, s32[8]{0:T(128)}, u32[]{:S(2)}) %copy-start.11) | copy-done | bytes 56
  19.4 2.0 %prepare.1 = (s32[8,512]{1,0:T(8,128)S(1)}, bf16[4,160,512]{2,1,0:T(8,128)(2,1)S(1)}, bf16[4,512,128]{2,1,0:T(8,128)(2,1)S(1)}, f32[8,512]{1,0:T(8,128)S(1)}, f3...) custom-call(s32[8]{0:T(128)S(1)} %copy-done.11, ...), custom_call_target="tpu_custom_call" | custom-call | flops 1 | bytes 1 | tf_op jit(solution)/shard_map/prepare/pallas_call | solution.py:283
  21.4 0.7 %copy-done.15 = bf16[4,256,128]{2,1,0:T(8,128)(2,1)} copy-done((bf16[4,256,128]{2,1,0:T(8,128)(2,1)}, bf16[4,256,128]{2,1,0:T(8,128)(2,1)S(1)}, u32[]{:S(2)}) %copy-start.15) | copy-done | bytes 262168
  22.1 0.8 %copy-done.14 = bf16[2,512,256]{2,1,0:T(8,128)(2,1)} copy-done((bf16[2,512,256]{2,1,0:T(8,128)(2,1)}, bf16[2,512,256]{2,1,0:T(8,128)(2,1)S(1)}, u32[]{:S(2)}) %copy-start.14) | copy-done | bytes 524312
  22.9 2.4 %all-to-all-done = bf16[16,32,512]{2,1,0:T(8,128)(2,1)S(1)} async-done(((bf16[16,32,512]{2,1,0:T(8,128)(2,1)}), bf16[16,32,512]{2,1,0:T(8,128)(2,1)S(1)}, u32[]{:S(2)}, u32[]{:S(2)}) %all-to-all-start) | async-done | bytes 524320 | tf_op jit(solution)/shard_map/all_to_all | solution.py:589
  25.3 5.5 %rank_slot.1 = f32[16,8,128]{2,1,0:T(8,128)S(1)} custom-call(bf16[4,512,256]{2,1,0:T(8,128)(2,1)} %rest_0_.2, bf16[2,512,256]{2,1,0:T(8,128)(2,1)} %copy-done.14, bf16[2,512,256]{2,1,0:T(8,128)(2,1)} %collective-permute-done.4.rest_2_, bf16[4,256,128]{2,1,0:T(8,128)(2,1)} %rest_3_, bf16[4,256,128]{2,1,0:T(8,128)(2,1)} %copy-done.15, ...), custom_call_target="tpu_custom_call" | custom-call | flops 1610612736 | bytes 6291456 | tf_op jit(solution)/shard_map/rank_slot/pallas_call | solution.py:466
  30.7 10.8 %all_to_all.10.returned_ref = f32[16,8,128]{2,1,0:T(8,128)S(1)} all-to-all(f32[16,8,128]{2,1,0:T(8,128)S(1)} %rank_slot.1), channel_id=1, replica_groups=mesh['groups'=2,'wide'=8,'narrow'=2] {'wide','narrow'}, dimensions={0} | all-to-all | bytes 131072 | tf_op jit(solution)/shard_map/all_to_all | solution.py:653
  41.5 0.9 %unpack_rows.1 = f32[8,8,128]{2,1,0:T(8,128)} custom-call(s32[8,128]{1,0:T(8,128)S(1)} %get-tuple-element.31.order_ref, s32[8,128]{1,0:T(8,128)S(1)} %get-tuple-element.32.back_ref, f32[16,8,128]{2,1,0:T(8,128)S(1)} %all_to_all.10.returned_ref), custom_call_target="tpu_custom_call" | custom-call | tf_op jit(solution)/shard_map/unpack_rows/pallas_call | solution.py:510
  (29 shorter events, 0.1 us)
Async XLA Ops:
  0.6 10.2 %copy-start.13 = (bf16[4,512,256]{2,1,0:T(8,128)(2,1)S(1)}, bf16[4,512,256]{2,1,0:T(8,128)(2,1)}, u32[]{:S(2)}) copy-start(bf16[4,512,256]{2,1,0:T(8,128)(2,1)} %rest_0_.2) | copy-start | bytes 3145732
  3.2 7.7 %copy-start.3 = (bf16[1,2,512,256]{3,2,1,0:T(8,128)(2,1)S(1)}, bf16[1,2,512,256]{3,2,1,0:T(8,128)(2,1)}, u32[]{:S(2)}) copy-start(bf16[1,2,512,256]{3,2,1,0:T(8,128)(2,1)} %rest_0_.1) | copy-start | bytes 1572868
  3.3 11.6 %copy-start.7 = (f32[1,4,512]{2,1,0:T(4,128)S(1)}, f32[1,4,512]{2,1,0:T(4,128)}, u32[]{:S(2)}) copy-start(f32[1,4,512]{2,1,0:T(4,128)} %rest_2_) | copy-start | bytes 24580
  3.3 11.9 %copy-start.8 = (f32[512]{0:T(512)S(1)}, f32[512]{0:T(512)}, u32[]{:S(2)}) copy-start(f32[512]{0:T(512)} %param.19) | copy-start | bytes 6148
  3.3 22.0 %all-to-all-start = ((bf16[16,32,512]{2,1,0:T(8,128)(2,1)}), bf16[16,32,512]{2,1,0:T(8,128)(2,1)S(1)}, u32[]{:S(2)}, u32[]{:S(2)}) async-start(bf16[16,32,512]{2,1,0:T(8,128)(2,1)} %bitcast.11), calls=%async_computation | async-start | bytes 1048576 | tf_op jit(solution)/shard_map/all_to_all | solution.py:589
  10.8 1.2 %copy-start.12 = (bf16[4,128]{1,0:T(4,128)(2,1)S(1)}, bf16[4,128]{1,0:T(4,128)(2,1)}, u32[]{:S(2)}) copy-start(bf16[4,128]{1,0:T(4,128)(2,1)} %rest_4_) | copy-start | bytes 3076
  10.8 4.4 %copy-start = (bf16[8,128,512]{2,1,0:T(8,128)(2,1)S(1)}, bf16[8,128,512]{2,1,0:T(8,128)(2,1)}, u32[]{:S(2)}) copy-start(bf16[8,128,512]{2,1,0:T(8,128)(2,1)} %cand_hbm.1) | copy-start | bytes 3145732
  10.8 4.4 %copy-start.1 = (bf16[512,512]{1,0:T(8,128)(2,1)S(1)}, bf16[512,512]{1,0:T(8,128)(2,1)}, u32[]{:S(2)}) copy-start(bf16[512,512]{1,0:T(8,128)(2,1)} %inner_ref.1) | copy-start | bytes 1572868
  10.8 4.4 %copy-start.2 = (bf16[512,512]{1,0:T(8,128)(2,1)S(1)}, bf16[512,512]{1,0:T(8,128)(2,1)}, u32[]{:S(2)}) copy-start(bf16[512,512]{1,0:T(8,128)(2,1)} %outer_ref.1) | copy-start | bytes 1572868
  10.9 4.3 %copy-start.6 = (bf16[8,512]{1,0:T(8,128)(2,1)S(1)}, bf16[8,512]{1,0:T(8,128)(2,1)}, u32[]{:S(2)}) copy-start(bf16[8,512]{1,0:T(8,128)(2,1)} %user_ref.1) | copy-start | bytes 24580
  11.0 7.8 %collective-permute-start = (bf16[1,2,512,256]{3,2,1,0:T(8,128)(2,1)S(1)}, bf16[1,2,512,256]{3,2,1,0:T(8,128)(2,1)S(1)}, u32[]{:S(2)}, u32[]{:S(2)}) collective-permute-start(bf16[1,2,512,256]{3,2,1,0:T(8,128)(2,1)S(1)} %copy-done.3), channel_id=1, source_target_pairs={{1,0},{0,1},{3,2},{2,3},{5,4},{4,5},{7,6},{6,7},{9,8},{8,9},{11,10... | collective-permute-start | bytes 1572872 | tf_op jit(solution)/shard_map/ppermute | solution.py:533
  11.4 9.9 %collective-permute-start.3 = (bf16[2,512,256]{2,1,0:T(8,128)(2,1)S(1)}, bf16[2,512,256]{2,1,0:T(8,128)(2,1)S(1)}, u32[]{:S(2)}, u32[]{:S(2)}) collective-permute-start(bf16[2,512,256]{2,1,0:T(8,128)(2,1)S(1)} %get-tuple-element.33), channel_id=1, source_target_pairs={{1,0},{0,1},{3,2},{2,3},{5,4},{4,5},{7,6},{6,7},{9,8},{8,9},{11,10... | collective-permute-start | bytes 1572872 | tf_op jit(solution)/shard_map/ppermute | solution.py:533
  11.5 11.4 %collective-permute-start.4 = (bf16[2,512,256]{2,1,0:T(8,128)(2,1)S(1)}, bf16[2,512,256]{2,1,0:T(8,128)(2,1)}, u32[]{:S(2)}, u32[]{:S(2)}) collective-permute-start(bf16[2,512,256]{2,1,0:T(8,128)(2,1)S(1)} %get-tuple-element.34), channel_id=1, source_target_pairs={{1,0},{0,1},{3,2},{2,3},{5,4},{4,5},{7,6},{6,7},{9,8},{8,9},{11,10... | collective-permute-start | bytes 1572872 | tf_op jit(solution)/shard_map/ppermute | solution.py:533
  11.9 9.4 %collective-permute-start.5 = (bf16[4,256,128]{2,1,0:T(8,128)(2,1)}, bf16[4,256,128]{2,1,0:T(8,128)(2,1)S(1)}, u32[]{:S(2)}, u32[]{:S(2)}) collective-permute-start(bf16[4,256,128]{2,1,0:T(8,128)(2,1)} %rest_3_), channel_id=1, source_target_pairs={{1,0},{0,1},{3,2},{2,3},{5,4},{4,5},{7,6},{6,7},{9,8},{8,9},{11,10... | collective-permute-start | bytes 786440 | tf_op jit(solution)/shard_map/ppermute | solution.py:533
  12.0 2.8 %collective-permute-start.2 = (bf16[4,128]{1,0:T(4,128)(2,1)S(1)}, bf16[4,128]{1,0:T(4,128)(2,1)S(1)}, u32[]{:S(2)}, u32[]{:S(2)}) collective-permute-start(bf16[4,128]{1,0:T(4,128)(2,1)S(1)} %copy-done.12), channel_id=1, source_target_pairs={{1,0},{0,1},{3,2},{2,3},{5,4},{4,5},{7,6},{6,7},{9,8},{8,9},{11,10... | collective-permute-start | bytes 3080 | tf_op jit(solution)/shard_map/ppermute | solution.py:533
  14.8 3.9 %collective-permute-start.1 = (f32[1,4,512]{2,1,0:T(4,128)S(1)}, f32[1,4,512]{2,1,0:T(4,128)S(1)}, u32[]{:S(2)}, u32[]{:S(2)}) collective-permute-start(f32[1,4,512]{2,1,0:T(4,128)S(1)} %copy-done.7), channel_id=1, source_target_pairs={{1,0},{0,1},{3,2},{2,3},{5,4},{4,5},{7,6},{6,7},{9,8},{8,9},{11,10... | collective-permute-start | bytes 24584 | tf_op jit(solution)/shard_map/ppermute | solution.py:533
  15.2 3.5 %copy-start.4 = (bf16[1,2,512,256]{3,2,1,0:T(8,128)(2,1)S(1)}, bf16[1,2,512,256]{3,2,1,0:T(8,128)(2,1)}, u32[]{:S(2)}) copy-start(bf16[1,2,512,256]{3,2,1,0:T(8,128)(2,1)} %rest_0_.1) | copy-start | bytes 1572868
  15.2 3.5 %copy-start.5 = (s32[8,512]{1,0:T(8,128)S(1)}, s32[8,512]{1,0:T(8,128)}, u32[]{:S(2)}) copy-start(s32[8,512]{1,0:T(8,128)} %kept_ref.1) | copy-start | bytes 49156
  15.3 3.5 %copy-start.10 = (f32[512]{0:T(512)S(1)}, f32[512]{0:T(512)}, u32[]{:S(2)}) copy-start(f32[512]{0:T(512)} %param.28) | copy-start | bytes 6148
  18.0 0.7 %copy-start.9 = (f32[8,8]{1,0:T(8,128)S(1)}, f32[8,8]{1,0:T(8,128)}, u32[]{:S(2)}) copy-start(f32[8,8]{1,0:T(8,128)} %rest_8_.1) | copy-start | bytes 772
  18.7 0.7 %copy-start.11 = (s32[8]{0:T(128)S(1)}, s32[8]{0:T(128)}, u32[]{:S(2)}) copy-start(s32[8]{0:T(128)} %slot_ref.1) | copy-start | bytes 100
  21.4 0.7 %copy-start.15 = (bf16[4,256,128]{2,1,0:T(8,128)(2,1)}, bf16[4,256,128]{2,1,0:T(8,128)(2,1)S(1)}, u32[]{:S(2)}) copy-start(bf16[4,256,128]{2,1,0:T(8,128)(2,1)S(1)} %collective-permute-done.5.rest_4_) | copy-start | bytes 786436
  22.1 0.8 %copy-start.14 = (bf16[2,512,256]{2,1,0:T(8,128)(2,1)}, bf16[2,512,256]{2,1,0:T(8,128)(2,1)S(1)}, u32[]{:S(2)}) copy-start(bf16[2,512,256]{2,1,0:T(8,128)(2,1)S(1)} %collective-permute-done.3.rest_1_) | copy-start | bytes 1572868

commit v6 on v5

--- a/solution.py
+++ b/solution.py
@@ -439,9 +439,14 @@
     if not spread:
         out_ref[...] = returned
         return
-    for s in range(shards):
-        at = s * half // LANES * LANES
-        out_ref[s] = returned[:, at : at + LANES]
+    rows_out = tasks // 2
+    low = lax.broadcasted_iota(jnp.int32, (rows_out, LANES), 1) < LANES // 2
+    for first in range(0, shards, LANES // half):
+        values = returned[:, first * half : first * half + LANES]
+        near, far = values[:rows_out], pltpu.roll(values, LANES // 2, 1)[rows_out:]
+        for i in range(LANES // half):
+            mixed = jnp.where(low, near, far) if 2 * i * half < LANES else jnp.where(low, far, near)
+            out_ref[(first + i) * rows_out : (first + i + 1) * rows_out, :] = mixed
 
 
 def rank_slot(
@@ -456,7 +461,7 @@
     expert_width = experts[0].shape[2]
     block = rows // expert_count
     if spread:
-        out_shape = jax.ShapeDtypeStruct((shards, tasks, LANES), jnp.float32)
+        out_shape = jax.ShapeDtypeStruct((shards * tasks // 2, LANES), jnp.float32)
     else:
         out_shape = jax.ShapeDtypeStruct((tasks, rows_in), jnp.float32)
     bf16 = jnp.bfloat16
@@ -487,26 +492,35 @@
 
 def unpack_body(narrow_count, order_ref, back_ref, returned_ref, out_ref):
     requests, shard_len = back_ref.shape
-    _, tasks, lanes = returned_ref.shape
-    row_at = lax.broadcasted_iota(jnp.int32, (narrow_count * lanes, shard_len), 0)
+    tasks = out_ref.shape[0]
+    half_tasks = tasks // 2
+    rows = narrow_count * half_tasks
+    lanes = returned_ref.shape[1]
+    lane_at = lax.broadcasted_iota(jnp.int32, (lanes, shard_len), 0)
     request_at = lax.broadcasted_iota(jnp.int32, (requests, shard_len), 0)
     results = [jnp.zeros((requests, shard_len), jnp.float32) for t in range(tasks)]
     for s in range(requests):
         mine = request_at == order_ref[s : s + 1, 0:1]
         back = jnp.sum(jnp.where(mine, back_ref[...], 0), axis=0, keepdims=True)
-        pieces = [returned_ref[s * narrow_count + i] for i in range(narrow_count)]
-        parts = three_parts(jnp.concatenate(pieces, axis=1))
-        pick = jnp.where(back == row_at, 1.0, 0.0).astype(jnp.bfloat16)
-        result = sum_parts(dot_f32(parts, pick), tasks)
+        picks = [
+            jnp.where(back == lane_at + i * lanes, 1.0, 0.0).astype(jnp.bfloat16) for i in range(narrow_count)
+        ]
+        near = returned_ref[s * rows : (s + 1) * rows, :]
+        parts = three_parts(jnp.concatenate([near, pltpu.roll(near, lanes // 2, 1)], axis=0))
+        result = sum_parts(dot_f32(parts, jnp.concatenate(picks, axis=1)), 2 * rows)
         for t in range(tasks):
-            results[t] = jnp.where(mine, result[t : t + 1, :], results[t])
+            at = t // half_tasks * rows + t % half_tasks
+            value = result[at : at + 1, :shard_len]
+            for i in range(1, narrow_count):
+                row = at + i * half_tasks
+                value = value + result[row : row + 1, i * shard_len : (i + 1) * shard_len]
+            results[t] = jnp.where(mine, value, results[t])
     for t in range(tasks):
         out_ref[t] = results[t]
 
 
-def unpack_rows(order, back, returned, narrow_count):
+def unpack_rows(order, back, returned, tasks, narrow_count):
     requests, shard_len = back.shape
-    tasks = returned.shape[1]
     return pl.pallas_call(
         functools.partial(unpack_body, narrow_count),
         out_shape=jax.ShapeDtypeStruct((tasks, requests, shard_len), jnp.float32),
@@ -571,7 +585,9 @@
         shard_len % 128 == 0
         and requests % 8 == 0
         and half % 16 == 0
-        and LANES % half == 0
+        and LANES % (2 * half) == 0
+        and tasks % 2 == 0
+        and narrow_count * tasks // 2 % 8 == 0
         and shards * half % LANES == 0
         and group_size == 1
     )
@@ -650,8 +666,10 @@
         )
 
     if blocked:
-        returned = lax.all_to_all(results[0], both, split_axis=0, concat_axis=0, tiled=True)
-        return (prerank_score, unpack_rows(order, back, returned, narrow_count))
+        sending = results[0].reshape(shards, tasks // 2, LANES)
+        returned = lax.all_to_all(sending, both, split_axis=0, concat_axis=0, tiled=True)
+        returned = returned.reshape(shards * tasks // 2, LANES)
+        return (prerank_score, unpack_rows(order, back, returned, tasks, narrow_count))
     sending = jnp.stack(results).reshape(group_size, tasks, shards, half)
     sending = jnp.transpose(sending, (2, 0, 1, 3)).reshape(shards, -1)
     returned = lax.all_to_all(sending, both, split_axis=0, concat_axis=0, tiled=True)

time: 42.8 us -> 42.6 us (level)
  no operation moved by 1% of the time
where the time goes in v6:
time: 42.6 us; the launch traced here: 42.2 us
  Pallas kernels  13.7 us (32%)
  blocking collectives  10.5 us (25%)
  starting transfers between devices  9.36 us (22%)
  waiting for transfers between devices  4.78 us (11%)
  local copies, waits for them, and re-layouts  2.27 us (5%)
  between operations  1.55 us (4%)
    all_to_all x1, blocking collectives, on_device(): lax.all_to_all(sending, both, split_axis=0, concat_axis=0, tiled=True)  10.5 us
    all_to_all x1, starting transfers between devices, on_device(): lax.all_to_all(packed, both, split_axis=0, concat_axis=0, tiled=True)  7.5 us
    pallas_call x1, Pallas kernels, rank_slot(): pl.pallas_call(functools.partial(rank_body, narrow_count, len(experts), s...  5.53 us
    pallas_call x1, Pallas kernels, prerank(): pl.pallas_call(functools.partial(prerank_body, shard_len), out_shape=jax....  2.76 us
    pallas_call x1, Pallas kernels, pack_rows(): pl.pallas_call(functools.partial(pack_body, narrow_count, half), out_shap...  2.6 us
    ppermute x6, waiting for transfers between devices, from_others(): pieces.append(lax.ppermute(values, 'narrow', steps))  2.4 us
    all_to_all x1, waiting for transfers between devices, on_device(): lax.all_to_all(packed, both, split_axis=0, concat_axis=0, tiled=True)  2.37 us
    unnamed x32, local copies, waits for them, and re-layouts  2.2 us
  transfers between devices with their start and end apart: 7, of which 2 were waited for; matrix products, arithmetic and copies ran while one was open for 0% of the time, Pallas kernels for 11%

profile of v6, /device:TPU:0, one launch (start us, length us, event | category | flops | bytes accessed | tf_op | source)
XLA Modules:
  0.0 42.2 jit_solution(11707389888726502632)
XLA Ops:
  0.6 0.0 copy-start.13
  0.6 2.6 %pack_rows.1 = (bf16[512,512]{1,0:T(8,128)(2,1)}, s32[8,128]{1,0:T(8,128)S(1)}, s32[8,128]{1,0:T(8,128)S(1)}, s32[8,128]{1,0:T(8,128)S(1)}) custom-call(s32[8]{0:T(128)} %slot_ref.1, s32[8,512]{1,0:T(8,128)} %kept_ref.1, bf16[8,128,512]{2,1,0:T(8,128)(2,1)} %cand_hbm.1), custom_call_target="tpu_custom_call" | custom-call | flops 67108864 | bytes 1048576 | tf_op jit(solution)/shard_map/pack_rows/pallas_call | solution.py:125
  3.3 0.0 copy-start.7
  3.3 0.0 copy-start.8
  3.3 7.5 %all-to-all-start = ((bf16[16,32,512]{2,1,0:T(8,128)(2,1)}), bf16[16,32,512]{2,1,0:T(8,128)(2,1)S(1)}, u32[]{:S(2)}, u32[]{:S(2)}) async-start(bf16[16,32,512]{2,1,0:T(8,128)(2,1)} %bitcast.15), calls=%async_computation | async-start | bytes 1048576 | tf_op jit(solution)/shard_map/all_to_all | solution.py:605
  10.8 0.0 copy-start.12
  10.8 0.0 copy-start
  10.9 0.1 fusion
  11.0 0.5 %collective-permute-start = (bf16[1,2,512,256]{3,2,1,0:T(8,128)(2,1)S(1)}, bf16[1,2,512,256]{3,2,1,0:T(8,128)(2,1)S(1)}, u32[]{:S(2)}, u32[]{:S(2)}) collective-permute-start(bf16[1,2,512,256]{3,2,1,0:T(8,128)(2,1)S(1)} %copy-done.3), channel_id=1, source_target_pairs={{1,0},{0,1},{3,2},{2,3},{5,4},{4,5},{7,6},{6,7},{9,8},{8,9},{11,10... | collective-permute-start | bytes 1572872 | tf_op jit(solution)/shard_map/ppermute | solution.py:547
  11.4 0.1 collective-permute-start.3
  11.5 0.4 collective-permute-start.4
  11.9 0.1 collective-permute-start.5
  12.0 0.4 collective-permute-start.2
  12.4 2.4 %collective-permute-done.2.rest_5_ = bf16[4,128]{1,0:T(4,128)(2,1)S(1)} collective-permute-done((bf16[4,128]{1,0:T(4,128)(2,1)S(1)}, bf16[4,128]{1,0:T(4,128)(2,1)S(1)}, u32[]{:S(2)}, u32[]{:S(2)}) %collective-permute-start.2) | collective-permute-done | bytes 1056 | tf_op jit(solution)/shard_map/ppermute | solution.py:547
  14.8 0.4 collective-permute-start.1
  15.3 2.8 %prerank.1 = f32[8,128]{1,0:T(8,128)} custom-call(bf16[1024,512]{1,0:T(8,128)(2,1)S(1)} %bitcast.8, bf16[512,512]{1,0:T(8,128)(2,1)S(1)} %copy-done.1, f32[1,512]{1,0:T(1,128)S(1)} %bitcast.12, bf16[512,512]{1,0:T(8,128)(2,1)S(1)} %copy-done.2, bf16[8,512]{1,0:T(8,128)(2,1)S(1)} %copy-done.6, s32[8,128]{1,0:T(8,128)S(1)} %get-tuple-element.29.lane_ref), custom_call_target="tpu_custom_call" | custom-call | flops 1 | bytes 1 | tf_op jit(solution)/shard_map/prerank/pallas_call | solution.py:165
  18.8 0.6 %copy-done.11 = s32[8]{0:T(128)S(1)} copy-done((s32[8]{0:T(128)S(1)}, s32[8]{0:T(128)}, u32[]{:S(2)}) %copy-start.11) | copy-done | bytes 56
  19.4 2.0 %prepare.1 = (s32[8,512]{1,0:T(8,128)S(1)}, bf16[4,160,512]{2,1,0:T(8,128)(2,1)S(1)}, bf16[4,512,128]{2,1,0:T(8,128)(2,1)S(1)}, f32[8,512]{1,0:T(8,128)S(1)}, f3...) custom-call(s32[8]{0:T(128)S(1)} %copy-done.11, ...), custom_call_target="tpu_custom_call" | custom-call | flops 1 | bytes 1 | tf_op jit(solution)/shard_map/prepare/pallas_call | solution.py:283
  21.4 0.7 %copy-done.15 = bf16[4,256,128]{2,1,0:T(8,128)(2,1)} copy-done((bf16[4,256,128]{2,1,0:T(8,128)(2,1)}, bf16[4,256,128]{2,1,0:T(8,128)(2,1)S(1)}, u32[]{:S(2)}) %copy-start.15) | copy-done | bytes 262168
  22.1 0.8 %copy-done.14 = bf16[2,512,256]{2,1,0:T(8,128)(2,1)} copy-done((bf16[2,512,256]{2,1,0:T(8,128)(2,1)}, bf16[2,512,256]{2,1,0:T(8,128)(2,1)S(1)}, u32[]{:S(2)}) %copy-start.14) | copy-done | bytes 524312
  22.9 2.4 %all-to-all-done = bf16[16,32,512]{2,1,0:T(8,128)(2,1)S(1)} async-done(((bf16[16,32,512]{2,1,0:T(8,128)(2,1)}), bf16[16,32,512]{2,1,0:T(8,128)(2,1)S(1)}, u32[]{:S(2)}, u32[]{:S(2)}) %all-to-all-start) | async-done | bytes 524320 | tf_op jit(solution)/shard_map/all_to_all | solution.py:605
  25.3 5.5 %rank_slot.1 = f32[64,128]{1,0:T(8,128)S(1)} custom-call(bf16[4,512,256]{2,1,0:T(8,128)(2,1)} %rest_0_.2, bf16[2,512,256]{2,1,0:T(8,128)(2,1)} %copy-done.14, bf16[2,512,256]{2,1,0:T(8,128)(2,1)} %collective-permute-done.4.rest_2_, bf16[4,256,128]{2,1,0:T(8,128)(2,1)} %rest_3_, bf16[4,256,128]{2,1,0:T(8,128)(2,1)} %copy-done.15, ...), custom_call_target="tpu_custom_call" | custom-call | flops 1610612736 | bytes 6291456 | tf_op jit(solution)/shard_map/rank_slot/pallas_call | solution.py:471
  30.8 10.5 %all_to_all.10 = f32[16,4,128]{2,1,0:T(4,128)S(1)} all-to-all(f32[16,4,128]{2,1,0:T(4,128)S(1)} %bitcast.10), channel_id=1, replica_groups=mesh['groups'=2,'wide'=8,'narrow'=2] {'wide','narrow'}, dimensions={0} | all-to-all | bytes 65536 | tf_op jit(solution)/shard_map/all_to_all | solution.py:670
  41.3 0.9 %unpack_rows.1 = f32[8,8,128]{2,1,0:T(8,128)} custom-call(s32[8,128]{1,0:T(8,128)S(1)} %get-tuple-element.31.order_ref, s32[8,128]{1,0:T(8,128)S(1)} %get-tuple-element.32.back_ref, f32[64,128]{1,0:T(8,128)S(1)} %bitcast.11), custom_call_target="tpu_custom_call" | custom-call | tf_op jit(solution)/shard_map/unpack_rows/pallas_call | solution.py:524
  (29 shorter events, 0.1 us)
Async XLA Ops:
  0.6 10.2 %copy-start.13 = (bf16[4,512,256]{2,1,0:T(8,128)(2,1)S(1)}, bf16[4,512,256]{2,1,0:T(8,128)(2,1)}, u32[]{:S(2)}) copy-start(bf16[4,512,256]{2,1,0:T(8,128)(2,1)} %rest_0_.2) | copy-start | bytes 3145732
  3.2 7.7 %copy-start.3 = (bf16[1,2,512,256]{3,2,1,0:T(8,128)(2,1)S(1)}, bf16[1,2,512,256]{3,2,1,0:T(8,128)(2,1)}, u32[]{:S(2)}) copy-start(bf16[1,2,512,256]{3,2,1,0:T(8,128)(2,1)} %rest_0_.1) | copy-start | bytes 1572868
  3.3 11.6 %copy-start.7 = (f32[1,4,512]{2,1,0:T(4,128)S(1)}, f32[1,4,512]{2,1,0:T(4,128)}, u32[]{:S(2)}) copy-start(f32[1,4,512]{2,1,0:T(4,128)} %rest_2_) | copy-start | bytes 24580
  3.3 11.9 %copy-start.8 = (f32[512]{0:T(512)S(1)}, f32[512]{0:T(512)}, u32[]{:S(2)}) copy-start(f32[512]{0:T(512)} %param.19) | copy-start | bytes 6148
  3.3 22.0 %all-to-all-start = ((bf16[16,32,512]{2,1,0:T(8,128)(2,1)}), bf16[16,32,512]{2,1,0:T(8,128)(2,1)S(1)}, u32[]{:S(2)}, u32[]{:S(2)}) async-start(bf16[16,32,512]{2,1,0:T(8,128)(2,1)} %bitcast.15), calls=%async_computation | async-start | bytes 1048576 | tf_op jit(solution)/shard_map/all_to_all | solution.py:605
  10.8 1.2 %copy-start.12 = (bf16[4,128]{1,0:T(4,128)(2,1)S(1)}, bf16[4,128]{1,0:T(4,128)(2,1)}, u32[]{:S(2)}) copy-start(bf16[4,128]{1,0:T(4,128)(2,1)} %rest_4_) | copy-start | bytes 3076
  10.8 4.4 %copy-start = (bf16[8,128,512]{2,1,0:T(8,128)(2,1)S(1)}, bf16[8,128,512]{2,1,0:T(8,128)(2,1)}, u32[]{:S(2)}) copy-start(bf16[8,128,512]{2,1,0:T(8,128)(2,1)} %cand_hbm.1) | copy-start | bytes 3145732
  10.8 4.4 %copy-start.1 = (bf16[512,512]{1,0:T(8,128)(2,1)S(1)}, bf16[512,512]{1,0:T(8,128)(2,1)}, u32[]{:S(2)}) copy-start(bf16[512,512]{1,0:T(8,128)(2,1)} %inner_ref.1) | copy-start | bytes 1572868
  10.8 4.4 %copy-start.2 = (bf16[512,512]{1,0:T(8,128)(2,1)S(1)}, bf16[512,512]{1,0:T(8,128)(2,1)}, u32[]{:S(2)}) copy-start(bf16[512,512]{1,0:T(8,128)(2,1)} %outer_ref.1) | copy-start | bytes 1572868
  10.9 4.3 %copy-start.6 = (bf16[8,512]{1,0:T(8,128)(2,1)S(1)}, bf16[8,512]{1,0:T(8,128)(2,1)}, u32[]{:S(2)}) copy-start(bf16[8,512]{1,0:T(8,128)(2,1)} %user_ref.1) | copy-start | bytes 24580
  11.0 7.8 %collective-permute-start = (bf16[1,2,512,256]{3,2,1,0:T(8,128)(2,1)S(1)}, bf16[1,2,512,256]{3,2,1,0:T(8,128)(2,1)S(1)}, u32[]{:S(2)}, u32[]{:S(2)}) collective-permute-start(bf16[1,2,512,256]{3,2,1,0:T(8,128)(2,1)S(1)} %copy-done.3), channel_id=1, source_target_pairs={{1,0},{0,1},{3,2},{2,3},{5,4},{4,5},{7,6},{6,7},{9,8},{8,9},{11,10... | collective-permute-start | bytes 1572872 | tf_op jit(solution)/shard_map/ppermute | solution.py:547
  11.4 9.9 %collective-permute-start.3 = (bf16[2,512,256]{2,1,0:T(8,128)(2,1)S(1)}, bf16[2,512,256]{2,1,0:T(8,128)(2,1)S(1)}, u32[]{:S(2)}, u32[]{:S(2)}) collective-permute-start(bf16[2,512,256]{2,1,0:T(8,128)(2,1)S(1)} %get-tuple-element.33), channel_id=1, source_target_pairs={{1,0},{0,1},{3,2},{2,3},{5,4},{4,5},{7,6},{6,7},{9,8},{8,9},{11,10... | collective-permute-start | bytes 1572872 | tf_op jit(solution)/shard_map/ppermute | solution.py:547
  11.5 11.4 %collective-permute-start.4 = (bf16[2,512,256]{2,1,0:T(8,128)(2,1)S(1)}, bf16[2,512,256]{2,1,0:T(8,128)(2,1)}, u32[]{:S(2)}, u32[]{:S(2)}) collective-permute-start(bf16[2,512,256]{2,1,0:T(8,128)(2,1)S(1)} %get-tuple-element.34), channel_id=1, source_target_pairs={{1,0},{0,1},{3,2},{2,3},{5,4},{4,5},{7,6},{6,7},{9,8},{8,9},{11,10... | collective-permute-start | bytes 1572872 | tf_op jit(solution)/shard_map/ppermute | solution.py:547
  11.9 9.4 %collective-permute-start.5 = (bf16[4,256,128]{2,1,0:T(8,128)(2,1)}, bf16[4,256,128]{2,1,0:T(8,128)(2,1)S(1)}, u32[]{:S(2)}, u32[]{:S(2)}) collective-permute-start(bf16[4,256,128]{2,1,0:T(8,128)(2,1)} %rest_3_), channel_id=1, source_target_pairs={{1,0},{0,1},{3,2},{2,3},{5,4},{4,5},{7,6},{6,7},{9,8},{8,9},{11,10... | collective-permute-start | bytes 786440 | tf_op jit(solution)/shard_map/ppermute | solution.py:547
  12.0 2.8 %collective-permute-start.2 = (bf16[4,128]{1,0:T(4,128)(2,1)S(1)}, bf16[4,128]{1,0:T(4,128)(2,1)S(1)}, u32[]{:S(2)}, u32[]{:S(2)}) collective-permute-start(bf16[4,128]{1,0:T(4,128)(2,1)S(1)} %copy-done.12), channel_id=1, source_target_pairs={{1,0},{0,1},{3,2},{2,3},{5,4},{4,5},{7,6},{6,7},{9,8},{8,9},{11,10... | collective-permute-start | bytes 3080 | tf_op jit(solution)/shard_map/ppermute | solution.py:547
  14.8 3.9 %collective-permute-start.1 = (f32[1,4,512]{2,1,0:T(4,128)S(1)}, f32[1,4,512]{2,1,0:T(4,128)S(1)}, u32[]{:S(2)}, u32[]{:S(2)}) collective-permute-start(f32[1,4,512]{2,1,0:T(4,128)S(1)} %copy-done.7), channel_id=1, source_target_pairs={{1,0},{0,1},{3,2},{2,3},{5,4},{4,5},{7,6},{6,7},{9,8},{8,9},{11,10... | collective-permute-start | bytes 24584 | tf_op jit(solution)/shard_map/ppermute | solution.py:547
  15.2 3.5 %copy-start.4 = (bf16[1,2,512,256]{3,2,1,0:T(8,128)(2,1)S(1)}, bf16[1,2,512,256]{3,2,1,0:T(8,128)(2,1)}, u32[]{:S(2)}) copy-start(bf16[1,2,512,256]{3,2,1,0:T(8,128)(2,1)} %rest_0_.1) | copy-start | bytes 1572868
  15.2 3.5 %copy-start.5 = (s32[8,512]{1,0:T(8,128)S(1)}, s32[8,512]{1,0:T(8,128)}, u32[]{:S(2)}) copy-start(s32[8,512]{1,0:T(8,128)} %kept_ref.1) | copy-start | bytes 49156
  15.3 3.5 %copy-start.10 = (f32[512]{0:T(512)S(1)}, f32[512]{0:T(512)}, u32[]{:S(2)}) copy-start(f32[512]{0:T(512)} %param.28) | copy-start | bytes 6148
  18.0 0.7 %copy-start.9 = (f32[8,8]{1,0:T(8,128)S(1)}, f32[8,8]{1,0:T(8,128)}, u32[]{:S(2)}) copy-start(f32[8,8]{1,0:T(8,128)} %rest_8_.1) | copy-start | bytes 772
  18.7 0.7 %copy-start.11 = (s32[8]{0:T(128)S(1)}, s32[8]{0:T(128)}, u32[]{:S(2)}) copy-start(s32[8]{0:T(128)} %slot_ref.1) | copy-start | bytes 100
  21.4 0.7 %copy-start.15 = (bf16[4,256,128]{2,1,0:T(8,128)(2,1)}, bf16[4,256,128]{2,1,0:T(8,128)(2,1)S(1)}, u32[]{:S(2)}) copy-start(bf16[4,256,128]{2,1,0:T(8,128)(2,1)S(1)} %collective-permute-done.5.rest_4_) | copy-start | bytes 786436
  22.1 0.8 %copy-start.14 = (bf16[2,512,256]{2,1,0:T(8,128)(2,1)}, bf16[2,512,256]{2,1,0:T(8,128)(2,1)S(1)}, u32[]{:S(2)}) copy-start(bf16[2,512,256]{2,1,0:T(8,128)(2,1)S(1)} %collective-permute-done.3.rest_1_) | copy-start | bytes 1572868

commit v7 on v6

--- a/solution.py
+++ b/solution.py
@@ -212,13 +212,15 @@
     offsets = jnp.where(gate_row == gate_lane, offsets.reshape(tasks * experts, experts), 0.0)
     gate_offsets_ref[...] = jnp.broadcast_to(jnp.sum(offsets, axis=1, keepdims=True), gate_offsets_ref.shape)
     tasks_here, tower_width = tower_outer_refs[0].shape
-    row = lax.broadcasted_iota(jnp.int32, (tasks, tower_width), 0)
+    row = lax.broadcasted_iota(jnp.int32, (tower_rows_ref.shape[0], tower_width), 0)
     for i in range(narrow_count):
+        outer = tower_outer_refs[i][...].astype(jnp.float32)
         for t in range(tasks_here):
             task = lax.rem(me + i, narrow_count) * tasks_here + t
-            outer = tower_outer_refs[i][t : t + 1, :].astype(jnp.float32)
             at = (i * tasks_here + t) * tower_width
-            tower_rows_ref[:, at : at + tower_width] = jnp.where(row == task, outer, 0.0).astype(jnp.bfloat16)
+            tower_rows_ref[:, at : at + tower_width] = jnp.where(row == task, outer[t : t + 1, :], 0.0).astype(
+                jnp.bfloat16
+            )
 
     kept_row = kept_ref[pl.ds(request, 1), :]
     edge = lax.broadcasted_iota(jnp.int32, (shards, kept_row.shape[1]), 0) * shard_len
@@ -247,10 +249,10 @@
                 head = 2 * t + h
                 masked = jnp.where(visible, bias_refs[i][slot_at, head : head + 1, :], -1e30)
                 bias = jnp.where(row == h, masked, bias)
-            parts = three_parts(bias)
-            keys_ref[at, tile:, :] = jnp.concatenate(
-                [parts, jnp.zeros((BIAS_ROWS, span), jnp.bfloat16)], axis=0
-            )
+            high = bias.astype(jnp.bfloat16).astype(jnp.float32)
+            middle = (bias - high).astype(jnp.bfloat16).astype(jnp.float32)
+            parts = [high, middle, bias - high - middle, jnp.zeros_like(bias)]
+            keys_ref[at, tile:, :] = jnp.concatenate(parts, axis=0).astype(jnp.bfloat16)
             values_ref[at] = history_refs[i][slot_at, 1, :, t * tile : (t + 1) * tile]
     for copy in copies:
         copy.wait()
@@ -288,7 +290,7 @@
             pltpu.VMEM((pairs, span, tile), bf16),
             pltpu.VMEM((8, width), jnp.float32),
             pltpu.VMEM((tasks * experts, LANES), jnp.float32),
-            pltpu.VMEM((tasks, tasks * tower_outer[0].shape[1]), bf16),
+            pltpu.VMEM((-(-tasks // 16) * 16, tasks * tower_outer[0].shape[1]), bf16),
             *[pltpu.VMEM(weight.shape, weight.dtype) for weight in weights],
         ),
         in_specs=[SMEM, SMEM] + [VMEM] * (4 + 3 * narrow_count) + [ANY] * len(weights),
@@ -433,7 +435,7 @@
         for t in range(tasks_here):
             at = i * tasks_here + t
             acts.append(jnp.maximum(dot_f32(mixture_ref[at], tower_refs[i, t]), 0.0).astype(jnp.bfloat16))
-    by_task = dot_nt(tower_rows_ref[...], jnp.concatenate(acts, axis=1))
+    by_task = dot_nt(tower_rows_ref[...], jnp.concatenate(acts, axis=1))[:tasks]
 
     returned = sum_parts(dot_f32(three_parts(by_task), placing), tasks)
     if not spread:
@@ -456,7 +458,7 @@
     narrow_count = len(towers)
     rows_in = arrived.shape[0]
     width = outer.shape[1]
-    tasks = tower_rows.shape[0]
+    tasks = narrow_count * towers[0].shape[0]
     expert_count = gate_rows.shape[0] // tasks
     expert_width = experts[0].shape[2]
     block = rows // expert_count

time: 42.6 us -> 42.6 us (level)
  no operation moved by 1% of the time
where the time goes in v7:
time: 42.6 us; the launch traced here: 42.2 us
  Pallas kernels  13.7 us (32%)
  blocking collectives  10.5 us (25%)
  starting transfers between devices  9.36 us (22%)
  waiting for transfers between devices  4.78 us (11%)
  local copies, waits for them, and re-layouts  2.27 us (5%)
  between operations  1.55 us (4%)
    all_to_all x1, blocking collectives, on_device(): lax.all_to_all(sending, both, split_axis=0, concat_axis=0, tiled=True)  10.5 us
    all_to_all x1, starting transfers between devices, on_device(): lax.all_to_all(packed, both, split_axis=0, concat_axis=0, tiled=True)  7.5 us
    pallas_call x1, Pallas kernels, rank_slot(): pl.pallas_call(functools.partial(rank_body, narrow_count, len(experts), s...  5.53 us
    pallas_call x1, Pallas kernels, prerank(): pl.pallas_call(functools.partial(prerank_body, shard_len), out_shape=jax....  2.76 us
    pallas_call x1, Pallas kernels, pack_rows(): pl.pallas_call(functools.partial(pack_body, narrow_count, half), out_shap...  2.6 us
    ppermute x6, waiting for transfers between devices, from_others(): pieces.append(lax.ppermute(values, 'narrow', steps))  2.4 us
    all_to_all x1, waiting for transfers between devices, on_device(): lax.all_to_all(packed, both, split_axis=0, concat_axis=0, tiled=True)  2.38 us
    unnamed x32, local copies, waits for them, and re-layouts  2.2 us
  transfers between devices with their start and end apart: 7, of which 2 were waited for; matrix products, arithmetic and copies ran while one was open for 0% of the time, Pallas kernels for 11%

profile of v7, /device:TPU:0, one launch (start us, length us, event | category | flops | bytes accessed | tf_op | source)
XLA Modules:
  0.0 42.2 jit_solution(10583986994111283888)
XLA Ops:
  0.6 0.0 copy-start.13
  0.6 2.6 %pack_rows.1 = (bf16[512,512]{1,0:T(8,128)(2,1)}, s32[8,128]{1,0:T(8,128)S(1)}, s32[8,128]{1,0:T(8,128)S(1)}, s32[8,128]{1,0:T(8,128)S(1)}) custom-call(s32[8]{0:T(128)} %slot_ref.1, s32[8,512]{1,0:T(8,128)} %kept_ref.1, bf16[8,128,512]{2,1,0:T(8,128)(2,1)} %cand_hbm.1), custom_call_target="tpu_custom_call" | custom-call | flops 67108864 | bytes 1048576 | tf_op jit(solution)/shard_map/pack_rows/pallas_call | solution.py:125
  3.3 0.0 copy-start.8
  3.3 7.5 %all-to-all-start = ((bf16[16,32,512]{2,1,0:T(8,128)(2,1)}), bf16[16,32,512]{2,1,0:T(8,128)(2,1)S(1)}, u32[]{:S(2)}, u32[]{:S(2)}) async-start(bf16[16,32,512]{2,1,0:T(8,128)(2,1)} %bitcast.15), calls=%async_computation | async-start | bytes 1048576 | tf_op jit(solution)/shard_map/all_to_all | solution.py:607
  10.8 0.0 copy-start
  10.8 0.0 copy-start.1
  10.9 0.1 fusion
  11.0 0.5 %collective-permute-start = (bf16[1,2,512,256]{3,2,1,0:T(8,128)(2,1)S(1)}, bf16[1,2,512,256]{3,2,1,0:T(8,128)(2,1)S(1)}, u32[]{:S(2)}, u32[]{:S(2)}) collective-permute-start(bf16[1,2,512,256]{3,2,1,0:T(8,128)(2,1)S(1)} %copy-done.3), channel_id=1, source_target_pairs={{1,0},{0,1},{3,2},{2,3},{5,4},{4,5},{7,6},{6,7},{9,8},{8,9},{11,10... | collective-permute-start | bytes 1572872 | tf_op jit(solution)/shard_map/ppermute | solution.py:549
  11.4 0.1 collective-permute-start.3
  11.5 0.4 collective-permute-start.4
  11.9 0.1 collective-permute-start.5
  12.0 0.4 collective-permute-start.2
  12.4 2.4 %collective-permute-done.2.rest_5_ = bf16[4,128]{1,0:T(4,128)(2,1)S(1)} collective-permute-done((bf16[4,128]{1,0:T(4,128)(2,1)S(1)}, bf16[4,128]{1,0:T(4,128)(2,1)S(1)}, u32[]{:S(2)}, u32[]{:S(2)}) %collective-permute-start.2) | collective-permute-done | bytes 1056 | tf_op jit(solution)/shard_map/ppermute | solution.py:549
  14.8 0.4 collective-permute-start.1
  15.2 0.0 copy-start.5
  15.3 2.8 %prerank.1 = f32[8,128]{1,0:T(8,128)} custom-call(bf16[1024,512]{1,0:T(8,128)(2,1)S(1)} %bitcast.8, bf16[512,512]{1,0:T(8,128)(2,1)S(1)} %copy-done.1, f32[1,512]{1,0:T(1,128)S(1)} %bitcast.12, bf16[512,512]{1,0:T(8,128)(2,1)S(1)} %copy-done.2, bf16[8,512]{1,0:T(8,128)(2,1)S(1)} %copy-done.6, s32[8,128]{1,0:T(8,128)S(1)} %get-tuple-element.29.lane_ref), custom_call_target="tpu_custom_call" | custom-call | flops 1 | bytes 1 | tf_op jit(solution)/shard_map/prerank/pallas_call | solution.py:165
  18.8 0.6 %copy-done.11 = s32[8]{0:T(128)S(1)} copy-done((s32[8]{0:T(128)S(1)}, s32[8]{0:T(128)}, u32[]{:S(2)}) %copy-start.11) | copy-done | bytes 56
  19.4 2.0 %prepare.1 = (s32[8,512]{1,0:T(8,128)S(1)}, bf16[4,160,512]{2,1,0:T(8,128)(2,1)S(1)}, bf16[4,512,128]{2,1,0:T(8,128)(2,1)S(1)}, f32[8,512]{1,0:T(8,128)S(1)}, f3...) custom-call(s32[8]{0:T(128)S(1)} %copy-done.11, ...), custom_call_target="tpu_custom_call" | custom-call | flops 1 | bytes 1 | tf_op jit(solution)/shard_map/prepare/pallas_call | solution.py:285
  21.4 0.7 %copy-done.15 = bf16[4,256,128]{2,1,0:T(8,128)(2,1)} copy-done((bf16[4,256,128]{2,1,0:T(8,128)(2,1)}, bf16[4,256,128]{2,1,0:T(8,128)(2,1)S(1)}, u32[]{:S(2)}) %copy-start.15) | copy-done | bytes 262168
  22.1 0.8 %copy-done.14 = bf16[2,512,256]{2,1,0:T(8,128)(2,1)} copy-done((bf16[2,512,256]{2,1,0:T(8,128)(2,1)}, bf16[2,512,256]{2,1,0:T(8,128)(2,1)S(1)}, u32[]{:S(2)}) %copy-start.14) | copy-done | bytes 524312
  22.9 2.4 %all-to-all-done = bf16[16,32,512]{2,1,0:T(8,128)(2,1)S(1)} async-done(((bf16[16,32,512]{2,1,0:T(8,128)(2,1)}), bf16[16,32,512]{2,1,0:T(8,128)(2,1)S(1)}, u32[]{:S(2)}, u32[]{:S(2)}) %all-to-all-start) | async-done | bytes 524320 | tf_op jit(solution)/shard_map/all_to_all | solution.py:607
  25.3 5.5 %rank_slot.1 = f32[64,128]{1,0:T(8,128)S(1)} custom-call(bf16[4,512,256]{2,1,0:T(8,128)(2,1)} %rest_0_.2, bf16[2,512,256]{2,1,0:T(8,128)(2,1)} %copy-done.14, bf16[2,512,256]{2,1,0:T(8,128)(2,1)} %collective-permute-done.4.rest_2_, bf16[4,256,128]{2,1,0:T(8,128)(2,1)} %rest_3_, bf16[4,256,128]{2,1,0:T(8,128)(2,1)} %copy-done.15, ...), custom_call_target="tpu_custom_call" | custom-call | flops 1610612736 | bytes 6291456 | tf_op jit(solution)/shard_map/rank_slot/pallas_call | solution.py:473
  30.8 10.5 %all_to_all.10 = f32[16,4,128]{2,1,0:T(4,128)S(1)} all-to-all(f32[16,4,128]{2,1,0:T(4,128)S(1)} %bitcast.10), channel_id=1, replica_groups=mesh['groups'=2,'wide'=8,'narrow'=2] {'wide','narrow'}, dimensions={0} | all-to-all | bytes 65536 | tf_op jit(solution)/shard_map/all_to_all | solution.py:672
  41.3 0.9 %unpack_rows.1 = f32[8,8,128]{2,1,0:T(8,128)} custom-call(s32[8,128]{1,0:T(8,128)S(1)} %get-tuple-element.31.order_ref, s32[8,128]{1,0:T(8,128)S(1)} %get-tuple-element.32.back_ref, f32[64,128]{1,0:T(8,128)S(1)} %bitcast.11), custom_call_target="tpu_custom_call" | custom-call | tf_op jit(solution)/shard_map/unpack_rows/pallas_call | solution.py:526
  (29 shorter events, 0.1 us)
Async XLA Ops:
  0.6 10.2 %copy-start.13 = (bf16[4,512,256]{2,1,0:T(8,128)(2,1)S(1)}, bf16[4,512,256]{2,1,0:T(8,128)(2,1)}, u32[]{:S(2)}) copy-start(bf16[4,512,256]{2,1,0:T(8,128)(2,1)} %rest_0_.2) | copy-start | bytes 3145732
  3.2 7.7 %copy-start.3 = (bf16[1,2,512,256]{3,2,1,0:T(8,128)(2,1)S(1)}, bf16[1,2,512,256]{3,2,1,0:T(8,128)(2,1)}, u32[]{:S(2)}) copy-start(bf16[1,2,512,256]{3,2,1,0:T(8,128)(2,1)} %rest_0_.1) | copy-start | bytes 1572868
  3.3 11.6 %copy-start.7 = (f32[1,4,512]{2,1,0:T(4,128)S(1)}, f32[1,4,512]{2,1,0:T(4,128)}, u32[]{:S(2)}) copy-start(f32[1,4,512]{2,1,0:T(4,128)} %rest_2_) | copy-start | bytes 24580
  3.3 11.9 %copy-start.8 = (f32[512]{0:T(512)S(1)}, f32[512]{0:T(512)}, u32[]{:S(2)}) copy-start(f32[512]{0:T(512)} %param.19) | copy-start | bytes 6148
  3.3 22.0 %all-to-all-start = ((bf16[16,32,512]{2,1,0:T(8,128)(2,1)}), bf16[16,32,512]{2,1,0:T(8,128)(2,1)S(1)}, u32[]{:S(2)}, u32[]{:S(2)}) async-start(bf16[16,32,512]{2,1,0:T(8,128)(2,1)} %bitcast.15), calls=%async_computation | async-start | bytes 1048576 | tf_op jit(solution)/shard_map/all_to_all | solution.py:607
  10.8 1.2 %copy-start.12 = (bf16[4,128]{1,0:T(4,128)(2,1)S(1)}, bf16[4,128]{1,0:T(4,128)(2,1)}, u32[]{:S(2)}) copy-start(bf16[4,128]{1,0:T(4,128)(2,1)} %rest_4_) | copy-start | bytes 3076
  10.8 4.4 %copy-start = (bf16[8,128,512]{2,1,0:T(8,128)(2,1)S(1)}, bf16[8,128,512]{2,1,0:T(8,128)(2,1)}, u32[]{:S(2)}) copy-start(bf16[8,128,512]{2,1,0:T(8,128)(2,1)} %cand_hbm.1) | copy-start | bytes 3145732
  10.8 4.4 %copy-start.1 = (bf16[512,512]{1,0:T(8,128)(2,1)S(1)}, bf16[512,512]{1,0:T(8,128)(2,1)}, u32[]{:S(2)}) copy-start(bf16[512,512]{1,0:T(8,128)(2,1)} %inner_ref.1) | copy-start | bytes 1572868
  10.8 4.4 %copy-start.2 = (bf16[512,512]{1,0:T(8,128)(2,1)S(1)}, bf16[512,512]{1,0:T(8,128)(2,1)}, u32[]{:S(2)}) copy-start(bf16[512,512]{1,0:T(8,128)(2,1)} %outer_ref.1) | copy-start | bytes 1572868
  10.9 4.3 %copy-start.6 = (bf16[8,512]{1,0:T(8,128)(2,1)S(1)}, bf16[8,512]{1,0:T(8,128)(2,1)}, u32[]{:S(2)}) copy-start(bf16[8,512]{1,0:T(8,128)(2,1)} %user_ref.1) | copy-start | bytes 24580
  11.0 7.8 %collective-permute-start = (bf16[1,2,512,256]{3,2,1,0:T(8,128)(2,1)S(1)}, bf16[1,2,512,256]{3,2,1,0:T(8,128)(2,1)S(1)}, u32[]{:S(2)}, u32[]{:S(2)}) collective-permute-start(bf16[1,2,512,256]{3,2,1,0:T(8,128)(2,1)S(1)} %copy-done.3), channel_id=1, source_target_pairs={{1,0},{0,1},{3,2},{2,3},{5,4},{4,5},{7,6},{6,7},{9,8},{8,9},{11,10... | collective-permute-start | bytes 1572872 | tf_op jit(solution)/shard_map/ppermute | solution.py:549
  11.4 9.9 %collective-permute-start.3 = (bf16[2,512,256]{2,1,0:T(8,128)(2,1)S(1)}, bf16[2,512,256]{2,1,0:T(8,128)(2,1)S(1)}, u32[]{:S(2)}, u32[]{:S(2)}) collective-permute-start(bf16[2,512,256]{2,1,0:T(8,128)(2,1)S(1)} %get-tuple-element.33), channel_id=1, source_target_pairs={{1,0},{0,1},{3,2},{2,3},{5,4},{4,5},{7,6},{6,7},{9,8},{8,9},{11,10... | collective-permute-start | bytes 1572872 | tf_op jit(solution)/shard_map/ppermute | solution.py:549
  11.5 11.4 %collective-permute-start.4 = (bf16[2,512,256]{2,1,0:T(8,128)(2,1)S(1)}, bf16[2,512,256]{2,1,0:T(8,128)(2,1)}, u32[]{:S(2)}, u32[]{:S(2)}) collective-permute-start(bf16[2,512,256]{2,1,0:T(8,128)(2,1)S(1)} %get-tuple-element.34), channel_id=1, source_target_pairs={{1,0},{0,1},{3,2},{2,3},{5,4},{4,5},{7,6},{6,7},{9,8},{8,9},{11,10... | collective-permute-start | bytes 1572872 | tf_op jit(solution)/shard_map/ppermute | solution.py:549
  11.9 9.4 %collective-permute-start.5 = (bf16[4,256,128]{2,1,0:T(8,128)(2,1)}, bf16[4,256,128]{2,1,0:T(8,128)(2,1)S(1)}, u32[]{:S(2)}, u32[]{:S(2)}) collective-permute-start(bf16[4,256,128]{2,1,0:T(8,128)(2,1)} %rest_3_), channel_id=1, source_target_pairs={{1,0},{0,1},{3,2},{2,3},{5,4},{4,5},{7,6},{6,7},{9,8},{8,9},{11,10... | collective-permute-start | bytes 786440 | tf_op jit(solution)/shard_map/ppermute | solution.py:549
  12.0 2.8 %collective-permute-start.2 = (bf16[4,128]{1,0:T(4,128)(2,1)S(1)}, bf16[4,128]{1,0:T(4,128)(2,1)S(1)}, u32[]{:S(2)}, u32[]{:S(2)}) collective-permute-start(bf16[4,128]{1,0:T(4,128)(2,1)S(1)} %copy-done.12), channel_id=1, source_target_pairs={{1,0},{0,1},{3,2},{2,3},{5,4},{4,5},{7,6},{6,7},{9,8},{8,9},{11,10... | collective-permute-start | bytes 3080 | tf_op jit(solution)/shard_map/ppermute | solution.py:549
  14.8 3.9 %collective-permute-start.1 = (f32[1,4,512]{2,1,0:T(4,128)S(1)}, f32[1,4,512]{2,1,0:T(4,128)S(1)}, u32[]{:S(2)}, u32[]{:S(2)}) collective-permute-start(f32[1,4,512]{2,1,0:T(4,128)S(1)} %copy-done.7), channel_id=1, source_target_pairs={{1,0},{0,1},{3,2},{2,3},{5,4},{4,5},{7,6},{6,7},{9,8},{8,9},{11,10... | collective-permute-start | bytes 24584 | tf_op jit(solution)/shard_map/ppermute | solution.py:549
  15.2 3.5 %copy-start.4 = (bf16[1,2,512,256]{3,2,1,0:T(8,128)(2,1)S(1)}, bf16[1,2,512,256]{3,2,1,0:T(8,128)(2,1)}, u32[]{:S(2)}) copy-start(bf16[1,2,512,256]{3,2,1,0:T(8,128)(2,1)} %rest_0_.1) | copy-start | bytes 1572868
  15.2 3.5 %copy-start.5 = (s32[8,512]{1,0:T(8,128)S(1)}, s32[8,512]{1,0:T(8,128)}, u32[]{:S(2)}) copy-start(s32[8,512]{1,0:T(8,128)} %kept_ref.1) | copy-start | bytes 49156
  15.3 3.5 %copy-start.10 = (f32[512]{0:T(512)S(1)}, f32[512]{0:T(512)}, u32[]{:S(2)}) copy-start(f32[512]{0:T(512)} %param.28) | copy-start | bytes 6148
  18.0 0.7 %copy-start.9 = (f32[8,8]{1,0:T(8,128)S(1)}, f32[8,8]{1,0:T(8,128)}, u32[]{:S(2)}) copy-start(f32[8,8]{1,0:T(8,128)} %rest_8_.1) | copy-start | bytes 772
  18.7 0.7 %copy-start.11 = (s32[8]{0:T(128)S(1)}, s32[8]{0:T(128)}, u32[]{:S(2)}) copy-start(s32[8]{0:T(128)} %slot_ref.1) | copy-start | bytes 100
  21.4 0.7 %copy-start.15 = (bf16[4,256,128]{2,1,0:T(8,128)(2,1)}, bf16[4,256,128]{2,1,0:T(8,128)(2,1)S(1)}, u32[]{:S(2)}) copy-start(bf16[4,256,128]{2,1,0:T(8,128)(2,1)S(1)} %collective-permute-done.5.rest_4_) | copy-start | bytes 786436
  22.1 0.8 %copy-start.14 = (bf16[2,512,256]{2,1,0:T(8,128)(2,1)}, bf16[2,512,256]{2,1,0:T(8,128)(2,1)S(1)}, u32[]{:S(2)}) copy-start(bf16[2,512,256]{2,1,0:T(8,128)(2,1)S(1)} %collective-permute-done.3.rest_1_) | copy-start | bytes 1572868

commit v8 on v7

--- a/solution.py
+++ b/solution.py
@@ -333,10 +333,11 @@
         tower_refs,
         sems,
     ) = rest[11:]
-    own = expert_hbm[0].shape[0]
-    own_copy = pltpu.make_async_copy(expert_hbm[0], expert_refs.at[pl.ds(0, own)], sems.at[0])
+    own = expert_hbm[0].shape[0] // 2
+    rest_of_own = pl.ds(own, expert_hbm[0].shape[0] - own)
+    own_copy = pltpu.make_async_copy(expert_hbm[0].at[pl.ds(0, own)], expert_refs.at[pl.ds(0, own)], sems.at[0])
     own_copy.start()
-    late_copies = []
+    late_copies = [pltpu.make_async_copy(expert_hbm[0].at[rest_of_own], expert_refs.at[rest_of_own], sems.at[1])]
     for i in range(1, pieces):
         at = sum(piece.shape[0] for piece in expert_hbm[:i])
         here = expert_refs.at[pl.ds(at, expert_hbm[i].shape[0])]

time: 42.6 us -> 42.5 us (level)
  no operation moved by 1% of the time
where the time goes in v8:
time: 42.5 us; the launch traced here: 42.1 us
  Pallas kernels  13.6 us (32%)
  blocking collectives  10.5 us (25%)
  starting transfers between devices  9.36 us (22%)
  waiting for transfers between devices  4.78 us (11%)
  local copies, waits for them, and re-layouts  2.27 us (5%)
  between operations  1.55 us (4%)
    all_to_all x1, blocking collectives, on_device(): lax.all_to_all(sending, both, split_axis=0, concat_axis=0, tiled=True)  10.5 us
    all_to_all x1, starting transfers between devices, on_device(): lax.all_to_all(packed, both, split_axis=0, concat_axis=0, tiled=True)  7.5 us
    pallas_call x1, Pallas kernels, rank_slot(): pl.pallas_call(functools.partial(rank_body, narrow_count, len(experts), s...  5.41 us
    pallas_call x1, Pallas kernels, prerank(): pl.pallas_call(functools.partial(prerank_body, shard_len), out_shape=jax....  2.76 us
    pallas_call x1, Pallas kernels, pack_rows(): pl.pallas_call(functools.partial(pack_body, narrow_count, half), out_shap...  2.6 us
    ppermute x6, waiting for transfers between devices, from_others(): pieces.append(lax.ppermute(values, 'narrow', steps))  2.4 us
    all_to_all x1, waiting for transfers between devices, on_device(): lax.all_to_all(packed, both, split_axis=0, concat_axis=0, tiled=True)  2.38 us
    unnamed x32, local copies, waits for them, and re-layouts  2.2 us
  transfers between devices with their start and end apart: 7, of which 2 were waited for; matrix products, arithmetic and copies ran while one was open for 0% of the time, Pallas kernels for 11%

profile of v8, /device:TPU:0, one launch (start us, length us, event | category | flops | bytes accessed | tf_op | source)
XLA Modules:
  0.0 42.1 jit_solution(13038914485967300997)
XLA Ops:
  0.6 0.0 copy-start.13
  0.6 2.6 %pack_rows.1 = (bf16[512,512]{1,0:T(8,128)(2,1)}, s32[8,128]{1,0:T(8,128)S(1)}, s32[8,128]{1,0:T(8,128)S(1)}, s32[8,128]{1,0:T(8,128)S(1)}) custom-call(s32[8]{0:T(128)} %slot_ref.1, s32[8,512]{1,0:T(8,128)} %kept_ref.1, bf16[8,128,512]{2,1,0:T(8,128)(2,1)} %cand_hbm.1), custom_call_target="tpu_custom_call" | custom-call | flops 67108864 | bytes 1048576 | tf_op jit(solution)/shard_map/pack_rows/pallas_call | solution.py:125
  3.3 0.0 copy-start.7
  3.3 0.0 copy-start.8
  3.3 7.5 %all-to-all-start = ((bf16[16,32,512]{2,1,0:T(8,128)(2,1)}), bf16[16,32,512]{2,1,0:T(8,128)(2,1)S(1)}, u32[]{:S(2)}, u32[]{:S(2)}) async-start(bf16[16,32,512]{2,1,0:T(8,128)(2,1)} %bitcast.15), calls=%async_computation | async-start | bytes 1048576 | tf_op jit(solution)/shard_map/all_to_all | solution.py:608
  10.8 0.0 copy-start.12
  10.8 0.0 copy-start
  10.9 0.1 fusion
  11.0 0.5 %collective-permute-start = (bf16[1,2,512,256]{3,2,1,0:T(8,128)(2,1)S(1)}, bf16[1,2,512,256]{3,2,1,0:T(8,128)(2,1)S(1)}, u32[]{:S(2)}, u32[]{:S(2)}) collective-permute-start(bf16[1,2,512,256]{3,2,1,0:T(8,128)(2,1)S(1)} %copy-done.3), channel_id=1, source_target_pairs={{1,0},{0,1},{3,2},{2,3},{5,4},{4,5},{7,6},{6,7},{9,8},{8,9},{11,10... | collective-permute-start | bytes 1572872 | tf_op jit(solution)/shard_map/ppermute | solution.py:550
  11.4 0.1 collective-permute-start.3
  11.5 0.4 collective-permute-start.4
  11.9 0.1 collective-permute-start.5
  12.0 0.4 collective-permute-start.2
  12.4 2.4 %collective-permute-done.2.rest_5_ = bf16[4,128]{1,0:T(4,128)(2,1)S(1)} collective-permute-done((bf16[4,128]{1,0:T(4,128)(2,1)S(1)}, bf16[4,128]{1,0:T(4,128)(2,1)S(1)}, u32[]{:S(2)}, u32[]{:S(2)}) %collective-permute-start.2) | collective-permute-done | bytes 1056 | tf_op jit(solution)/shard_map/ppermute | solution.py:550
  14.8 0.4 collective-permute-start.1
  15.3 2.8 %prerank.1 = f32[8,128]{1,0:T(8,128)} custom-call(bf16[1024,512]{1,0:T(8,128)(2,1)S(1)} %bitcast.8, bf16[512,512]{1,0:T(8,128)(2,1)S(1)} %copy-done.1, f32[1,512]{1,0:T(1,128)S(1)} %bitcast.12, bf16[512,512]{1,0:T(8,128)(2,1)S(1)} %copy-done.2, bf16[8,512]{1,0:T(8,128)(2,1)S(1)} %copy-done.6, s32[8,128]{1,0:T(8,128)S(1)} %get-tuple-element.29.lane_ref), custom_call_target="tpu_custom_call" | custom-call | flops 1 | bytes 1 | tf_op jit(solution)/shard_map/prerank/pallas_call | solution.py:165
  18.8 0.6 %copy-done.11 = s32[8]{0:T(128)S(1)} copy-done((s32[8]{0:T(128)S(1)}, s32[8]{0:T(128)}, u32[]{:S(2)}) %copy-start.11) | copy-done | bytes 56
  19.4 2.0 %prepare.1 = (s32[8,512]{1,0:T(8,128)S(1)}, bf16[4,160,512]{2,1,0:T(8,128)(2,1)S(1)}, bf16[4,512,128]{2,1,0:T(8,128)(2,1)S(1)}, f32[8,512]{1,0:T(8,128)S(1)}, f3...) custom-call(s32[8]{0:T(128)S(1)} %copy-done.11, ...), custom_call_target="tpu_custom_call" | custom-call | flops 1 | bytes 1 | tf_op jit(solution)/shard_map/prepare/pallas_call | solution.py:285
  21.4 0.7 %copy-done.15 = bf16[4,256,128]{2,1,0:T(8,128)(2,1)} copy-done((bf16[4,256,128]{2,1,0:T(8,128)(2,1)}, bf16[4,256,128]{2,1,0:T(8,128)(2,1)S(1)}, u32[]{:S(2)}) %copy-start.15) | copy-done | bytes 262168
  22.1 0.8 %copy-done.14 = bf16[2,512,256]{2,1,0:T(8,128)(2,1)} copy-done((bf16[2,512,256]{2,1,0:T(8,128)(2,1)}, bf16[2,512,256]{2,1,0:T(8,128)(2,1)S(1)}, u32[]{:S(2)}) %copy-start.14) | copy-done | bytes 524312
  22.9 2.4 %all-to-all-done = bf16[16,32,512]{2,1,0:T(8,128)(2,1)S(1)} async-done(((bf16[16,32,512]{2,1,0:T(8,128)(2,1)}), bf16[16,32,512]{2,1,0:T(8,128)(2,1)S(1)}, u32[]{:S(2)}, u32[]{:S(2)}) %all-to-all-start) | async-done | bytes 524320 | tf_op jit(solution)/shard_map/all_to_all | solution.py:608
  25.3 5.4 %rank_slot.1 = f32[64,128]{1,0:T(8,128)S(1)} custom-call(bf16[4,512,256]{2,1,0:T(8,128)(2,1)} %rest_0_.2, bf16[2,512,256]{2,1,0:T(8,128)(2,1)} %copy-done.14, bf16[2,512,256]{2,1,0:T(8,128)(2,1)} %collective-permute-done.4.rest_2_, bf16[4,256,128]{2,1,0:T(8,128)(2,1)} %rest_3_, bf16[4,256,128]{2,1,0:T(8,128)(2,1)} %copy-done.15, ...), custom_call_target="tpu_custom_call" | custom-call | flops 1610612736 | bytes 6291456 | tf_op jit(solution)/shard_map/rank_slot/pallas_call | solution.py:474
  30.7 10.5 %all_to_all.10 = f32[16,4,128]{2,1,0:T(4,128)S(1)} all-to-all(f32[16,4,128]{2,1,0:T(4,128)S(1)} %bitcast.10), channel_id=1, replica_groups=mesh['groups'=2,'wide'=8,'narrow'=2] {'wide','narrow'}, dimensions={0} | all-to-all | bytes 65536 | tf_op jit(solution)/shard_map/all_to_all | solution.py:673
  41.2 0.9 %unpack_rows.1 = f32[8,8,128]{2,1,0:T(8,128)} custom-call(s32[8,128]{1,0:T(8,128)S(1)} %get-tuple-element.31.order_ref, s32[8,128]{1,0:T(8,128)S(1)} %get-tuple-element.32.back_ref, f32[64,128]{1,0:T(8,128)S(1)} %bitcast.11), custom_call_target="tpu_custom_call" | custom-call | tf_op jit(solution)/shard_map/unpack_rows/pallas_call | solution.py:527
  (29 shorter events, 0.1 us)
Async XLA Ops:
  0.6 10.2 %copy-start.13 = (bf16[4,512,256]{2,1,0:T(8,128)(2,1)S(1)}, bf16[4,512,256]{2,1,0:T(8,128)(2,1)}, u32[]{:S(2)}) copy-start(bf16[4,512,256]{2,1,0:T(8,128)(2,1)} %rest_0_.2) | copy-start | bytes 3145732
  3.2 7.7 %copy-start.3 = (bf16[1,2,512,256]{3,2,1,0:T(8,128)(2,1)S(1)}, bf16[1,2,512,256]{3,2,1,0:T(8,128)(2,1)}, u32[]{:S(2)}) copy-start(bf16[1,2,512,256]{3,2,1,0:T(8,128)(2,1)} %rest_0_.1) | copy-start | bytes 1572868
  3.3 11.6 %copy-start.7 = (f32[1,4,512]{2,1,0:T(4,128)S(1)}, f32[1,4,512]{2,1,0:T(4,128)}, u32[]{:S(2)}) copy-start(f32[1,4,512]{2,1,0:T(4,128)} %rest_2_) | copy-start | bytes 24580
  3.3 11.9 %copy-start.8 = (f32[512]{0:T(512)S(1)}, f32[512]{0:T(512)}, u32[]{:S(2)}) copy-start(f32[512]{0:T(512)} %param.19) | copy-start | bytes 6148
  3.3 22.0 %all-to-all-start = ((bf16[16,32,512]{2,1,0:T(8,128)(2,1)}), bf16[16,32,512]{2,1,0:T(8,128)(2,1)S(1)}, u32[]{:S(2)}, u32[]{:S(2)}) async-start(bf16[16,32,512]{2,1,0:T(8,128)(2,1)} %bitcast.15), calls=%async_computation | async-start | bytes 1048576 | tf_op jit(solution)/shard_map/all_to_all | solution.py:608
  10.8 1.2 %copy-start.12 = (bf16[4,128]{1,0:T(4,128)(2,1)S(1)}, bf16[4,128]{1,0:T(4,128)(2,1)}, u32[]{:S(2)}) copy-start(bf16[4,128]{1,0:T(4,128)(2,1)} %rest_4_) | copy-start | bytes 3076
  10.8 4.4 %copy-start = (bf16[8,128,512]{2,1,0:T(8,128)(2,1)S(1)}, bf16[8,128,512]{2,1,0:T(8,128)(2,1)}, u32[]{:S(2)}) copy-start(bf16[8,128,512]{2,1,0:T(8,128)(2,1)} %cand_hbm.1) | copy-start | bytes 3145732
  10.8 4.4 %copy-start.1 = (bf16[512,512]{1,0:T(8,128)(2,1)S(1)}, bf16[512,512]{1,0:T(8,128)(2,1)}, u32[]{:S(2)}) copy-start(bf16[512,512]{1,0:T(8,128)(2,1)} %inner_ref.1) | copy-start | bytes 1572868
  10.8 4.4 %copy-start.2 = (bf16[512,512]{1,0:T(8,128)(2,1)S(1)}, bf16[512,512]{1,0:T(8,128)(2,1)}, u32[]{:S(2)}) copy-start(bf16[512,512]{1,0:T(8,128)(2,1)} %outer_ref.1) | copy-start | bytes 1572868
  10.9 4.3 %copy-start.6 = (bf16[8,512]{1,0:T(8,128)(2,1)S(1)}, bf16[8,512]{1,0:T(8,128)(2,1)}, u32[]{:S(2)}) copy-start(bf16[8,512]{1,0:T(8,128)(2,1)} %user_ref.1) | copy-start | bytes 24580
  11.0 7.8 %collective-permute-start = (bf16[1,2,512,256]{3,2,1,0:T(8,128)(2,1)S(1)}, bf16[1,2,512,256]{3,2,1,0:T(8,128)(2,1)S(1)}, u32[]{:S(2)}, u32[]{:S(2)}) collective-permute-start(bf16[1,2,512,256]{3,2,1,0:T(8,128)(2,1)S(1)} %copy-done.3), channel_id=1, source_target_pairs={{1,0},{0,1},{3,2},{2,3},{5,4},{4,5},{7,6},{6,7},{9,8},{8,9},{11,10... | collective-permute-start | bytes 1572872 | tf_op jit(solution)/shard_map/ppermute | solution.py:550
  11.4 9.9 %collective-permute-start.3 = (bf16[2,512,256]{2,1,0:T(8,128)(2,1)S(1)}, bf16[2,512,256]{2,1,0:T(8,128)(2,1)S(1)}, u32[]{:S(2)}, u32[]{:S(2)}) collective-permute-start(bf16[2,512,256]{2,1,0:T(8,128)(2,1)S(1)} %get-tuple-element.33), channel_id=1, source_target_pairs={{1,0},{0,1},{3,2},{2,3},{5,4},{4,5},{7,6},{6,7},{9,8},{8,9},{11,10... | collective-permute-start | bytes 1572872 | tf_op jit(solution)/shard_map/ppermute | solution.py:550
  11.5 11.4 %collective-permute-start.4 = (bf16[2,512,256]{2,1,0:T(8,128)(2,1)S(1)}, bf16[2,512,256]{2,1,0:T(8,128)(2,1)}, u32[]{:S(2)}, u32[]{:S(2)}) collective-permute-start(bf16[2,512,256]{2,1,0:T(8,128)(2,1)S(1)} %get-tuple-element.34), channel_id=1, source_target_pairs={{1,0},{0,1},{3,2},{2,3},{5,4},{4,5},{7,6},{6,7},{9,8},{8,9},{11,10... | collective-permute-start | bytes 1572872 | tf_op jit(solution)/shard_map/ppermute | solution.py:550
  11.9 9.4 %collective-permute-start.5 = (bf16[4,256,128]{2,1,0:T(8,128)(2,1)}, bf16[4,256,128]{2,1,0:T(8,128)(2,1)S(1)}, u32[]{:S(2)}, u32[]{:S(2)}) collective-permute-start(bf16[4,256,128]{2,1,0:T(8,128)(2,1)} %rest_3_), channel_id=1, source_target_pairs={{1,0},{0,1},{3,2},{2,3},{5,4},{4,5},{7,6},{6,7},{9,8},{8,9},{11,10... | collective-permute-start | bytes 786440 | tf_op jit(solution)/shard_map/ppermute | solution.py:550
  12.0 2.8 %collective-permute-start.2 = (bf16[4,128]{1,0:T(4,128)(2,1)S(1)}, bf16[4,128]{1,0:T(4,128)(2,1)S(1)}, u32[]{:S(2)}, u32[]{:S(2)}) collective-permute-start(bf16[4,128]{1,0:T(4,128)(2,1)S(1)} %copy-done.12), channel_id=1, source_target_pairs={{1,0},{0,1},{3,2},{2,3},{5,4},{4,5},{7,6},{6,7},{9,8},{8,9},{11,10... | collective-permute-start | bytes 3080 | tf_op jit(solution)/shard_map/ppermute | solution.py:550
  14.8 3.9 %collective-permute-start.1 = (f32[1,4,512]{2,1,0:T(4,128)S(1)}, f32[1,4,512]{2,1,0:T(4,128)S(1)}, u32[]{:S(2)}, u32[]{:S(2)}) collective-permute-start(f32[1,4,512]{2,1,0:T(4,128)S(1)} %copy-done.7), channel_id=1, source_target_pairs={{1,0},{0,1},{3,2},{2,3},{5,4},{4,5},{7,6},{6,7},{9,8},{8,9},{11,10... | collective-permute-start | bytes 24584 | tf_op jit(solution)/shard_map/ppermute | solution.py:550
  15.2 3.5 %copy-start.4 = (bf16[1,2,512,256]{3,2,1,0:T(8,128)(2,1)S(1)}, bf16[1,2,512,256]{3,2,1,0:T(8,128)(2,1)}, u32[]{:S(2)}) copy-start(bf16[1,2,512,256]{3,2,1,0:T(8,128)(2,1)} %rest_0_.1) | copy-start | bytes 1572868
  15.2 3.5 %copy-start.5 = (s32[8,512]{1,0:T(8,128)S(1)}, s32[8,512]{1,0:T(8,128)}, u32[]{:S(2)}) copy-start(s32[8,512]{1,0:T(8,128)} %kept_ref.1) | copy-start | bytes 49156
  15.3 3.5 %copy-start.10 = (f32[512]{0:T(512)S(1)}, f32[512]{0:T(512)}, u32[]{:S(2)}) copy-start(f32[512]{0:T(512)} %param.28) | copy-start | bytes 6148
  18.0 0.7 %copy-start.9 = (f32[8,8]{1,0:T(8,128)S(1)}, f32[8,8]{1,0:T(8,128)}, u32[]{:S(2)}) copy-start(f32[8,8]{1,0:T(8,128)} %rest_8_.1) | copy-start | bytes 772
  18.7 0.7 %copy-start.11 = (s32[8]{0:T(128)S(1)}, s32[8]{0:T(128)}, u32[]{:S(2)}) copy-start(s32[8]{0:T(128)} %slot_ref.1) | copy-start | bytes 100
  21.4 0.7 %copy-start.15 = (bf16[4,256,128]{2,1,0:T(8,128)(2,1)}, bf16[4,256,128]{2,1,0:T(8,128)(2,1)S(1)}, u32[]{:S(2)}) copy-start(bf16[4,256,128]{2,1,0:T(8,128)(2,1)S(1)} %collective-permute-done.5.rest_4_) | copy-start | bytes 786436
  22.1 0.8 %copy-start.14 = (bf16[2,512,256]{2,1,0:T(8,128)(2,1)}, bf16[2,512,256]{2,1,0:T(8,128)(2,1)S(1)}, u32[]{:S(2)}) copy-start(bf16[2,512,256]{2,1,0:T(8,128)(2,1)S(1)} %collective-permute-done.3.rest_1_) | copy-start | bytes 1572868

commit v9 on v8

--- a/solution.py
+++ b/solution.py
@@ -333,7 +333,7 @@
         tower_refs,
         sems,
     ) = rest[11:]
-    own = expert_hbm[0].shape[0] // 2
+    own = max(1, expert_hbm[0].shape[0] // 4)
     rest_of_own = pl.ds(own, expert_hbm[0].shape[0] - own)
     own_copy = pltpu.make_async_copy(expert_hbm[0].at[pl.ds(0, own)], expert_refs.at[pl.ds(0, own)], sems.at[0])
     own_copy.start()

time: 42.5 us -> 42.3 us (level)
  no operation moved by 1% of the time
where the time goes in v9:
time: 42.3 us; the launch traced here: 42 us
  Pallas kernels  13.5 us (32%)
  blocking collectives  10.5 us (25%)
  starting transfers between devices  9.36 us (22%)
  waiting for transfers between devices  4.78 us (11%)
  local copies, waits for them, and re-layouts  2.27 us (5%)
  between operations  1.55 us (4%)
    all_to_all x1, blocking collectives, on_device(): lax.all_to_all(sending, both, split_axis=0, concat_axis=0, tiled=True)  10.5 us
    all_to_all x1, starting transfers between devices, on_device(): lax.all_to_all(packed, both, split_axis=0, concat_axis=0, tiled=True)  7.5 us
    pallas_call x1, Pallas kernels, rank_slot(): pl.pallas_call(functools.partial(rank_body, narrow_count, len(experts), s...  5.28 us
    pallas_call x1, Pallas kernels, prerank(): pl.pallas_call(functools.partial(prerank_body, shard_len), out_shape=jax....  2.76 us
    pallas_call x1, Pallas kernels, pack_rows(): pl.pallas_call(functools.partial(pack_body, narrow_count, half), out_shap...  2.6 us
    ppermute x6, waiting for transfers between devices, from_others(): pieces.append(lax.ppermute(values, 'narrow', steps))  2.4 us
    all_to_all x1, waiting for transfers between devices, on_device(): lax.all_to_all(packed, both, split_axis=0, concat_axis=0, tiled=True)  2.38 us
    unnamed x32, local copies, waits for them, and re-layouts  2.2 us
  transfers between devices with their start and end apart: 7, of which 2 were waited for; matrix products, arithmetic and copies ran while one was open for 0% of the time, Pallas kernels for 11%

profile of v9, /device:TPU:0, one launch (start us, length us, event | category | flops | bytes accessed | tf_op | source)
XLA Modules:
  0.0 42.0 jit_solution(11393266411734570483)
XLA Ops:
  0.6 0.0 copy-start.13
  0.6 2.6 %pack_rows.1 = (bf16[512,512]{1,0:T(8,128)(2,1)}, s32[8,128]{1,0:T(8,128)S(1)}, s32[8,128]{1,0:T(8,128)S(1)}, s32[8,128]{1,0:T(8,128)S(1)}) custom-call(s32[8]{0:T(128)} %slot_ref.1, s32[8,512]{1,0:T(8,128)} %kept_ref.1, bf16[8,128,512]{2,1,0:T(8,128)(2,1)} %cand_hbm.1), custom_call_target="tpu_custom_call" | custom-call | flops 67108864 | bytes 1048576 | tf_op jit(solution)/shard_map/pack_rows/pallas_call | solution.py:125
  3.3 0.0 copy-start.8
  3.3 7.5 %all-to-all-start = ((bf16[16,32,512]{2,1,0:T(8,128)(2,1)}), bf16[16,32,512]{2,1,0:T(8,128)(2,1)S(1)}, u32[]{:S(2)}, u32[]{:S(2)}) async-start(bf16[16,32,512]{2,1,0:T(8,128)(2,1)} %bitcast.15), calls=%async_computation | async-start | bytes 1048576 | tf_op jit(solution)/shard_map/all_to_all | solution.py:608
  10.8 0.0 copy-start
  10.8 0.0 copy-start.1
  10.9 0.1 fusion
  11.0 0.5 %collective-permute-start = (bf16[1,2,512,256]{3,2,1,0:T(8,128)(2,1)S(1)}, bf16[1,2,512,256]{3,2,1,0:T(8,128)(2,1)S(1)}, u32[]{:S(2)}, u32[]{:S(2)}) collective-permute-start(bf16[1,2,512,256]{3,2,1,0:T(8,128)(2,1)S(1)} %copy-done.3), channel_id=1, source_target_pairs={{1,0},{0,1},{3,2},{2,3},{5,4},{4,5},{7,6},{6,7},{9,8},{8,9},{11,10... | collective-permute-start | bytes 1572872 | tf_op jit(solution)/shard_map/ppermute | solution.py:550
  11.4 0.1 collective-permute-start.3
  11.5 0.4 collective-permute-start.4
  11.9 0.1 collective-permute-start.5
  12.0 0.4 collective-permute-start.2
  12.4 2.4 %collective-permute-done.2.rest_5_ = bf16[4,128]{1,0:T(4,128)(2,1)S(1)} collective-permute-done((bf16[4,128]{1,0:T(4,128)(2,1)S(1)}, bf16[4,128]{1,0:T(4,128)(2,1)S(1)}, u32[]{:S(2)}, u32[]{:S(2)}) %collective-permute-start.2) | collective-permute-done | bytes 1056 | tf_op jit(solution)/shard_map/ppermute | solution.py:550
  14.8 0.4 collective-permute-start.1
  15.2 0.0 copy-start.5
  15.3 2.8 %prerank.1 = f32[8,128]{1,0:T(8,128)} custom-call(bf16[1024,512]{1,0:T(8,128)(2,1)S(1)} %bitcast.8, bf16[512,512]{1,0:T(8,128)(2,1)S(1)} %copy-done.1, f32[1,512]{1,0:T(1,128)S(1)} %bitcast.12, bf16[512,512]{1,0:T(8,128)(2,1)S(1)} %copy-done.2, bf16[8,512]{1,0:T(8,128)(2,1)S(1)} %copy-done.6, s32[8,128]{1,0:T(8,128)S(1)} %get-tuple-element.29.lane_ref), custom_call_target="tpu_custom_call" | custom-call | flops 1 | bytes 1 | tf_op jit(solution)/shard_map/prerank/pallas_call | solution.py:165
  18.8 0.6 %copy-done.11 = s32[8]{0:T(128)S(1)} copy-done((s32[8]{0:T(128)S(1)}, s32[8]{0:T(128)}, u32[]{:S(2)}) %copy-start.11) | copy-done | bytes 56
  19.4 2.0 %prepare.1 = (s32[8,512]{1,0:T(8,128)S(1)}, bf16[4,160,512]{2,1,0:T(8,128)(2,1)S(1)}, bf16[4,512,128]{2,1,0:T(8,128)(2,1)S(1)}, f32[8,512]{1,0:T(8,128)S(1)}, f3...) custom-call(s32[8]{0:T(128)S(1)} %copy-done.11, ...), custom_call_target="tpu_custom_call" | custom-call | flops 1 | bytes 1 | tf_op jit(solution)/shard_map/prepare/pallas_call | solution.py:285
  21.4 0.7 %copy-done.15 = bf16[4,256,128]{2,1,0:T(8,128)(2,1)} copy-done((bf16[4,256,128]{2,1,0:T(8,128)(2,1)}, bf16[4,256,128]{2,1,0:T(8,128)(2,1)S(1)}, u32[]{:S(2)}) %copy-start.15) | copy-done | bytes 262168
  22.1 0.8 %copy-done.14 = bf16[2,512,256]{2,1,0:T(8,128)(2,1)} copy-done((bf16[2,512,256]{2,1,0:T(8,128)(2,1)}, bf16[2,512,256]{2,1,0:T(8,128)(2,1)S(1)}, u32[]{:S(2)}) %copy-start.14) | copy-done | bytes 524312
  22.9 2.4 %all-to-all-done = bf16[16,32,512]{2,1,0:T(8,128)(2,1)S(1)} async-done(((bf16[16,32,512]{2,1,0:T(8,128)(2,1)}), bf16[16,32,512]{2,1,0:T(8,128)(2,1)S(1)}, u32[]{:S(2)}, u32[]{:S(2)}) %all-to-all-start) | async-done | bytes 524320 | tf_op jit(solution)/shard_map/all_to_all | solution.py:608
  25.3 5.3 %rank_slot.1 = f32[64,128]{1,0:T(8,128)S(1)} custom-call(bf16[4,512,256]{2,1,0:T(8,128)(2,1)} %rest_0_.2, bf16[2,512,256]{2,1,0:T(8,128)(2,1)} %copy-done.14, bf16[2,512,256]{2,1,0:T(8,128)(2,1)} %collective-permute-done.4.rest_2_, bf16[4,256,128]{2,1,0:T(8,128)(2,1)} %rest_3_, bf16[4,256,128]{2,1,0:T(8,128)(2,1)} %copy-done.15, ...), custom_call_target="tpu_custom_call" | custom-call | flops 1610612736 | bytes 6291456 | tf_op jit(solution)/shard_map/rank_slot/pallas_call | solution.py:474
  30.5 10.5 %all_to_all.10 = f32[16,4,128]{2,1,0:T(4,128)S(1)} all-to-all(f32[16,4,128]{2,1,0:T(4,128)S(1)} %bitcast.10), channel_id=1, replica_groups=mesh['groups'=2,'wide'=8,'narrow'=2] {'wide','narrow'}, dimensions={0} | all-to-all | bytes 65536 | tf_op jit(solution)/shard_map/all_to_all | solution.py:673
  41.1 0.9 %unpack_rows.1 = f32[8,8,128]{2,1,0:T(8,128)} custom-call(s32[8,128]{1,0:T(8,128)S(1)} %get-tuple-element.31.order_ref, s32[8,128]{1,0:T(8,128)S(1)} %get-tuple-element.32.back_ref, f32[64,128]{1,0:T(8,128)S(1)} %bitcast.11), custom_call_target="tpu_custom_call" | custom-call | tf_op jit(solution)/shard_map/unpack_rows/pallas_call | solution.py:527
  (29 shorter events, 0.1 us)
Async XLA Ops:
  0.6 10.2 %copy-start.13 = (bf16[4,512,256]{2,1,0:T(8,128)(2,1)S(1)}, bf16[4,512,256]{2,1,0:T(8,128)(2,1)}, u32[]{:S(2)}) copy-start(bf16[4,512,256]{2,1,0:T(8,128)(2,1)} %rest_0_.2) | copy-start | bytes 3145732
  3.2 7.7 %copy-start.3 = (bf16[1,2,512,256]{3,2,1,0:T(8,128)(2,1)S(1)}, bf16[1,2,512,256]{3,2,1,0:T(8,128)(2,1)}, u32[]{:S(2)}) copy-start(bf16[1,2,512,256]{3,2,1,0:T(8,128)(2,1)} %rest_0_.1) | copy-start | bytes 1572868
  3.3 11.6 %copy-start.7 = (f32[1,4,512]{2,1,0:T(4,128)S(1)}, f32[1,4,512]{2,1,0:T(4,128)}, u32[]{:S(2)}) copy-start(f32[1,4,512]{2,1,0:T(4,128)} %rest_2_) | copy-start | bytes 24580
  3.3 11.9 %copy-start.8 = (f32[512]{0:T(512)S(1)}, f32[512]{0:T(512)}, u32[]{:S(2)}) copy-start(f32[512]{0:T(512)} %param.19) | copy-start | bytes 6148
  3.3 22.0 %all-to-all-start = ((bf16[16,32,512]{2,1,0:T(8,128)(2,1)}), bf16[16,32,512]{2,1,0:T(8,128)(2,1)S(1)}, u32[]{:S(2)}, u32[]{:S(2)}) async-start(bf16[16,32,512]{2,1,0:T(8,128)(2,1)} %bitcast.15), calls=%async_computation | async-start | bytes 1048576 | tf_op jit(solution)/shard_map/all_to_all | solution.py:608
  10.8 1.2 %copy-start.12 = (bf16[4,128]{1,0:T(4,128)(2,1)S(1)}, bf16[4,128]{1,0:T(4,128)(2,1)}, u32[]{:S(2)}) copy-start(bf16[4,128]{1,0:T(4,128)(2,1)} %rest_4_) | copy-start | bytes 3076
  10.8 4.4 %copy-start = (bf16[8,128,512]{2,1,0:T(8,128)(2,1)S(1)}, bf16[8,128,512]{2,1,0:T(8,128)(2,1)}, u32[]{:S(2)}) copy-start(bf16[8,128,512]{2,1,0:T(8,128)(2,1)} %cand_hbm.1) | copy-start | bytes 3145732
  10.8 4.4 %copy-start.1 = (bf16[512,512]{1,0:T(8,128)(2,1)S(1)}, bf16[512,512]{1,0:T(8,128)(2,1)}, u32[]{:S(2)}) copy-start(bf16[512,512]{1,0:T(8,128)(2,1)} %inner_ref.1) | copy-start | bytes 1572868
  10.8 4.4 %copy-start.2 = (bf16[512,512]{1,0:T(8,128)(2,1)S(1)}, bf16[512,512]{1,0:T(8,128)(2,1)}, u32[]{:S(2)}) copy-start(bf16[512,512]{1,0:T(8,128)(2,1)} %outer_ref.1) | copy-start | bytes 1572868
  10.9 4.3 %copy-start.6 = (bf16[8,512]{1,0:T(8,128)(2,1)S(1)}, bf16[8,512]{1,0:T(8,128)(2,1)}, u32[]{:S(2)}) copy-start(bf16[8,512]{1,0:T(8,128)(2,1)} %user_ref.1) | copy-start | bytes 24580
  11.0 7.8 %collective-permute-start = (bf16[1,2,512,256]{3,2,1,0:T(8,128)(2,1)S(1)}, bf16[1,2,512,256]{3,2,1,0:T(8,128)(2,1)S(1)}, u32[]{:S(2)}, u32[]{:S(2)}) collective-permute-start(bf16[1,2,512,256]{3,2,1,0:T(8,128)(2,1)S(1)} %copy-done.3), channel_id=1, source_target_pairs={{1,0},{0,1},{3,2},{2,3},{5,4},{4,5},{7,6},{6,7},{9,8},{8,9},{11,10... | collective-permute-start | bytes 1572872 | tf_op jit(solution)/shard_map/ppermute | solution.py:550
  11.4 9.9 %collective-permute-start.3 = (bf16[2,512,256]{2,1,0:T(8,128)(2,1)S(1)}, bf16[2,512,256]{2,1,0:T(8,128)(2,1)S(1)}, u32[]{:S(2)}, u32[]{:S(2)}) collective-permute-start(bf16[2,512,256]{2,1,0:T(8,128)(2,1)S(1)} %get-tuple-element.33), channel_id=1, source_target_pairs={{1,0},{0,1},{3,2},{2,3},{5,4},{4,5},{7,6},{6,7},{9,8},{8,9},{11,10... | collective-permute-start | bytes 1572872 | tf_op jit(solution)/shard_map/ppermute | solution.py:550
  11.5 11.4 %collective-permute-start.4 = (bf16[2,512,256]{2,1,0:T(8,128)(2,1)S(1)}, bf16[2,512,256]{2,1,0:T(8,128)(2,1)}, u32[]{:S(2)}, u32[]{:S(2)}) collective-permute-start(bf16[2,512,256]{2,1,0:T(8,128)(2,1)S(1)} %get-tuple-element.34), channel_id=1, source_target_pairs={{1,0},{0,1},{3,2},{2,3},{5,4},{4,5},{7,6},{6,7},{9,8},{8,9},{11,10... | collective-permute-start | bytes 1572872 | tf_op jit(solution)/shard_map/ppermute | solution.py:550
  11.9 9.4 %collective-permute-start.5 = (bf16[4,256,128]{2,1,0:T(8,128)(2,1)}, bf16[4,256,128]{2,1,0:T(8,128)(2,1)S(1)}, u32[]{:S(2)}, u32[]{:S(2)}) collective-permute-start(bf16[4,256,128]{2,1,0:T(8,128)(2,1)} %rest_3_), channel_id=1, source_target_pairs={{1,0},{0,1},{3,2},{2,3},{5,4},{4,5},{7,6},{6,7},{9,8},{8,9},{11,10... | collective-permute-start | bytes 786440 | tf_op jit(solution)/shard_map/ppermute | solution.py:550
  12.0 2.8 %collective-permute-start.2 = (bf16[4,128]{1,0:T(4,128)(2,1)S(1)}, bf16[4,128]{1,0:T(4,128)(2,1)S(1)}, u32[]{:S(2)}, u32[]{:S(2)}) collective-permute-start(bf16[4,128]{1,0:T(4,128)(2,1)S(1)} %copy-done.12), channel_id=1, source_target_pairs={{1,0},{0,1},{3,2},{2,3},{5,4},{4,5},{7,6},{6,7},{9,8},{8,9},{11,10... | collective-permute-start | bytes 3080 | tf_op jit(solution)/shard_map/ppermute | solution.py:550
  14.8 3.9 %collective-permute-start.1 = (f32[1,4,512]{2,1,0:T(4,128)S(1)}, f32[1,4,512]{2,1,0:T(4,128)S(1)}, u32[]{:S(2)}, u32[]{:S(2)}) collective-permute-start(f32[1,4,512]{2,1,0:T(4,128)S(1)} %copy-done.7), channel_id=1, source_target_pairs={{1,0},{0,1},{3,2},{2,3},{5,4},{4,5},{7,6},{6,7},{9,8},{8,9},{11,10... | collective-permute-start | bytes 24584 | tf_op jit(solution)/shard_map/ppermute | solution.py:550
  15.2 3.5 %copy-start.4 = (bf16[1,2,512,256]{3,2,1,0:T(8,128)(2,1)S(1)}, bf16[1,2,512,256]{3,2,1,0:T(8,128)(2,1)}, u32[]{:S(2)}) copy-start(bf16[1,2,512,256]{3,2,1,0:T(8,128)(2,1)} %rest_0_.1) | copy-start | bytes 1572868
  15.2 3.5 %copy-start.5 = (s32[8,512]{1,0:T(8,128)S(1)}, s32[8,512]{1,0:T(8,128)}, u32[]{:S(2)}) copy-start(s32[8,512]{1,0:T(8,128)} %kept_ref.1) | copy-start | bytes 49156
  15.3 3.5 %copy-start.10 = (f32[512]{0:T(512)S(1)}, f32[512]{0:T(512)}, u32[]{:S(2)}) copy-start(f32[512]{0:T(512)} %param.28) | copy-start | bytes 6148
  18.0 0.7 %copy-start.9 = (f32[8,8]{1,0:T(8,128)S(1)}, f32[8,8]{1,0:T(8,128)}, u32[]{:S(2)}) copy-start(f32[8,8]{1,0:T(8,128)} %rest_8_.1) | copy-start | bytes 772
  18.7 0.7 %copy-start.11 = (s32[8]{0:T(128)S(1)}, s32[8]{0:T(128)}, u32[]{:S(2)}) copy-start(s32[8]{0:T(128)} %slot_ref.1) | copy-start | bytes 100
  21.4 0.7 %copy-start.15 = (bf16[4,256,128]{2,1,0:T(8,128)(2,1)}, bf16[4,256,128]{2,1,0:T(8,128)(2,1)S(1)}, u32[]{:S(2)}) copy-start(bf16[4,256,128]{2,1,0:T(8,128)(2,1)S(1)} %collective-permute-done.5.rest_4_) | copy-start | bytes 786436
  22.1 0.8 %copy-start.14 = (bf16[2,512,256]{2,1,0:T(8,128)(2,1)}, bf16[2,512,256]{2,1,0:T(8,128)(2,1)S(1)}, u32[]{:S(2)}) copy-start(bf16[2,512,256]{2,1,0:T(8,128)(2,1)S(1)} %collective-permute-done.3.rest_1_) | copy-start | bytes 1572868
